TPU v7x, 512 devices: a whole 4x8x8 slice. The times are simulated.
512 devices in a mesh: lib: 32 (over y, x), ctx: 2 (over core), head: 8 (over z).
Axes of the slice: x: 4, y: 8, z: 8, core: 2. Of those that a mesh axis runs over, the one named last changes fastest.
Arguments:
- queries: bfloat16 [32, 128, 8192], P('lib', None, 'head'), may hold values from -50 to 50
- passage_keys: bfloat16 [512, 512, 1024], P('lib', 'ctx', 'head'), may hold values from -6 to 6
- passage_values: bfloat16 [512, 512, 1024], P('lib', 'ctx', 'head'), may hold values from -6 to 6
- offsets: int32 [512], P('lib'), may hold values from 0 to 4095
- out_weight: bfloat16 [8192, 8192], P('head', 'lib'), may hold values from -0.5 to 0.5
- passage_list: int32 [32, 16], P('lib'), may hold values from 0 to 511, as said below
- targets: int32 [32, 16], P('lib'), may hold values from 0 to 8191
- row_counts: int32 [32], P('lib'), may hold values from 1 to 128
Outputs:
- output: bfloat16 [2, 2048, 8192], P('ctx', 'head', 'lib')
Inputs may be any that keep to these rules, and one draw needn't show every extreme that they name: `passage_list`: each row names 16 different passages; passage i belongs to owner i // 16; no row names more than 2 passages of one owner, and in every row some owner has exactly 2.
All inputs are finite; a program needn't handle non-finite values.
Results may differ from a plain program's by a relative error of at most 0.012.
The roundings to bfloat16 on the way count: a program that leaves them out, or rounds other values in their place, can miss the bound.
Values may be sent and summed in bfloat16 or wider, within the bound.
No kernel may reach another device: no remote copies, remote signals or barrier semaphores. Data moves between devices by JAX's collectives and lax.ppermute only.
A program may use at most 64 MiB of HBM per device.

v0:
```python
import jax
import jax.numpy as jnp
from jax import lax
from jax.sharding import Mesh
from jax.sharding import PartitionSpec as P

LIB = ("lib_0", "lib_1")


theta_base = 500000.0


def in_blocks(value, dim, length):
    before, after = (value.shape[:dim], value.shape[dim + 1 :])
    return jnp.moveaxis(value.reshape(*before, length, -1, *after), dim, 0)


def joined_along(tiles, dim):
    tiles = jnp.moveaxis(tiles, 0, dim)
    lengths = tiles.shape
    return tiles.reshape(*lengths[:dim], lengths[dim] * lengths[dim + 1], *lengths[dim + 2 :])


def exchange_in_order(tiles, axes, order):
    lengths = [lax.axis_size(a) for a in axes]
    tiles = tiles.reshape(*lengths, *tiles.shape[1:])
    for k in order:
        tiles = lax.all_to_all(tiles, axes[k], split_axis=k, concat_axis=k, tiled=True)
    return tiles.reshape(-1, *tiles.shape[len(axes) :])


def one_axis_at_a_time(value, axes, order, split_dim, concat_dim):
    tiles = in_blocks(value, split_dim, lax.axis_size(axes))
    return joined_along(exchange_in_order(tiles, axes, order), concat_dim)


def sent_together(arrays, axis, split_dim, concat_dim, along):
    ends, at = ([], 0)
    for a in arrays[:-1]:
        at += a.shape[along]
        ends.append(at)
    both = jnp.concatenate(arrays, axis=along)
    return tuple(
        jnp.split(
            lax.all_to_all(both, axis, split_axis=split_dim, concat_axis=concat_dim, tiled=True),
            ends,
            axis=along,
        )
    )


def whole_of(value, axes, dim):
    for axis in reversed(axes):
        value = lax.all_gather(value, axis, axis=dim, tiled=True)
    return value


def rotate_keys(block, delta):
    width = block.shape[-1]
    half = width // 2
    inverse = theta_base ** (-2.0 * jnp.arange(half, dtype=jnp.float32) / width)
    angle = delta.astype(jnp.float32)[:, None] * inverse[None, :]
    cosine = jnp.cos(angle)[:, None, :]
    sine = jnp.sin(angle)[:, None, :]
    first = block[..., :half].astype(jnp.float32)
    second = block[..., half:].astype(jnp.float32)
    return jnp.concatenate(
        [first * cosine - second * sine, second * cosine + first * sine], axis=-1
    )


def partial_softmax(query, keys, values):
    scores = lax.dot_general(
        query, keys, (((1,), (1,)), ((), ())), preferred_element_type=jnp.float32
    )
    scores = scores * query.shape[1] ** (-0.5)
    highest = jnp.max(scores, axis=1)
    weights = jnp.exp(scores - highest[:, None])
    totals = jnp.sum(weights, axis=1)
    summed = jnp.dot(weights.astype(jnp.bfloat16), values, preferred_element_type=jnp.float32)
    return (highest, totals, summed)


def combine(first, second):
    highest = jnp.maximum(first[0], second[0])
    early = jnp.exp(first[0] - highest)
    later = jnp.exp(second[0] - highest)
    return (
        highest,
        first[1] * early + second[1] * later,
        first[2] * early[..., None] + second[2] * later[..., None],
    )


def attend_blocks(query, keys, values):
    row_total = query.shape[0]
    block_rows = min(512, row_total)
    blocked = query.reshape(row_total // block_rows, block_rows, query.shape[1])
    highest, totals, summed = lax.map(
        lambda part_rows: partial_softmax(part_rows, keys, values), blocked
    )
    return (
        highest.reshape(row_total),
        totals.reshape(row_total),
        summed.reshape(row_total, keys.shape[1]),
    )


def body(
    queries, passage_keys, passage_values, offsets, out_weight, passage_list, targets, row_counts
):
    owners = lax.axis_size(LIB)
    halves_count = lax.axis_size("ctx")
    pass_dev = passage_keys.shape[0]
    chosen = passage_list[0]
    listed = chosen.shape[0]
    most_each = 4 * listed // owners
    slot_count = owners * most_each
    owner_of = chosen // pass_dev
    position = jnp.arange(listed, dtype=jnp.int32)
    before = (owner_of[:, None] == owner_of[None, :]) & (position[None, :] < position[:, None])
    slot_of = owner_of * most_each + jnp.sum(before.astype(jnp.int32), axis=1)
    matched = (jnp.arange(slot_count, dtype=jnp.int32)[:, None] == slot_of[None, :]).astype(
        jnp.int32
    )
    wanted_local = jnp.sum(matched * (chosen % pass_dev)[None, :], axis=1)
    wanted_target = jnp.sum(matched * targets[0][None, :], axis=1)
    requests = jnp.stack([wanted_local, wanted_target], axis=1)
    arrived = one_axis_at_a_time(requests, LIB, (0, 1), 0, 0)
    asked = arrived[:, 0]
    lookup = (asked[:, None] == jnp.arange(pass_dev, dtype=jnp.int32)[None, :]).astype(jnp.int32)
    shift_by = arrived[:, 1] - jnp.sum(lookup * offsets[None, :], axis=1)
    sent_keys = rotate_keys(jnp.take(passage_keys, asked, axis=0), shift_by).astype(jnp.bfloat16)
    sent_values = jnp.take(passage_values, asked, axis=0)
    got_keys, got_values = sent_together((sent_keys, sent_values), LIB, 0, 0, 1)
    width = passage_keys.shape[2]
    key_rows = jnp.take(got_keys, slot_of, axis=0).reshape(-1, width)
    value_rows = jnp.take(got_values, slot_of, axis=0).reshape(-1, width)
    prompt_rows = queries.shape[1]
    group = queries.shape[2] // width
    query = queries[0].reshape(prompt_rows * group, width)
    highest, totals, summed = attend_blocks(query, key_rows, value_rows)
    pieces = (
        lax.all_to_all(highest[None], "ctx", split_axis=1, concat_axis=0, tiled=True),
        lax.all_to_all(totals[None], "ctx", split_axis=1, concat_axis=0, tiled=True),
        lax.all_to_all(summed[None], "ctx", split_axis=1, concat_axis=0, tiled=True),
    )
    state = (pieces[0][0], pieces[1][0], pieces[2][0])
    state = combine(state, (pieces[0][1], pieces[1][1], pieces[2][1]))
    highest, totals, summed = state
    half_rows = prompt_rows // halves_count
    attended = (summed / totals[:, None]).reshape(half_rows, group * width)
    first_row = lax.axis_index("ctx") * half_rows
    live = (first_row + jnp.arange(half_rows, dtype=jnp.int32) < row_counts[0])[:, None]
    attended = jnp.where(live, attended, jnp.zeros_like(attended)).astype(jnp.bfloat16)
    partial_terms = jnp.dot(
        whole_of(attended, LIB, 0), out_weight, preferred_element_type=jnp.float32
    )
    combined = lax.psum_scatter(partial_terms, "head", scatter_dimension=0, tiled=True)
    return combined.astype(jnp.bfloat16)[None]


def solution(mesh):
    finer = Mesh(
        mesh.devices.reshape(8, 4, mesh.shape["ctx"], mesh.shape["head"]),
        ("lib_0", "lib_1", "ctx", "head"),
    )
    return jax.shard_map(
        body,
        mesh=finer,
        in_specs=(
            P(LIB, None, "head"),
            P(LIB, "ctx", "head"),
            P(LIB, "ctx", "head"),
            P(LIB),
            P("head", LIB),
            P(LIB, None),
            P(LIB, None),
            P(LIB),
        ),
        out_specs=P("ctx", "head", LIB),
        check_vma=False,
    )
```

profile of v0, /device:TPU:6, one launch (start us, length us, event | category | flops | bytes accessed | tf_op | source)
XLA Modules:
  0.0 409.1 jit_solution(7321575644462482309)
XLA Ops:
  6.5 0.8 and_select_fusion.2
  8.1 0.7 select_reduce_fusion.2
  9.4 14.7 %all_to_all.59 = s32[8,4,2,2]{1,3,2,0:T(2,128)S(1)} all-to-all(s32[8,4,2,2]{1,3,2,0:T(2,128)S(1)} %copy.14), channel_id=1, replica_groups=mesh['lib_0'=8,'lib_1'=4,'ctx'=2,'head'=8] {'lib_0'}, dimensions={0} | all-to-all | bytes 1024 | tf_op jit(solution)/shard_map/all_to_all | solution.py:28
  24.0 0.7 copy.15
  24.7 4.8 %all-to-all-start.1 = ((s32[8,4,2,2]{0,3,2,1:T(2,128)}), s32[8,4,2,2]{0,3,2,1:T(2,128)S(1)}, u32[]{:S(2)}, u32[]{:S(2)}) async-start(s32[8,4,2,2]{0,3,2,1:T(2,128)} %copy.15), calls=%async_computation.1 | async-start | bytes 16384 | tf_op jit(solution)/shard_map/all_to_all | solution.py:28
  29.5 3.2 all-to-all-done.1
  33.0 3.0 gather_fusion
  36.1 3.1 gather_fusion.1
  39.4 4.0 broadcast_select_fusion.1
  43.4 3.8 fusion.16
  47.1 4.8 %pad_maximum_fusion = bf16[64,512,128]{2,1,0:T(8,128)(2,1)} fusion(bf16[64,256,128]{2,1,0:T(8,128)(2,1)S(1)} %get-tuple-element.83, bf16[64,256,64]{2,1,0:T(8,128)(2,1)S(1)} %get-tuple-element.77, bf16[64,256,64]{2,1,0:T(8,128)(2,1)S(1)} %get-tuple-element.76), kind=kLoop, calls=%fused_computation.24 | loop fusion | flops 25165824 | bytes 16777216 | tf_op jit(solution)/shard_map/concatenate | solution.py:42
  52.0 6.7 %all-to-all-start.2 = ((bf16[64,512,128]{2,1,0:T(8,128)(2,1)}), bf16[64,512,128]{2,1,0:T(8,128)(2,1)}, u32[]{:S(2)}, u32[]{:S(2)}) async-start(bf16[64,512,128]{2,1,0:T(8,128)(2,1)} %pad_maximum_fusion), calls=%async_computation.2 | async-start | bytes 16777216 | tf_op jit(solution)/shard_map/all_to_all | solution.py:45
  59.6 179.1 %all-to-all-done.2 = bf16[64,512,128]{2,1,0:T(8,128)(2,1)} async-done(((bf16[64,512,128]{2,1,0:T(8,128)(2,1)}), bf16[64,512,128]{2,1,0:T(8,128)(2,1)}, u32[]{:S(2)}, u32[]{:S(2)}) %all-to-all-start.2) | async-done | bytes 8388640 | tf_op jit(solution)/shard_map/all_to_all | solution.py:45
  238.7 5.9 %fusion.31 = (bf16[64,256,128]{2,1,0:T(8,128)(2,1)}, bf16[64,256,128]{2,1,0:T(8,128)(2,1)}) fusion(bf16[64,512,128]{2,1,0:T(8,128)(2,1)} %all-to-all-done.2), kind=kLoop, calls=%fused_computation.82 | loop fusion | bytes 16777216 | tf_op jit(solution)/shard_map/split | solution.py:44
  244.7 2.9 gather_fusion.2
  247.6 3.9 gather_fusion.3
  251.5 1.5 broadcast_select_fusion.2
  252.9 8.9 %while.14 = (s32[]{:T(128)}, f32[2,512]{1,0:T(2,128)S(1)}, f32[2,512]{1,0:T(2,128)S(1)}, f32[2,512,128]{2,1,0:T(8,128)}, bf16[2,512,128]{2,1,0:T(8,128)(2,1)S(1)...) while((s32[]{:T(128)}, f32[2,512]{1,0:T(2,128)S(1)}, ...), condition=%wide.region_7.10_spmd, body=%wide.region_4.9_spmd.sunk | while | flops 1090518016 | bytes 31867044 | solution.py:99
  253.0 1.3 multiply_reduce_fusion.2
  254.3 1.5 fusion.46
  255.8 1.5 fusion.45
  257.4 1.3 multiply_reduce_fusion.2
  258.8 1.5 fusion.46
  260.2 1.5 fusion.45
  261.9 5.4 %all_to_all.60 = f32[1,1024,128]{2,0,1:T(1,128)S(1)} all-to-all(f32[1,1024,128]{2,0,1:T(1,128)} %bitcast.100), channel_id=1, replica_groups=mesh['lib_0'=8,'lib_1'=4,'ctx'=2,'head'=8] {'ctx'}, dimensions={1} | all-to-all | bytes 1048576 | tf_op jit(solution)/shard_map/all_to_all | solution.py:146
  268.0 3.7 all_to_all.61
  272.0 3.7 all_to_all.62
  276.5 14.9 %all_gather.6 = bf16[256,1024]{1,0:T(8,128)(2,1)} all-gather(bf16[64,1024]{1,0:T(8,128)(2,1)S(1)} %fusion.20), channel_id=1, replica_groups=mesh['lib_0'=8,'lib_1'=4,'ctx'=2,'head'=8] {'lib_1'}, dimensions={0}, use_global_device_ids=true | all-gather | bytes 655360 | tf_op jit(solution)/shard_map/all_gather | solution.py:54
  291.5 59.3 %all-gather.2.cloned.1.call-done = bf16[2048,1024]{1,0:T(8,128)(2,1)} async-done(((bf16[256,1024]{1,0:T(8,128)(2,1)}), bf16[2048,1024]{1,0:T(8,128)(2,1)}) %all-gather.2.cloned.1.call-update) | async-done | bytes 4194320 | tf_op jit(solution)/shard_map/all_gather | solution.py:54
  350.8 4.8 %fusion.32 = f32[2048,256]{1,0:T(8,128)} fusion(bf16[2048,1024]{1,0:T(8,128)(2,1)} %all-gather.2.cloned.1.call-done, bf16[1024,256]{1,0:T(8,128)(2,1)S(1)} %copy-done.7), kind=kOutput, calls=%fused_computation.83 | convolution fusion | flops 1073741824 | bytes 6815744 | tf_op jit(solution)/shard_map/dot_general | solution.py:156
  355.6 45.0 %reduce-scatter.2.cloned.1.call-done = f32[256,256]{1,0:T(8,128)} async-done(((f32[2048,256]{1,0:T(8,128)}), f32[256,256]{1,0:T(8,128)}) %reduce-scatter.2.cloned.1.call-update) | async-done | bytes 262160 | tf_op jit(solution)/shard_map/reduce_scatter | solution.py:159
  400.6 1.6 convert_bitcast_fusion
  (72 shorter events, 4.2 us)
Async XLA Ops:
  6.5 26.5 %copy-start = (bf16[16,256,128]{2,1,0:T(8,128)(2,1)S(1)}, bf16[16,256,128]{2,1,0:T(8,128)(2,1)}, u32[]{:S(2)}) copy-start(bf16[16,256,128]{2,1,0:T(8,128)(2,1)} %param.15) | copy-start | bytes 3145732
  24.7 8.0 %all-to-all-start.1 = ((s32[8,4,2,2]{0,3,2,1:T(2,128)}), s32[8,4,2,2]{0,3,2,1:T(2,128)S(1)}, u32[]{:S(2)}, u32[]{:S(2)}) async-start(s32[8,4,2,2]{0,3,2,1:T(2,128)} %copy.15), calls=%async_computation.1 | async-start | bytes 16384 | tf_op jit(solution)/shard_map/all_to_all | solution.py:28
  33.0 3.0 copy-start.2
  36.1 3.1 copy-start.8
  52.0 6.8 %copy-start.5 = (bf16[1,128,1024]{2,1,0:T(8,128)(2,1)S(1)}, bf16[1,128,1024]{2,1,0:T(8,128)(2,1)}, u32[]{:S(2)}) copy-start(bf16[1,128,1024]{2,1,0:T(8,128)(2,1)} %param.14) | copy-start | bytes 786436
  52.0 7.6 %copy-start.6 = (s32[1,16]{1,0:T(1,128)S(1)}, s32[1,16]{1,0:T(1,128)}, u32[]{:S(2)}) copy-start(s32[1,16]{1,0:T(1,128)} %param.19) | copy-start | bytes 196
  52.0 186.7 %all-to-all-start.2 = ((bf16[64,512,128]{2,1,0:T(8,128)(2,1)}), bf16[64,512,128]{2,1,0:T(8,128)(2,1)}, u32[]{:S(2)}, u32[]{:S(2)}) async-start(bf16[64,512,128]{2,1,0:T(8,128)(2,1)} %pad_maximum_fusion), calls=%async_computation.2 | async-start | bytes 16777216 | tf_op jit(solution)/shard_map/all_to_all | solution.py:45
  58.7 292.1 %all-gather.2.cloned.1.call-start = ((), (), s32[]{:S(2)}) async-start(), calls=%async_computation.7 | async-start | bytes 4718592 | tf_op jit(solution)/shard_map/all_gather | solution.py:54
  252.9 1.3 copy-start.3
  255.8 1.5 copy-start.4
  257.4 1.3 copy-start.3
  260.2 1.5 copy-start.4
  261.9 88.9 %copy-start.7 = (bf16[1024,256]{1,0:T(8,128)(2,1)S(1)}, bf16[1024,256]{1,0:T(8,128)(2,1)}, u32[]{:S(2)}) copy-start(bf16[1024,256]{1,0:T(8,128)(2,1)} %param.18) | copy-start | bytes 1572868
  291.5 110.8 %copy-start.1 = (bf16[16,256,128]{2,1,0:T(8,128)(2,1)S(1)}, bf16[16,256,128]{2,1,0:T(8,128)(2,1)}, u32[]{:S(2)}) copy-start(bf16[16,256,128]{2,1,0:T(8,128)(2,1)} %param.15) | copy-start | bytes 3145732
  291.5 109.2 %reduce-scatter.2.cloned.1.call-start = ((), (), s32[]{:S(2)}) async-start(), calls=%async_computation.8 | async-start | bytes 2359296 | tf_op jit(solution)/shard_map/reduce_scatter | solution.py:159
Sparse Core Ops, SparseCore 0:
  291.6 59.1 all-gather.1
  355.7 44.8 reduce-scatter.1
where the time goes:
time: 410 us; the launch traced here: 409 us
  waiting for transfers between devices  287 us (70%)
  blocking collectives  42.3 us (10%)
  local copies, waits for them, and re-layouts  22.1 us (5%)
  other arithmetic  21.6 us (5%)
  between operations  14.4 us (4%)
  starting transfers between devices  11.6 us (3%)
  matrix products  10.4 us (3%)
    all_to_all x1, waiting for transfers between devices, sent_together(): lax.all_to_all(both, axis, split_axis=split_dim, concat_axis=concat_dim,...  179 us
    all_gather x1, waiting for transfers between devices, whole_of(): value = lax.all_gather(value, axis, axis=dim, tiled=True)  59.3 us
    reduce_scatter x1, waiting for transfers between devices, body(): lax.psum_scatter(partial_terms, 'head', scatter_dimension=0, tiled=True)  45 us
    all_gather x1, blocking collectives, whole_of(): value = lax.all_gather(value, axis, axis=dim, tiled=True)  14.9 us
    all_to_all x1, blocking collectives, exchange_in_order(): lax.all_to_all(tiles, axes[k], split_axis=k, concat_axis=k, tiled=True)  14.7 us
  transfers between devices with their start and end apart: 4, of which 4 were waited for; matrix products, arithmetic and copies ran while one was open for 0% of the time, Pallas kernels for 0%

commit v1 on v0

v1 whole, which is shorter than its diff:
```python
import functools

import jax
import jax.numpy as jnp
from jax import lax
from jax.experimental import pallas as pl
from jax.experimental.pallas import tpu as pltpu
from jax.sharding import Mesh
from jax.sharding import PartitionSpec as P

ROW, COL = "lib_0", "lib_1"
LIB = (ROW, COL)
theta_base = 500000.0
EMPTY = -1e30
CHUNK = 256
MOST = 2


def shift(value, axis, by):
    n = lax.axis_size(axis)
    return lax.ppermute(value, axis, [(i, (i + by) % n) for i in range(n)])


def ring_gather(value, axis):
    n = lax.axis_size(axis)
    pieces = [value] + [None] * (n - 1)
    behind = ahead = value
    for d in range(1, (n + 1) // 2):
        behind = shift(behind, axis, 1)
        ahead = shift(ahead, axis, -1)
        pieces[n - d], pieces[d] = behind, ahead
    if n % 2 == 0:
        half = value.shape[0] // 2
        pieces[n // 2] = jnp.concatenate(
            [shift(behind[:half], axis, 1), shift(ahead[half:], axis, -1)], axis=0
        )
    return pieces


def attend_kernel(scale, slot_ref, q_ref, cos_ref, sin_ref, *refs):
    key_refs, value_refs = refs[:4], refs[4:8]
    out_ref, lse_ref, q_scr, k_scr, s_scr, m_scr, l_scr, acc_scr, used = refs[8:]
    prompt = pl.program_id(0)
    listed = cos_ref.shape[1]
    rows, width = q_ref.shape[1], cos_ref.shape[2]
    group = q_ref.shape[2] // width
    total_rows = rows * group
    held = key_refs[0].shape[0]
    log2e = 1.4426950408889634
    for g in range(group):
        q_scr[g * rows : (g + 1) * rows] = q_ref[0, :, g * width : (g + 1) * width]
    m_scr[...] = jnp.full_like(m_scr, EMPTY)
    l_scr[...] = jnp.zeros_like(l_scr)
    acc_scr[...] = jnp.zeros_like(acc_scr)

    def score(k, count):
        slot = slot_ref[prompt * listed + k]

        @pl.when(slot >= 0)
        def _():
            piece, at = slot // held, slot % held
            for d in range(4):

                @pl.when(piece == d)
                def _():
                    k_scr[...] = key_refs[d][at]

            used[count] = slot
            keys = k_scr[...].astype(jnp.float32)
            cosine = cos_ref[0, pl.ds(k, 1), :]
            sine = sin_ref[0, pl.ds(k, 1), :]
            turned = keys * cosine + pltpu.roll(keys, width // 2, 1) * sine
            turned = turned.astype(jnp.bfloat16)
            for r in range(0, total_rows, CHUNK):
                s = lax.dot_general(
                    q_scr[r : r + CHUNK],
                    turned,
                    (((1,), (1,)), ((), ())),
                    preferred_element_type=jnp.float32,
                )
                s_scr[count, r : r + CHUNK] = s
                highest = m_scr[r : r + CHUNK]
                for t in range(0, s.shape[1], width):
                    highest = jnp.maximum(highest, s[:, t : t + width])
                m_scr[r : r + CHUNK] = highest

        return count + jnp.where(slot >= 0, 1, 0)

    count = lax.fori_loop(0, listed, score, 0)
    for r in range(0, total_rows, CHUNK):
        m = jnp.max(m_scr[r : r + CHUNK], axis=1, keepdims=True)
        m_scr[r : r + CHUNK] = jnp.broadcast_to(m, (CHUNK, width))

    def weigh(t, carry):
        slot = used[t]
        piece, at = slot // held, slot % held
        for d in range(4):

            @pl.when(piece == d)
            def _():
                k_scr[...] = value_refs[d][at]

        for r in range(0, total_rows, CHUNK):
            m = m_scr[r : r + CHUNK]
            s = s_scr[t, r : r + CHUNK]
            parts = [
                jnp.exp2((s[:, u : u + width] - m) * (scale * log2e))
                for u in range(0, s.shape[1], width)
            ]
            l_scr[r : r + CHUNK] += functools.reduce(jnp.add, parts)
            weights = jnp.concatenate(parts, axis=1).astype(jnp.bfloat16)
            acc_scr[r : r + CHUNK] += jnp.dot(
                weights, k_scr[...], preferred_element_type=jnp.float32
            )
        return carry

    lax.fori_loop(0, count, weigh, 0)
    row = lax.broadcasted_iota(jnp.int32, (rows, rows), 0)
    column = lax.broadcasted_iota(jnp.int32, (rows, rows), 1)
    halves = out_ref.shape[0]
    part = rows // halves
    none = count == 0
    for g in range(group):
        span = slice(g * rows, (g + 1) * rows)
        total = jnp.sum(l_scr[span], axis=1, keepdims=True)
        total = jnp.where(none, 1.0, total)
        out = (acc_scr[span] / total).astype(out_ref.dtype)
        for c in range(halves):
            out_ref[c, g, 0] = out[c * part : (c + 1) * part]
        lse = jnp.where(none, EMPTY, m_scr[span] * scale + jnp.log(total))
        lse_ref[0, g : g + 1, :] = jnp.sum(
            jnp.where(row == column, lse, 0.0), axis=0, keepdims=True
        )


def attend(slots, query, cosine, sine, keys, values, halves):
    prompts, rows, features = query.shape
    listed, width = cosine.shape[1:]
    group = features // width
    tokens = keys[0].shape[1]
    most = MOST * len(keys)
    part = rows // halves
    whole = pl.BlockSpec(memory_space=pltpu.VMEM)
    table = pl.BlockSpec((1, listed, width), lambda j, s: (j, 0, 0))
    return pl.pallas_call(
        functools.partial(attend_kernel, width**-0.5),
        out_shape=(
            jax.ShapeDtypeStruct((halves, group, prompts, part, width), jnp.bfloat16),
            jax.ShapeDtypeStruct((prompts, group, rows), jnp.float32),
        ),
        grid_spec=pltpu.PrefetchScalarGridSpec(
            num_scalar_prefetch=1,
            grid=(prompts,),
            in_specs=[pl.BlockSpec((1, rows, features), lambda j, s: (j, 0, 0)), table, table]
            + [whole] * 8,
            out_specs=(
                pl.BlockSpec((halves, group, 1, part, width), lambda j, s: (0, 0, j, 0, 0)),
                pl.BlockSpec((1, group, rows), lambda j, s: (j, 0, 0)),
            ),
            scratch_shapes=[
                pltpu.VMEM((rows * group, width), jnp.bfloat16),
                pltpu.VMEM((tokens, width), jnp.bfloat16),
                pltpu.VMEM((most, rows * group, tokens), jnp.float32),
                pltpu.VMEM((rows * group, width), jnp.float32),
                pltpu.VMEM((rows * group, width), jnp.float32),
                pltpu.VMEM((rows * group, width), jnp.float32),
                pltpu.SMEM((most,), jnp.int32),
            ],
        ),
        compiler_params=pltpu.CompilerParams(vmem_limit_bytes=48 * 1024 * 1024),
    )(slots, query, cosine, sine, *keys, *values)


def project_kernel(columns, where_ref, *refs):
    pieces, weight_ref = refs[:columns], refs[columns]
    out_ref, acc = refs[columns + 1 :]
    step = pl.program_id(0)
    heads, rows = pieces[0].shape[1:3]
    left = jnp.concatenate(
        [jnp.concatenate([p[0, h] for h in range(heads)], axis=1) for p in pieces], axis=0
    )
    right = jnp.concatenate([weight_ref[h, 0] for h in range(heads)], axis=0)
    term = jnp.dot(left, right, preferred_element_type=jnp.float32)

    @pl.when(step == 0)
    def _():
        acc[...] = term

    @pl.when(step > 0)
    def _():
        acc[...] += term

    @pl.when(step == pl.num_programs(0) - 1)
    def _():
        for d in range(columns):
            at = pl.multiple_of(where_ref[pl.num_programs(0) + d] * rows, rows)
            out_ref[pl.ds(at, rows), :] = acc[d * rows : (d + 1) * rows].astype(out_ref.dtype)


def project(where, pieces, weight):
    columns = len(pieces)
    steps, heads, rows, width = pieces[0].shape
    out_columns = weight.shape[-1]
    return pl.pallas_call(
        functools.partial(project_kernel, columns),
        out_shape=jax.ShapeDtypeStruct((columns * rows, out_columns), jnp.bfloat16),
        grid_spec=pltpu.PrefetchScalarGridSpec(
            num_scalar_prefetch=1,
            grid=(steps,),
            in_specs=[pl.BlockSpec((1, heads, rows, width), lambda s, w: (s, 0, 0, 0))] * columns
            + [pl.BlockSpec((heads, 1, width, out_columns), lambda s, w: (0, w[s], 0, 0))],
            out_specs=pl.BlockSpec((columns * rows, out_columns), lambda s, w: (0, 0)),
            scratch_shapes=[pltpu.VMEM((columns * rows, out_columns), jnp.float32)],
        ),
        compiler_params=pltpu.CompilerParams(vmem_limit_bytes=32 * 1024 * 1024),
    )(where, *pieces, weight)


def merged(outs, lses):
    top = jnp.max(lses, axis=0)
    share = jnp.exp(lses - top)
    total = jnp.sum(share, axis=0)
    share = share / total
    out = jnp.sum(outs.astype(jnp.float32) * share[..., None], axis=0)
    return out, top + jnp.log(total)


def three_parts(value):
    first = lax.reduce_precision(value, 8, 7)
    rest = value - first
    second = lax.reduce_precision(rest, 8, 7)
    return jnp.stack([first, second, rest - second]).astype(jnp.bfloat16)


def body(
    queries, passage_keys, passage_values, offsets, out_weight, passage_list, targets, row_counts
):
    rows_of, columns = lax.axis_size(ROW), lax.axis_size(COL)
    y, x, c = lax.axis_index(ROW), lax.axis_index(COL), lax.axis_index("ctx")
    held, tokens, width = passage_keys.shape
    listed = passage_list.shape[1]
    prompt_rows, features = queries.shape[1:]
    group = features // width
    halves = lax.axis_size("ctx")
    half_rows = prompt_rows // halves

    keys = [passage_keys, shift(passage_keys, COL, -1), None, shift(passage_keys, COL, 1)]
    values = [passage_values, shift(passage_values, COL, -1), None, shift(passage_values, COL, 1)]
    keys[2] = shift(keys[3], COL, 1)
    values[2] = shift(values[1], COL, -1)

    asked = jnp.concatenate([passage_list, targets, row_counts[:, None]], axis=1)
    asked = lax.all_gather(asked, ROW, axis=0, tiled=True)
    near_offsets = lax.all_gather(offsets, COL, axis=0, tiled=True)
    query = lax.all_gather(queries, ROW, axis=0, tiled=True)
    weight = lax.all_gather(out_weight, "head", axis=0, tiled=True)

    near = columns * held
    local = asked[:, :listed] - y * near
    mine = (local >= 0) & (local < near)
    ahead = (local // held - x) % columns
    slots = jnp.where(mine, ahead * held + local % held, -1)
    same = local[..., None] == jnp.arange(near, dtype=jnp.int32)
    delta = asked[:, listed : 2 * listed] - jnp.sum(
        jnp.where(same, near_offsets, 0), axis=-1
    )
    half = width // 2
    inverse = theta_base ** (-2.0 * jnp.arange(half, dtype=jnp.float32) / width)
    angle = delta.astype(jnp.float32)[..., None] * inverse
    cosine, sine = jnp.cos(angle), jnp.sin(angle)
    cosine = jnp.concatenate([cosine, cosine], axis=-1)
    sine = jnp.concatenate([-sine, sine], axis=-1)

    out, lse = attend(slots.reshape(-1), query, cosine, sine, keys, values, halves)

    lse = jnp.transpose(lse.reshape(rows_of, group, halves, half_rows), (2, 1, 0, 3))
    swap = [(i, 1 - i) for i in range(2)]
    pick = functools.partial(lax.dynamic_index_in_dim, axis=0, keepdims=False)
    other = lax.ppermute(pick(out, 1 - c), "ctx", swap)
    other_lse = lax.ppermute(pick(lse, 1 - c), "ctx", swap)
    out, lse = merged(
        jnp.stack([pick(out, c), other]), jnp.stack([pick(lse, c), other_lse])
    )

    out = out.astype(jnp.bfloat16).reshape(group, rows_of * half_rows, width)
    parts = jnp.moveaxis(three_parts(lse), 0, 1).reshape(group, -1, width)
    extra = parts.shape[1]
    parts = jnp.pad(parts, ((0, 0), (0, -extra % 16), (0, 0)))
    sent = jnp.concatenate([out, parts], axis=1)
    got = lax.all_to_all(sent, ROW, split_axis=0, concat_axis=0, tiled=True)
    outs = got[:, : rows_of * half_rows].reshape(rows_of, rows_of, half_rows, width)
    lses = got[:, rows_of * half_rows : rows_of * half_rows + extra].astype(jnp.float32)
    lses = jnp.sum(lses.reshape(rows_of, 3, rows_of, half_rows), axis=1)
    attended, _ = merged(outs, lses)
    live = c * half_rows + jnp.arange(half_rows, dtype=jnp.int32) < asked[:, 2 * listed :]
    attended = jnp.where(live[..., None], attended, 0.0).astype(jnp.bfloat16)

    attended = lax.all_to_all(attended, "head", split_axis=0, concat_axis=0, tiled=True)
    pieces = ring_gather(jnp.stack(ring_gather(attended, ROW)), COL)
    where = jnp.concatenate(
        [
            (y + jnp.arange(rows_of, dtype=jnp.int32)) % rows_of,
            (x + jnp.arange(columns, dtype=jnp.int32)) % columns,
        ]
    )
    weight = weight.reshape(lax.axis_size("head"), group, width, -1)
    return project(where, pieces, weight)[None]


def solution(mesh):
    finer = Mesh(
        mesh.devices.reshape(8, 4, mesh.shape["ctx"], mesh.shape["head"]),
        ("lib_0", "lib_1", "ctx", "head"),
    )
    return jax.shard_map(
        body,
        mesh=finer,
        in_specs=(
            P(LIB, None, "head"),
            P(LIB, "ctx", "head"),
            P(LIB, "ctx", "head"),
            P(LIB),
            P("head", LIB),
            P(LIB, None),
            P(LIB, None),
            P(LIB),
        ),
        out_specs=P("ctx", "head", LIB),
        check_vma=False,
    )
```

time: 410 us -> 281 us (0.69)
  waiting for transfers between devices: 287 us -> 76.5 us
  starting transfers between devices: 11.6 us -> 78.4 us
  Pallas kernels: 0 us -> 36 us
  other arithmetic: 21.6 us -> 5.09 us
  blocking collectives: 42.3 us -> 53.6 us
  local copies, waits for them, and re-layouts: 22.1 us -> 10.8 us
  matrix products: 10.4 us -> 0 us
    all_to_all x2 -> x1, waiting for transfers between devices: 182 us -> 29.8 us  [body(): got = lax.all_to_all(sent, ROW, split_axis=0, concat_axis=0, tiled=True)]
    ppermute x0 -> x20, starting transfers between devices: none -> 73.4 us  [the longest x18 69.1 us: shift(): return lax.ppermute(value, axis, [(i, (i + by) % n) for i in range(n)])]
    all_gather x1 -> x2, waiting for transfers between devices: 59.3 us -> 0.05 us  [the longest x1 0.03 us: body(): weight = lax.all_gather(out_weight, 'head', axis=0, tiled=True)]
    ppermute x0 -> x20, waiting for transfers between devices: none -> 45.9 us  [the longest x18 45.1 us: shift(): return lax.ppermute(value, axis, [(i, (i + by) % n) for i in range(n)])]
    reduce_scatter x1 -> x0, waiting for transfers between devices: 45 us -> none  [body(): lax.psum_scatter(partial_terms, 'head', scatter_dimension=0, tiled=True)]
    pallas_call x0 -> x2, Pallas kernels: none -> 36 us  [the longest x1 31.7 us: attend(): pl.pallas_call(functools.partial(attend_kernel, width ** (-0.5)), out_sha...]
    unnamed x0 -> x1, blocking collectives: none -> 19.2 us
    gather x4 -> x0, local copies, waits for them, and re-layouts: 12.9 us -> none  [the longest x1 3.86 us: body(): value_rows = jnp.take(got_values, slot_of, axis=0).reshape(-1, width)]
  transfers between devices with their start and end apart: 4 -> 23, of which waited for: 4 -> 11; matrix products, arithmetic and copies ran while one was open for 0% -> 3% of each run, Pallas kernels for 0% -> 0%
where the time goes in v1:
time: 281 us; the launch traced here: 277 us
  starting transfers between devices  78.4 us (28%)
  waiting for transfers between devices  76.5 us (27%)
  blocking collectives  53.6 us (19%)
  Pallas kernels  36 us (13%)
  between operations  16.6 us (6%)
  local copies, waits for them, and re-layouts  10.8 us (4%)
  other arithmetic  5.09 us (2%)
    ppermute x18, starting transfers between devices, shift(): return lax.ppermute(value, axis, [(i, (i + by) % n) for i in range(n)])  69.1 us
    ppermute x18, waiting for transfers between devices, shift(): return lax.ppermute(value, axis, [(i, (i + by) % n) for i in range(n)])  45.1 us
    pallas_call x1, Pallas kernels, attend(): pl.pallas_call(functools.partial(attend_kernel, width ** (-0.5)), out_sha...  31.7 us
    all_to_all x1, waiting for transfers between devices, body(): got = lax.all_to_all(sent, ROW, split_axis=0, concat_axis=0, tiled=True)  29.8 us
    all_to_all x1, blocking collectives, body(): lax.all_to_all(attended, 'head', split_axis=0, concat_axis=0, tiled=True)  21.3 us
    unnamed x1, blocking collectives  19.2 us
    all_gather x1, blocking collectives, body(): asked = lax.all_gather(asked, ROW, axis=0, tiled=True)  13.2 us
    unnamed x21, local copies, waits for them, and re-layouts  8.11 us
  transfers between devices with their start and end apart: 23, of which 11 were waited for; matrix products, arithmetic and copies ran while one was open for 3% of the time, Pallas kernels for 0%

profile of v1, /device:TPU:6, one launch (start us, length us, event | category | flops | bytes accessed | tf_op | source)
XLA Modules:
  0.0 277.1 jit_solution(14529612860072883638)
XLA Ops:
  8.1 7.8 %collective-permute-start.1 = (bf16[16,256,128]{2,1,0:T(8,128)(2,1)}, bf16[16,256,128]{2,1,0:T(8,128)(2,1)S(1)}, u32[]{:S(2)}, u32[]{:S(2)}) collective-permute-start(bf16[16,256,128]{2,1,0:T(8,128)(2,1)} %refs_0_.1), channel_id=1, source_target_pairs={{0,16},{16,32},{32,48},{48,0},{1,17},{17,33},{33,49},{49,1},{2,18}... | collective-permute-start | bytes 3145736 | tf_op jit(solution)/shard_map/ppermute | solution.py:21
  15.9 1.9 collective-permute-start.3
  17.8 1.9 collective-permute-start
  19.8 5.1 %collective-permute-start.5 = (bf16[16,256,128]{2,1,0:T(8,128)(2,1)}, bf16[16,256,128]{2,1,0:T(8,128)(2,1)}, u32[]{:S(2)}, u32[]{:S(2)}) collective-permute-start(bf16[16,256,128]{2,1,0:T(8,128)(2,1)} %refs_4_.1), channel_id=1, source_target_pairs={{0,16},{16,32},{32,48},{48,0},{1,17},{17,33},{33,49},{49,1},{2,18}... | collective-permute-start | bytes 3145736 | tf_op jit(solution)/shard_map/ppermute | solution.py:21
  25.6 14.3 %collective-permute-done.1.refs_3_ = bf16[16,256,128]{2,1,0:T(8,128)(2,1)S(1)} collective-permute-done((bf16[16,256,128]{2,1,0:T(8,128)(2,1)}, bf16[16,256,128]{2,1,0:T(8,128)(2,1)S(1)}, u32[]{:S(2)}, u32[]{:S(2)}) %collective-permute-start.1) | collective-permute-done | bytes 1048608 | tf_op jit(solution)/shard_map/ppermute | solution.py:21
  39.8 5.5 %collective-permute-start.2 = (bf16[16,256,128]{2,1,0:T(8,128)(2,1)S(1)}, bf16[16,256,128]{2,1,0:T(8,128)(2,1)S(1)}, u32[]{:S(2)}, u32[]{:S(2)}) collective-permute-start(bf16[16,256,128]{2,1,0:T(8,128)(2,1)S(1)} %collective-permute-done.1.refs_3_), channel_id=1, source_target_pairs={{0,16},{16,32},{32,48},{48,0},{1,17},{17,33},{33,49},{49,1},{2,18}... | collective-permute-start | bytes 3145736 | tf_op jit(solution)/shard_map/ppermute | solution.py:21
  45.4 1.9 collective-permute-start.4
  48.1 13.2 %all-gather = s32[8,1,33]{2,1,0:T(1,128)S(1)} all-gather(s32[1,1,33]{2,1,0:T(1,128)S(1)} %add_bitcast_fusion), channel_id=1, replica_groups=mesh['lib_0'=8,'lib_1'=4,'ctx'=2,'head'=8] {'lib_0'}, dimensions={0}, use_global_device_ids=true | all-gather | bytes 1188 | tf_op jit(solution)/shard_map/all_gather | solution.py:253
  64.2 19.2 %all-reduce.1 = s32[64]{0:T(128)S(1)} all-reduce(s32[64]{0:T(128)S(1)} %dynamic-update-slice), channel_id=1, replica_groups=mesh['lib_0'=8,'lib_1'=4,'ctx'=2,'head'=8] {'lib_1'}, use_global_device_ids=true, to_apply=%add.1 | all-reduce | flops 64 | bytes 512
  86.7 31.7 %shard_map.82 = (bf16[2,8,8,64,128]{4,3,2,1,0:T(8,128)(2,1)}, f32[8,8,128]{2,1,0:T(8,128)S(1)}) custom-call(s32[128]{0:T(128)S(1)} %reshape.106.slot_ref, bf16[8,128,1024]{2,1,0:T(8,128)(2,1)} %all-gather.4.cloned.1.call-done.q_ref, f32[8,16,128]{2,1,0:T(8,128)S(1)} %get-tuple-element.22.cos_ref, f32[8,16,128]{2,1,0:T(8,128)S(1)} %get-tuple-element.23.sin_ref, ...), custom_call_target="tpu_custom_call" | custom-call | tf_op jit(solution)/shard_map/pallas_call | solution.py:145
  120.2 1.9 collective-permute-start.6
  122.3 2.4 collective-permute-start.7
  128.1 5.0 %all-to-all-start = ((bf16[8,528,128]{2,1,0:T(8,128)(2,1)}), bf16[8,528,128]{2,1,0:T(8,128)(2,1)S(1)}, u32[]{:S(2)}, u32[]{:S(2)}) async-start(bf16[8,528,128]{2,1,0:T(8,128)(2,1)} %fusion.1), calls=%async_computation | async-start | bytes 2162688 | tf_op jit(solution)/shard_map/all_to_all | solution.py:290
  133.3 29.8 %all-to-all-done = bf16[8,528,128]{2,1,0:T(8,128)(2,1)S(1)} async-done(((bf16[8,528,128]{2,1,0:T(8,128)(2,1)}), bf16[8,528,128]{2,1,0:T(8,128)(2,1)S(1)}, u32[]{:S(2)}, u32[]{:S(2)}) %all-to-all-start) | async-done | bytes 1081376 | tf_op jit(solution)/shard_map/all_to_all | solution.py:290
  164.3 21.3 %all_to_all.10 = bf16[8,64,128]{2,1,0:T(8,128)(2,1)S(1)} all-to-all(bf16[8,64,128]{2,1,0:T(8,128)(2,1)S(1)} %select_convert_fusion), channel_id=1, replica_groups=mesh['lib_0'=8,'lib_1'=4,'ctx'=2,'head'=8] {'head'}, dimensions={0} | all-to-all | bytes 262144 | tf_op jit(solution)/shard_map/all_to_all | solution.py:298
  185.6 1.9 collective-permute-start.8
  187.5 3.9 %collective-permute-start.11 = (bf16[8,64,128]{2,1,0:T(8,128)(2,1)S(1)}, bf16[8,64,128]{2,1,0:T(8,128)(2,1)S(1)}, u32[]{:S(2)}, u32[]{:S(2)}) collective-permute-start(bf16[8,64,128]{2,1,0:T(8,128)(2,1)S(1)} %all_to_all.10), channel_id=1, source_target_pairs={{0,64},{64,128},{128,192},{192,256},{256,320},{320,384},{384,448},... | collective-permute-start | bytes 393224 | tf_op jit(solution)/shard_map/ppermute | solution.py:21
  192.4 3.1 %collective-permute-start.9 = (bf16[8,64,128]{2,1,0:T(8,128)(2,1)S(1)}, bf16[8,64,128]{2,1,0:T(8,128)(2,1)S(1)}, u32[]{:S(2)}, u32[]{:S(2)}) collective-permute-start(bf16[8,64,128]{2,1,0:T(8,128)(2,1)S(1)} %collective-permute-done.8), channel_id=1, source_target_pairs={{0,448},{64,0},{128,64},{192,128},{256,192},{320,256},{384,320},{4... | collective-permute-start | bytes 393224 | tf_op jit(solution)/shard_map/ppermute | solution.py:21
  195.6 2.7 collective-permute-start.12
  199.3 4.3 %collective-permute-start.10 = (bf16[8,64,128]{2,1,0:T(8,128)(2,1)S(1)}, bf16[8,64,128]{2,1,0:T(8,128)(2,1)S(1)}, u32[]{:S(2)}, u32[]{:S(2)}) collective-permute-start(bf16[8,64,128]{2,1,0:T(8,128)(2,1)S(1)} %collective-permute-done.9), channel_id=1, source_target_pairs={{0,448},{64,0},{128,64},{192,128},{256,192},{320,256},{384,320},{4... | collective-permute-start | bytes 393224 | tf_op jit(solution)/shard_map/ppermute | solution.py:21
  203.6 1.9 collective-permute-start.13
  206.1 5.5 %collective-permute-start.15 = (bf16[4,64,128]{2,1,0:T(8,128)(2,1)S(1)}, bf16[4,64,128]{2,1,0:T(8,128)(2,1)S(1)}, u32[]{:S(2)}, u32[]{:S(2)}) collective-permute-start(bf16[4,64,128]{2,1,0:T(8,128)(2,1)S(1)} %slice.42), channel_id=1, source_target_pairs={{0,448},{64,0},{128,64},{192,128},{256,192},{320,256},{384,320},{4... | collective-permute-start | bytes 196616 | tf_op jit(solution)/shard_map/ppermute | solution.py:21
  211.7 1.9 collective-permute-start.14
  213.7 5.4 %collective-permute-done.14 = bf16[4,64,128]{2,1,0:T(8,128)(2,1)S(1)} collective-permute-done((bf16[4,64,128]{2,1,0:T(8,128)(2,1)S(1)}, bf16[4,64,128]{2,1,0:T(8,128)(2,1)S(1)}, u32[]{:S(2)}, u32[]{:S(2)}) %collective-permute-start.14) | collective-permute-done | bytes 65568 | tf_op jit(solution)/shard_map/ppermute | solution.py:21
  219.2 4.9 %collective-permute-start.16 = (bf16[8,8,64,128]{3,2,1,0:T(8,128)(2,1)S(1)}, bf16[8,8,64,128]{3,2,1,0:T(8,128)(2,1)S(1)}, u32[]{:S(2)}, u32[]{:S(2)}) collective-permute-start(bf16[8,8,64,128]{3,2,1,0:T(8,128)(2,1)S(1)} %bitcast_dynamic-update-slice_fusion.refs_0_), channel_id=1, source_target_pairs={{0,48},{16,0},{32,16},{48,32},{1,49},{17,1},{33,17},{49,33},{2,50}... | collective-permute-start | bytes 3145736 | tf_op jit(solution)/shard_map/ppermute | solution.py:21
  224.1 7.6 %collective-permute-start.17 = (bf16[8,8,64,128]{3,2,1,0:T(8,128)(2,1)S(1)}, bf16[8,8,64,128]{3,2,1,0:T(8,128)(2,1)S(1)}, u32[]{:S(2)}, u32[]{:S(2)}) collective-permute-start(bf16[8,8,64,128]{3,2,1,0:T(8,128)(2,1)S(1)} %bitcast_dynamic-update-slice_fusion.refs_0_), channel_id=1, source_target_pairs={{0,16},{16,32},{32,48},{48,0},{1,17},{17,33},{33,49},{49,1},{2,18}... | collective-permute-start | bytes 3145736 | tf_op jit(solution)/shard_map/ppermute | solution.py:21
  231.7 16.2 %collective-permute-done.16.refs_1_ = bf16[8,8,64,128]{3,2,1,0:T(8,128)(2,1)S(1)} collective-permute-done((bf16[8,8,64,128]{3,2,1,0:T(8,128)(2,1)S(1)}, bf16[8,8,64,128]{3,2,1,0:T(8,128)(2,1)S(1)}, u32[]{:S(2)}, u32[]{:S(2)}) %collective-permute-start.16) | collective-permute-done | bytes 1048608 | tf_op jit(solution)/shard_map/ppermute | solution.py:21
  248.0 1.9 collective-permute-start.19
  250.0 5.1 %collective-permute-start.18 = (bf16[4,8,64,128]{3,2,1,0:T(8,128)(2,1)S(1)}, bf16[4,8,64,128]{3,2,1,0:T(8,128)(2,1)S(1)}, u32[]{:S(2)}, u32[]{:S(2)}) collective-permute-start(bf16[4,8,64,128]{3,2,1,0:T(8,128)(2,1)S(1)} %slice.43), channel_id=1, source_target_pairs={{0,16},{16,32},{32,48},{48,0},{1,17},{17,33},{33,49},{49,1},{2,18}... | collective-permute-start | bytes 1572872 | tf_op jit(solution)/shard_map/ppermute | solution.py:21
  255.2 5.1 %collective-permute-done.19 = bf16[4,8,64,128]{3,2,1,0:T(8,128)(2,1)S(1)} collective-permute-done((bf16[4,8,64,128]{3,2,1,0:T(8,128)(2,1)S(1)}, bf16[4,8,64,128]{3,2,1,0:T(8,128)(2,1)S(1)}, u32[]{:S(2)}, u32[]{:S(2)}) %collective-permute-start.19) | collective-permute-done | bytes 524320 | tf_op jit(solution)/shard_map/ppermute | solution.py:21
  261.9 2.2 copy-done
  265.3 4.3 %shard_map.83 = bf16[256,256]{1,0:T(8,128)(2,1)} custom-call(s32[12]{0:T(128)S(1)} %pad_add_fusion.where_ref, bf16[8,8,64,128]{3,2,1,0:T(8,128)(2,1)S(1)} %copy-done.2, bf16[8,8,64,128]{3,2,1,0:T(8,128)(2,1)S(1)} %collective-permute-done.16.refs_1_, bf16[8,8,64,128]{3,2,1,0:T(8,128)(2,1)S(1)} %pad_maximum_fusion.refs_2_, ...), custom_call_target="tpu_custom_call" | custom-call | tf_op jit(solution)/shard_map/pallas_call | solution.py:204
  (85 shorter events, 19.6 us)
Async XLA Ops:
  7.4 76.8 %all-gather.4.cloned.1.call-start = ((), (), s32[]{:S(2)}) async-start(), calls=%async_computation.2 | async-start | bytes 2359296 | tf_op jit(solution)/shard_map/all_gather | solution.py:255
  8.1 253.8 %all-gather.6.cloned.1.call-start = ((), (), s32[]{:S(2)}) async-start(), calls=%async_computation.3 | async-start | bytes 4718592 | tf_op jit(solution)/shard_map/all_gather | solution.py:256
  8.1 31.7 %collective-permute-start.1 = (bf16[16,256,128]{2,1,0:T(8,128)(2,1)}, bf16[16,256,128]{2,1,0:T(8,128)(2,1)S(1)}, u32[]{:S(2)}, u32[]{:S(2)}) collective-permute-start(bf16[16,256,128]{2,1,0:T(8,128)(2,1)} %refs_0_.1), channel_id=1, source_target_pairs={{0,16},{16,32},{32,48},{48,0},{1,17},{17,33},{33,49},{49,1},{2,18}... | collective-permute-start | bytes 3145736 | tf_op jit(solution)/shard_map/ppermute | solution.py:21
  15.9 29.5 %collective-permute-start.3 = (bf16[16,256,128]{2,1,0:T(8,128)(2,1)}, bf16[16,256,128]{2,1,0:T(8,128)(2,1)}, u32[]{:S(2)}, u32[]{:S(2)}) collective-permute-start(bf16[16,256,128]{2,1,0:T(8,128)(2,1)} %refs_4_.1), channel_id=1, source_target_pairs={{0,48},{16,0},{32,16},{48,32},{1,49},{17,1},{33,17},{49,33},{2,50}... | collective-permute-start | bytes 3145736 | tf_op jit(solution)/shard_map/ppermute | solution.py:21
  17.8 66.3 %collective-permute-start = (bf16[16,256,128]{2,1,0:T(8,128)(2,1)}, bf16[16,256,128]{2,1,0:T(8,128)(2,1)S(1)}, u32[]{:S(2)}, u32[]{:S(2)}) collective-permute-start(bf16[16,256,128]{2,1,0:T(8,128)(2,1)} %refs_0_.1), channel_id=1, source_target_pairs={{0,48},{16,0},{32,16},{48,32},{1,49},{17,1},{33,17},{49,33},{2,50}... | collective-permute-start | bytes 3145736 | tf_op jit(solution)/shard_map/ppermute | solution.py:21
  19.8 64.4 %collective-permute-start.5 = (bf16[16,256,128]{2,1,0:T(8,128)(2,1)}, bf16[16,256,128]{2,1,0:T(8,128)(2,1)}, u32[]{:S(2)}, u32[]{:S(2)}) collective-permute-start(bf16[16,256,128]{2,1,0:T(8,128)(2,1)} %refs_4_.1), channel_id=1, source_target_pairs={{0,16},{16,32},{32,48},{48,0},{1,17},{17,33},{33,49},{49,1},{2,18}... | collective-permute-start | bytes 3145736 | tf_op jit(solution)/shard_map/ppermute | solution.py:21
  39.8 44.3 %collective-permute-start.2 = (bf16[16,256,128]{2,1,0:T(8,128)(2,1)S(1)}, bf16[16,256,128]{2,1,0:T(8,128)(2,1)S(1)}, u32[]{:S(2)}, u32[]{:S(2)}) collective-permute-start(bf16[16,256,128]{2,1,0:T(8,128)(2,1)S(1)} %collective-permute-done.1.refs_3_), channel_id=1, source_target_pairs={{0,16},{16,32},{32,48},{48,0},{1,17},{17,33},{33,49},{49,1},{2,18}... | collective-permute-start | bytes 3145736 | tf_op jit(solution)/shard_map/ppermute | solution.py:21
  45.4 38.7 %collective-permute-start.4 = (bf16[16,256,128]{2,1,0:T(8,128)(2,1)}, bf16[16,256,128]{2,1,0:T(8,128)(2,1)}, u32[]{:S(2)}, u32[]{:S(2)}) collective-permute-start(bf16[16,256,128]{2,1,0:T(8,128)(2,1)} %collective-permute-done.3.refs_5_), channel_id=1, source_target_pairs={{0,48},{16,0},{32,16},{48,32},{1,49},{17,1},{33,17},{49,33},{2,50}... | collective-permute-start | bytes 3145736 | tf_op jit(solution)/shard_map/ppermute | solution.py:21
  84.2 1.2 copy-start.3
  85.4 1.2 copy-start.4
  120.2 5.6 %collective-permute-start.6 = (bf16[8,8,64,128]{3,2,1,0:T(8,128)(2,1)S(1)}, bf16[8,8,64,128]{3,2,1,0:T(8,128)(2,1)S(1)}, u32[]{:S(2)}, u32[]{:S(2)}) collective-permute-start(bf16[8,8,64,128]{3,2,1,0:T(8,128)(2,1)S(1)} %get-tuple-element.14), channel_id=1, source_target_pairs={{0,8},{8,0},{1,9},{9,1},{2,10},{10,2},{3,11},{11,3},{4,12},{12,4},... | collective-permute-start | bytes 3145736 | tf_op jit(solution)/shard_map/ppermute | solution.py:279
  122.3 3.3 %collective-permute-start.7 = (f32[8,8,64]{2,1,0:T(8,128)S(1)}, f32[8,8,64]{2,1,0:T(8,128)S(1)}, u32[]{:S(2)}, u32[]{:S(2)}) collective-permute-start(f32[8,8,64]{2,1,0:T(8,128)S(1)} %bitcast.71), channel_id=1, source_target_pairs={{0,8},{8,0},{1,9},{9,1},{2,10},{10,2},{3,11},{11,3},{4,12},{12,4},... | collective-permute-start | bytes 49160 | tf_op jit(solution)/shard_map/ppermute | solution.py:280
  128.1 35.0 %all-to-all-start = ((bf16[8,528,128]{2,1,0:T(8,128)(2,1)}), bf16[8,528,128]{2,1,0:T(8,128)(2,1)S(1)}, u32[]{:S(2)}, u32[]{:S(2)}) async-start(bf16[8,528,128]{2,1,0:T(8,128)(2,1)} %fusion.1), calls=%async_computation | async-start | bytes 2162688 | tf_op jit(solution)/shard_map/all_to_all | solution.py:290
  185.6 6.8 %collective-permute-start.8 = (bf16[8,64,128]{2,1,0:T(8,128)(2,1)S(1)}, bf16[8,64,128]{2,1,0:T(8,128)(2,1)S(1)}, u32[]{:S(2)}, u32[]{:S(2)}) collective-permute-start(bf16[8,64,128]{2,1,0:T(8,128)(2,1)S(1)} %all_to_all.10), channel_id=1, source_target_pairs={{0,448},{64,0},{128,64},{192,128},{256,192},{320,256},{384,320},{4... | collective-permute-start | bytes 393224 | tf_op jit(solution)/shard_map/ppermute | solution.py:21
  187.5 8.1 %collective-permute-start.11 = (bf16[8,64,128]{2,1,0:T(8,128)(2,1)S(1)}, bf16[8,64,128]{2,1,0:T(8,128)(2,1)S(1)}, u32[]{:S(2)}, u32[]{:S(2)}) collective-permute-start(bf16[8,64,128]{2,1,0:T(8,128)(2,1)S(1)} %all_to_all.10), channel_id=1, source_target_pairs={{0,64},{64,128},{128,192},{192,256},{256,320},{320,384},{384,448},... | collective-permute-start | bytes 393224 | tf_op jit(solution)/shard_map/ppermute | solution.py:21
  192.4 6.8 %collective-permute-start.9 = (bf16[8,64,128]{2,1,0:T(8,128)(2,1)S(1)}, bf16[8,64,128]{2,1,0:T(8,128)(2,1)S(1)}, u32[]{:S(2)}, u32[]{:S(2)}) collective-permute-start(bf16[8,64,128]{2,1,0:T(8,128)(2,1)S(1)} %collective-permute-done.8), channel_id=1, source_target_pairs={{0,448},{64,0},{128,64},{192,128},{256,192},{320,256},{384,320},{4... | collective-permute-start | bytes 393224 | tf_op jit(solution)/shard_map/ppermute | solution.py:21
  195.6 8.1 %collective-permute-start.12 = (bf16[8,64,128]{2,1,0:T(8,128)(2,1)S(1)}, bf16[8,64,128]{2,1,0:T(8,128)(2,1)S(1)}, u32[]{:S(2)}, u32[]{:S(2)}) collective-permute-start(bf16[8,64,128]{2,1,0:T(8,128)(2,1)S(1)} %collective-permute-done.11), channel_id=1, source_target_pairs={{0,64},{64,128},{128,192},{192,256},{256,320},{320,384},{384,448},... | collective-permute-start | bytes 393224 | tf_op jit(solution)/shard_map/ppermute | solution.py:21
  199.3 6.8 %collective-permute-start.10 = (bf16[8,64,128]{2,1,0:T(8,128)(2,1)S(1)}, bf16[8,64,128]{2,1,0:T(8,128)(2,1)S(1)}, u32[]{:S(2)}, u32[]{:S(2)}) collective-permute-start(bf16[8,64,128]{2,1,0:T(8,128)(2,1)S(1)} %collective-permute-done.9), channel_id=1, source_target_pairs={{0,448},{64,0},{128,64},{192,128},{256,192},{320,256},{384,320},{4... | collective-permute-start | bytes 393224 | tf_op jit(solution)/shard_map/ppermute | solution.py:21
  203.6 8.1 %collective-permute-start.13 = (bf16[8,64,128]{2,1,0:T(8,128)(2,1)S(1)}, bf16[8,64,128]{2,1,0:T(8,128)(2,1)S(1)}, u32[]{:S(2)}, u32[]{:S(2)}) collective-permute-start(bf16[8,64,128]{2,1,0:T(8,128)(2,1)S(1)} %collective-permute-done.12), channel_id=1, source_target_pairs={{0,64},{64,128},{128,192},{192,256},{256,320},{320,384},{384,448},... | collective-permute-start | bytes 393224 | tf_op jit(solution)/shard_map/ppermute | solution.py:21
  206.1 7.5 %collective-permute-start.15 = (bf16[4,64,128]{2,1,0:T(8,128)(2,1)S(1)}, bf16[4,64,128]{2,1,0:T(8,128)(2,1)S(1)}, u32[]{:S(2)}, u32[]{:S(2)}) collective-permute-start(bf16[4,64,128]{2,1,0:T(8,128)(2,1)S(1)} %slice.42), channel_id=1, source_target_pairs={{0,448},{64,0},{128,64},{192,128},{256,192},{320,256},{384,320},{4... | collective-permute-start | bytes 196616 | tf_op jit(solution)/shard_map/ppermute | solution.py:21
  211.7 7.4 %collective-permute-start.14 = (bf16[4,64,128]{2,1,0:T(8,128)(2,1)S(1)}, bf16[4,64,128]{2,1,0:T(8,128)(2,1)S(1)}, u32[]{:S(2)}, u32[]{:S(2)}) collective-permute-start(bf16[4,64,128]{2,1,0:T(8,128)(2,1)S(1)} %slice.41), channel_id=1, source_target_pairs={{0,64},{64,128},{128,192},{192,256},{256,320},{320,384},{384,448},... | collective-permute-start | bytes 196616 | tf_op jit(solution)/shard_map/ppermute | solution.py:21
  219.2 41.1 %copy-start.1 = (bf16[8,8,64,128]{3,2,1,0:T(8,128)(2,1)}, bf16[8,8,64,128]{3,2,1,0:T(8,128)(2,1)S(1)}, u32[]{:S(2)}) copy-start(bf16[8,8,64,128]{3,2,1,0:T(8,128)(2,1)S(1)} %bitcast_dynamic-update-slice_fusion.refs_0_) | copy-start | bytes 3145732
  219.2 28.8 %collective-permute-start.16 = (bf16[8,8,64,128]{3,2,1,0:T(8,128)(2,1)S(1)}, bf16[8,8,64,128]{3,2,1,0:T(8,128)(2,1)S(1)}, u32[]{:S(2)}, u32[]{:S(2)}) collective-permute-start(bf16[8,8,64,128]{3,2,1,0:T(8,128)(2,1)S(1)} %bitcast_dynamic-update-slice_fusion.refs_0_), channel_id=1, source_target_pairs={{0,48},{16,0},{32,16},{48,32},{1,49},{17,1},{33,17},{49,33},{2,50}... | collective-permute-start | bytes 3145736 | tf_op jit(solution)/shard_map/ppermute | solution.py:21
  224.1 25.8 %collective-permute-start.17 = (bf16[8,8,64,128]{3,2,1,0:T(8,128)(2,1)S(1)}, bf16[8,8,64,128]{3,2,1,0:T(8,128)(2,1)S(1)}, u32[]{:S(2)}, u32[]{:S(2)}) collective-permute-start(bf16[8,8,64,128]{3,2,1,0:T(8,128)(2,1)S(1)} %bitcast_dynamic-update-slice_fusion.refs_0_), channel_id=1, source_target_pairs={{0,16},{16,32},{32,48},{48,0},{1,17},{17,33},{33,49},{49,1},{2,18}... | collective-permute-start | bytes 3145736 | tf_op jit(solution)/shard_map/ppermute | solution.py:21
  248.0 12.3 %collective-permute-start.19 = (bf16[4,8,64,128]{3,2,1,0:T(8,128)(2,1)S(1)}, bf16[4,8,64,128]{3,2,1,0:T(8,128)(2,1)S(1)}, u32[]{:S(2)}, u32[]{:S(2)}) collective-permute-start(bf16[4,8,64,128]{3,2,1,0:T(8,128)(2,1)S(1)} %slice.44), channel_id=1, source_target_pairs={{0,48},{16,0},{32,16},{48,32},{1,49},{17,1},{33,17},{49,33},{2,50}... | collective-permute-start | bytes 1572872 | tf_op jit(solution)/shard_map/ppermute | solution.py:21
  250.0 11.8 %collective-permute-start.18 = (bf16[4,8,64,128]{3,2,1,0:T(8,128)(2,1)S(1)}, bf16[4,8,64,128]{3,2,1,0:T(8,128)(2,1)S(1)}, u32[]{:S(2)}, u32[]{:S(2)}) collective-permute-start(bf16[4,8,64,128]{3,2,1,0:T(8,128)(2,1)S(1)} %slice.43), channel_id=1, source_target_pairs={{0,16},{16,32},{32,48},{48,0},{1,17},{17,33},{33,49},{49,1},{2,18}... | collective-permute-start | bytes 1572872 | tf_op jit(solution)/shard_map/ppermute | solution.py:21
  261.9 2.2 copy-start
  264.1 1.2 copy-start.2
Sparse Core Ops, SparseCore 0:
  10.3 47.9 all-gather.3
Sparse Core Ops, SparseCore 1:
  124.9 67.4 all-gather.5

commit v2 on v1

--- a/solution.py
+++ b/solution.py
@@ -21,23 +21,26 @@
     return lax.ppermute(value, axis, [(i, (i + by) % n) for i in range(n)])
 
 
-def ring_gather(value, axis):
+def far_first(n):
+    return sorted(range(1, n), key=lambda d: -min(d, n - d))
+
+
+def exchange(pieces, axis):
+    arrived = list(pieces)
+    for d in far_first(len(pieces)):
+        arrived[d] = shift(pieces[d], axis, d)
+    return arrived
+
+
+def gather_pieces(value, axis):
     n = lax.axis_size(axis)
-    pieces = [value] + [None] * (n - 1)
-    behind = ahead = value
-    for d in range(1, (n + 1) // 2):
-        behind = shift(behind, axis, 1)
-        ahead = shift(ahead, axis, -1)
-        pieces[n - d], pieces[d] = behind, ahead
-    if n % 2 == 0:
-        half = value.shape[0] // 2
-        pieces[n // 2] = jnp.concatenate(
-            [shift(behind[:half], axis, 1), shift(ahead[half:], axis, -1)], axis=0
-        )
+    pieces = [value] * n
+    for d in far_first(n):
+        pieces[d] = shift(value, axis, -d)
     return pieces
 
 
-def attend_kernel(scale, slot_ref, q_ref, cos_ref, sin_ref, *refs):
+def attend_kernel(scale, slot_ref, place_ref, q_ref, cos_ref, sin_ref, *refs):
     key_refs, value_refs = refs[:4], refs[4:8]
     out_ref, lse_ref, q_scr, k_scr, s_scr, m_scr, l_scr, acc_scr, used = refs[8:]
     prompt = pl.program_id(0)
@@ -126,14 +129,14 @@
         total = jnp.where(none, 1.0, total)
         out = (acc_scr[span] / total).astype(out_ref.dtype)
         for c in range(halves):
-            out_ref[c, g, 0] = out[c * part : (c + 1) * part]
+            out_ref[c, place_ref[g], 0] = out[c * part : (c + 1) * part]
         lse = jnp.where(none, EMPTY, m_scr[span] * scale + jnp.log(total))
-        lse_ref[0, g : g + 1, :] = jnp.sum(
+        lse_ref[0, pl.ds(place_ref[g], 1), :] = jnp.sum(
             jnp.where(row == column, lse, 0.0), axis=0, keepdims=True
         )
 
 
-def attend(slots, query, cosine, sine, keys, values, halves):
+def attend(slots, place, query, cosine, sine, keys, values, halves):
     prompts, rows, features = query.shape
     listed, width = cosine.shape[1:]
     group = features // width
@@ -141,7 +144,7 @@
     most = MOST * len(keys)
     part = rows // halves
     whole = pl.BlockSpec(memory_space=pltpu.VMEM)
-    table = pl.BlockSpec((1, listed, width), lambda j, s: (j, 0, 0))
+    table = pl.BlockSpec((1, listed, width), lambda j, s, p: (j, 0, 0))
     return pl.pallas_call(
         functools.partial(attend_kernel, width**-0.5),
         out_shape=(
@@ -149,13 +152,13 @@
             jax.ShapeDtypeStruct((prompts, group, rows), jnp.float32),
         ),
         grid_spec=pltpu.PrefetchScalarGridSpec(
-            num_scalar_prefetch=1,
+            num_scalar_prefetch=2,
             grid=(prompts,),
-            in_specs=[pl.BlockSpec((1, rows, features), lambda j, s: (j, 0, 0)), table, table]
+            in_specs=[pl.BlockSpec((1, rows, features), lambda j, s, p: (j, 0, 0)), table, table]
             + [whole] * 8,
             out_specs=(
-                pl.BlockSpec((halves, group, 1, part, width), lambda j, s: (0, 0, j, 0, 0)),
-                pl.BlockSpec((1, group, rows), lambda j, s: (j, 0, 0)),
+                pl.BlockSpec((halves, group, 1, part, width), lambda j, s, p: (0, 0, j, 0, 0)),
+                pl.BlockSpec((1, group, rows), lambda j, s, p: (j, 0, 0)),
             ),
             scratch_shapes=[
                 pltpu.VMEM((rows * group, width), jnp.bfloat16),
@@ -168,49 +171,35 @@
             ],
         ),
         compiler_params=pltpu.CompilerParams(vmem_limit_bytes=48 * 1024 * 1024),
-    )(slots, query, cosine, sine, *keys, *values)
+    )(slots, place, query, cosine, sine, *keys, *values)
 
 
 def project_kernel(columns, where_ref, *refs):
-    pieces, weight_ref = refs[:columns], refs[columns]
-    out_ref, acc = refs[columns + 1 :]
-    step = pl.program_id(0)
-    heads, rows = pieces[0].shape[1:3]
+    pieces, weight_ref, out_ref = refs[:columns], refs[columns], refs[columns + 1]
+    heads, rows = pieces[0].shape[:2]
     left = jnp.concatenate(
-        [jnp.concatenate([p[0, h] for h in range(heads)], axis=1) for p in pieces], axis=0
+        [jnp.concatenate([p[h] for h in range(heads)], axis=1) for p in pieces], axis=0
     )
     right = jnp.concatenate([weight_ref[h, 0] for h in range(heads)], axis=0)
-    term = jnp.dot(left, right, preferred_element_type=jnp.float32)
-
-    @pl.when(step == 0)
-    def _():
-        acc[...] = term
-
-    @pl.when(step > 0)
-    def _():
-        acc[...] += term
-
-    @pl.when(step == pl.num_programs(0) - 1)
-    def _():
-        for d in range(columns):
-            at = pl.multiple_of(where_ref[pl.num_programs(0) + d] * rows, rows)
-            out_ref[pl.ds(at, rows), :] = acc[d * rows : (d + 1) * rows].astype(out_ref.dtype)
+    term = jnp.dot(left, right, preferred_element_type=jnp.float32).astype(out_ref.dtype)
+    for d in range(columns):
+        at = pl.multiple_of(where_ref[pl.num_programs(0) + d] * rows, rows)
+        out_ref[0, pl.ds(at, rows), :] = term[d * rows : (d + 1) * rows]
 
 
 def project(where, pieces, weight):
     columns = len(pieces)
-    steps, heads, rows, width = pieces[0].shape
-    out_columns = weight.shape[-1]
+    heads, rows, width = pieces[0].shape
+    owners, out_columns = weight.shape[1], weight.shape[3]
     return pl.pallas_call(
         functools.partial(project_kernel, columns),
-        out_shape=jax.ShapeDtypeStruct((columns * rows, out_columns), jnp.bfloat16),
+        out_shape=jax.ShapeDtypeStruct((owners, columns * rows, out_columns), jnp.bfloat16),
         grid_spec=pltpu.PrefetchScalarGridSpec(
             num_scalar_prefetch=1,
-            grid=(steps,),
-            in_specs=[pl.BlockSpec((1, heads, rows, width), lambda s, w: (s, 0, 0, 0))] * columns
+            grid=(owners,),
+            in_specs=[pl.BlockSpec((heads, rows, width), lambda s, w: (0, 0, 0))] * columns
             + [pl.BlockSpec((heads, 1, width, out_columns), lambda s, w: (0, w[s], 0, 0))],
-            out_specs=pl.BlockSpec((columns * rows, out_columns), lambda s, w: (0, 0)),
-            scratch_shapes=[pltpu.VMEM((columns * rows, out_columns), jnp.float32)],
+            out_specs=pl.BlockSpec((1, columns * rows, out_columns), lambda s, w: (s, 0, 0)),
         ),
         compiler_params=pltpu.CompilerParams(vmem_limit_bytes=32 * 1024 * 1024),
     )(where, *pieces, weight)
@@ -251,16 +240,18 @@
 
     asked = jnp.concatenate([passage_list, targets, row_counts[:, None]], axis=1)
     asked = lax.all_gather(asked, ROW, axis=0, tiled=True)
-    near_offsets = lax.all_gather(offsets, COL, axis=0, tiled=True)
+    near_offsets = jnp.concatenate(gather_pieces(offsets, COL))
     query = lax.all_gather(queries, ROW, axis=0, tiled=True)
-    weight = lax.all_gather(out_weight, "head", axis=0, tiled=True)
+    weight = out_weight.reshape(group, width, -1)
+    weight = lax.all_to_all(weight, ROW, split_axis=0, concat_axis=0, tiled=True)
+    weight = lax.all_gather(weight[None], "head", axis=0, tiled=True)
 
     near = columns * held
     local = asked[:, :listed] - y * near
     mine = (local >= 0) & (local < near)
     ahead = (local // held - x) % columns
     slots = jnp.where(mine, ahead * held + local % held, -1)
-    same = local[..., None] == jnp.arange(near, dtype=jnp.int32)
+    same = slots[..., None] == jnp.arange(near, dtype=jnp.int32)
     delta = asked[:, listed : 2 * listed] - jnp.sum(
         jnp.where(same, near_offsets, 0), axis=-1
     )
@@ -271,7 +262,8 @@
     cosine = jnp.concatenate([cosine, cosine], axis=-1)
     sine = jnp.concatenate([-sine, sine], axis=-1)
 
-    out, lse = attend(slots.reshape(-1), query, cosine, sine, keys, values, halves)
+    place = (jnp.arange(group, dtype=jnp.int32) - y) % rows_of
+    out, lse = attend(slots.reshape(-1), place, query, cosine, sine, keys, values, halves)
 
     lse = jnp.transpose(lse.reshape(rows_of, group, halves, half_rows), (2, 1, 0, 3))
     swap = [(i, 1 - i) for i in range(2)]
@@ -286,8 +278,9 @@
     parts = jnp.moveaxis(three_parts(lse), 0, 1).reshape(group, -1, width)
     extra = parts.shape[1]
     parts = jnp.pad(parts, ((0, 0), (0, -extra % 16), (0, 0)))
-    sent = jnp.concatenate([out, parts], axis=1)
-    got = lax.all_to_all(sent, ROW, split_axis=0, concat_axis=0, tiled=True)
+    got = jnp.stack(
+        exchange([jnp.concatenate([out[d], parts[d]], axis=0) for d in range(rows_of)], ROW)
+    )
     outs = got[:, : rows_of * half_rows].reshape(rows_of, rows_of, half_rows, width)
     lses = got[:, rows_of * half_rows : rows_of * half_rows + extra].astype(jnp.float32)
     lses = jnp.sum(lses.reshape(rows_of, 3, rows_of, half_rows), axis=1)
@@ -296,15 +289,16 @@
     attended = jnp.where(live[..., None], attended, 0.0).astype(jnp.bfloat16)
 
     attended = lax.all_to_all(attended, "head", split_axis=0, concat_axis=0, tiled=True)
-    pieces = ring_gather(jnp.stack(ring_gather(attended, ROW)), COL)
     where = jnp.concatenate(
         [
             (y + jnp.arange(rows_of, dtype=jnp.int32)) % rows_of,
             (x + jnp.arange(columns, dtype=jnp.int32)) % columns,
         ]
     )
-    weight = weight.reshape(lax.axis_size("head"), group, width, -1)
-    return project(where, pieces, weight)[None]
+    terms = project(where, gather_pieces(attended, COL), weight)
+    terms = exchange([terms[d] for d in range(rows_of)], ROW)
+    total = functools.reduce(jnp.add, [t.astype(jnp.float32) for t in terms])
+    return total.astype(jnp.bfloat16)[None]
 
 
 def solution(mesh):

time: 281 us -> 273 us (0.972)
  starting transfers between devices: 78.4 us -> 141 us
  blocking collectives: 53.6 us -> 16.3 us
  Pallas kernels: 36 us -> 14.9 us
  local copies, waits for them, and re-layouts: 10.8 us -> 5.17 us
  waiting for transfers between devices: 76.5 us -> 73.5 us
    ppermute x18 -> x26, starting transfers between devices: 69.1 us -> 119 us  [shift(): return lax.ppermute(value, axis, [(i, (i + by) % n) for i in range(n)])]
    all_to_all x1 -> x0, blocking collectives: 21.3 us -> none  [body(): lax.all_to_all(attended, 'head', split_axis=0, concat_axis=0, tiled=True)]
    all_to_all x1 -> x2, waiting for transfers between devices: 29.8 us -> 9.07 us  [the longest x1 9.07 us: body(): lax.all_to_all(attended, 'head', split_axis=0, concat_axis=0, tiled=True)]
    pallas_call x1, Pallas kernels: 31.7 us -> 11.5 us  [attend(): pl.pallas_call(functools.partial(attend_kernel, width ** (-0.5)), out_sha...]
    unnamed x1 -> x0, blocking collectives: 19.2 us -> none
    ppermute x18 -> x26, waiting for transfers between devices: 45.1 us -> 61.8 us  [shift(): return lax.ppermute(value, axis, [(i, (i + by) % n) for i in range(n)])]
    all_to_all x1 -> x2, starting transfers between devices: 4.97 us -> 17.6 us  [the longest x1 10.3 us: body(): lax.all_to_all(attended, 'head', split_axis=0, concat_axis=0, tiled=True)]
    unnamed x21 -> x20, local copies, waits for them, and re-layouts: 8.11 us -> 2.34 us
  transfers between devices with their start and end apart: 23 -> 32, of which waited for: 11 -> 15; matrix products, arithmetic and copies ran while one was open for 3% -> 3% of each run, Pallas kernels for 0% -> 4%
where the time goes in v2:
time: 273 us; the launch traced here: 270 us
  starting transfers between devices  141 us (52%)
  waiting for transfers between devices  73.5 us (27%)
  blocking collectives  16.3 us (6%)
  Pallas kernels  14.9 us (5%)
  between operations  14.7 us (5%)
  local copies, waits for them, and re-layouts  5.17 us (2%)
  other arithmetic  4.87 us (2%)
    ppermute x26, starting transfers between devices, shift(): return lax.ppermute(value, axis, [(i, (i + by) % n) for i in range(n)])  119 us
    ppermute x26, waiting for transfers between devices, shift(): return lax.ppermute(value, axis, [(i, (i + by) % n) for i in range(n)])  61.8 us
    all_gather x1, blocking collectives, body(): asked = lax.all_gather(asked, ROW, axis=0, tiled=True)  16.3 us
    pallas_call x1, Pallas kernels, attend(): pl.pallas_call(functools.partial(attend_kernel, width ** (-0.5)), out_sha...  11.5 us
    all_to_all x1, starting transfers between devices, body(): lax.all_to_all(attended, 'head', split_axis=0, concat_axis=0, tiled=True)  10.3 us
    all_to_all x1, waiting for transfers between devices, body(): lax.all_to_all(attended, 'head', split_axis=0, concat_axis=0, tiled=True)  9.07 us
    all_to_all x1, starting transfers between devices, body(): lax.all_to_all(weight, ROW, split_axis=0, concat_axis=0, tiled=True)  7.24 us
  transfers between devices with their start and end apart: 32, of which 15 were waited for; matrix products, arithmetic and copies ran while one was open for 3% of the time, Pallas kernels for 4%

profile of v2, /device:TPU:6, one launch (start us, length us, event | category | flops | bytes accessed | tf_op | source)
XLA Modules:
  0.0 270.2 jit_solution(8715981398372452988)
XLA Ops:
  7.3 7.2 %all-to-all-start.1 = ((bf16[8,128,256]{2,1,0:T(8,128)(2,1)}), bf16[8,128,256]{2,1,0:T(8,128)(2,1)}, u32[]{:S(2)}, u32[]{:S(2)}) async-start(bf16[8,128,256]{2,1,0:T(8,128)(2,1)} %bitcast.116), calls=%async_computation.1 | async-start | bytes 1048576 | tf_op jit(solution)/shard_map/all_to_all | solution.py:246
  14.6 4.8 %collective-permute-start.4 = (bf16[16,256,128]{2,1,0:T(8,128)(2,1)S(1)}, bf16[16,256,128]{2,1,0:T(8,128)(2,1)S(1)}, u32[]{:S(2)}, u32[]{:S(2)}) collective-permute-start(bf16[16,256,128]{2,1,0:T(8,128)(2,1)S(1)} %copy-done.1), channel_id=1, source_target_pairs={{0,16},{16,32},{32,48},{48,0},{1,17},{17,33},{33,49},{49,1},{2,18}... | collective-permute-start | bytes 3145736 | tf_op jit(solution)/shard_map/ppermute | solution.py:21
  23.3 5.1 %collective-permute-start.8 = (bf16[16,256,128]{2,1,0:T(8,128)(2,1)}, bf16[16,256,128]{2,1,0:T(8,128)(2,1)}, u32[]{:S(2)}, u32[]{:S(2)}) collective-permute-start(bf16[16,256,128]{2,1,0:T(8,128)(2,1)} %refs_4_.1), channel_id=1, source_target_pairs={{0,16},{16,32},{32,48},{48,0},{1,17},{17,33},{33,49},{49,1},{2,18}... | collective-permute-start | bytes 3145736 | tf_op jit(solution)/shard_map/ppermute | solution.py:21
  28.4 3.9 %collective-permute-start.2 = (s32[16]{0:T(128)S(1)}, s32[16]{0:T(128)S(1)}, u32[]{:S(2)}, u32[]{:S(2)}) collective-permute-start(s32[16]{0:T(128)S(1)} %copy-done.3), channel_id=1, source_target_pairs={{0,16},{16,32},{32,48},{48,0},{1,17},{17,33},{33,49},{49,1},{2,18}... | collective-permute-start | bytes 200 | tf_op jit(solution)/shard_map/ppermute | solution.py:21
  33.1 16.3 %all-gather.1 = s32[8,1,33]{2,1,0:T(1,128)S(1)} all-gather(s32[1,1,33]{2,1,0:T(1,128)S(1)} %add_bitcast_fusion), channel_id=1, replica_groups=mesh['lib_0'=8,'lib_1'=4,'ctx'=2,'head'=8] {'lib_0'}, dimensions={0}, use_global_device_ids=true | all-gather | bytes 1188 | tf_op jit(solution)/shard_map/all_gather | solution.py:242
  51.4 3.9 %collective-permute-start.7 = (bf16[16,256,128]{2,1,0:T(8,128)(2,1)}, bf16[16,256,128]{2,1,0:T(8,128)(2,1)}, u32[]{:S(2)}, u32[]{:S(2)}) collective-permute-start(bf16[16,256,128]{2,1,0:T(8,128)(2,1)} %collective-permute-done.6.refs_5_), channel_id=1, source_target_pairs={{0,48},{16,0},{32,16},{48,32},{1,49},{17,1},{33,17},{49,33},{2,50}... | collective-permute-start | bytes 3145736 | tf_op jit(solution)/shard_map/ppermute | solution.py:21
  55.6 10.0 %collective-permute-done.2 = s32[16]{0:T(128)S(1)} collective-permute-done((s32[16]{0:T(128)S(1)}, s32[16]{0:T(128)S(1)}, u32[]{:S(2)}, u32[]{:S(2)}) %collective-permute-start.2) | collective-permute-done | bytes 96 | tf_op jit(solution)/shard_map/ppermute | solution.py:21
  65.6 3.8 %collective-permute-start.1 = (s32[16]{0:T(128)S(1)}, s32[16]{0:T(128)S(1)}, u32[]{:S(2)}, u32[]{:S(2)}) collective-permute-start(s32[16]{0:T(128)S(1)} %copy-done.3), channel_id=1, source_target_pairs={{0,32},{16,48},{32,0},{48,16},{1,33},{17,49},{33,1},{49,17},{2,34}... | collective-permute-start | bytes 200 | tf_op jit(solution)/shard_map/ppermute | solution.py:21
  69.4 19.8 %collective-permute-done.1 = s32[16]{0:T(128)S(1)} collective-permute-done((s32[16]{0:T(128)S(1)}, s32[16]{0:T(128)S(1)}, u32[]{:S(2)}, u32[]{:S(2)}) %collective-permute-start.1) | collective-permute-done | bytes 96 | tf_op jit(solution)/shard_map/ppermute | solution.py:21
  91.2 4.7 %collective-permute-done = s32[16]{0:T(128)S(1)} collective-permute-done((s32[16]{0:T(128)S(1)}, s32[16]{0:T(128)S(1)}, u32[]{:S(2)}, u32[]{:S(2)}) %collective-permute-start) | collective-permute-done | bytes 96 | tf_op jit(solution)/shard_map/ppermute | solution.py:21
  96.9 11.5 %shard_map.82 = (bf16[2,8,8,64,128]{4,3,2,1,0:T(8,128)(2,1)}, f32[8,8,128]{2,1,0:T(8,128)S(1)}) custom-call(s32[128]{0:T(128)S(1)} %reshape.122.slot_ref, s32[8]{0:T(128)S(1)} %and_select_fusion.place_ref, bf16[8,128,1024]{2,1,0:T(8,128)(2,1)} %all-gather.5.cloned.1.call-done.q_ref, f32[8,16,128]{2,1,0:T(8,128)S(1)} %get-tuple-element.43.cos_ref, ...), custom_call_target="tpu_custom_call" | custom-call | tf_op jit(solution)/shard_map/pallas_call | solution.py:148
  118.3 22.4 %collective-permute-start.11 = (bf16[528,128]{1,0:T(8,128)(2,1)S(1)}, bf16[528,128]{1,0:T(8,128)(2,1)S(1)}, u32[]{:S(2)}, u32[]{:S(2)}) collective-permute-start(bf16[528,128]{1,0:T(8,128)(2,1)S(1)} %pad_maximum_fusion), channel_id=1, source_target_pairs={{0,64},{64,128},{128,192},{192,256},{256,320},{320,384},{384,448},... | collective-permute-start | bytes 405512 | tf_op jit(solution)/shard_map/ppermute | solution.py:21
  142.7 9.1 %collective-permute-start.13 = (bf16[528,128]{1,0:T(8,128)(2,1)S(1)}, bf16[528,128]{1,0:T(8,128)(2,1)S(1)}, u32[]{:S(2)}, u32[]{:S(2)}) collective-permute-start(bf16[528,128]{1,0:T(8,128)(2,1)S(1)} %pad_maximum_fusion.2), channel_id=1, source_target_pairs={{0,192},{64,256},{128,320},{192,384},{256,448},{320,0},{384,64},{4... | collective-permute-start | bytes 405512 | tf_op jit(solution)/shard_map/ppermute | solution.py:21
  151.8 6.5 %collective-permute-start.14 = (bf16[528,128]{1,0:T(8,128)(2,1)S(1)}, bf16[528,128]{1,0:T(8,128)(2,1)S(1)}, u32[]{:S(2)}, u32[]{:S(2)}) collective-permute-start(bf16[528,128]{1,0:T(8,128)(2,1)S(1)} %pad_maximum_fusion.3), channel_id=1, source_target_pairs={{0,256},{64,320},{128,384},{192,448},{256,0},{320,64},{384,128},{4... | collective-permute-start | bytes 405512 | tf_op jit(solution)/shard_map/ppermute | solution.py:21
  158.3 6.9 %collective-permute-start.15 = (bf16[528,128]{1,0:T(8,128)(2,1)S(1)}, bf16[528,128]{1,0:T(8,128)(2,1)S(1)}, u32[]{:S(2)}, u32[]{:S(2)}) collective-permute-start(bf16[528,128]{1,0:T(8,128)(2,1)S(1)} %pad_maximum_fusion.4), channel_id=1, source_target_pairs={{0,320},{64,384},{128,448},{192,0},{256,64},{320,128},{384,192},{4... | collective-permute-start | bytes 405512 | tf_op jit(solution)/shard_map/ppermute | solution.py:21
  167.2 2.5 collective-permute-start.17
  169.7 4.4 %collective-permute-done.13 = bf16[528,128]{1,0:T(8,128)(2,1)S(1)} collective-permute-done((bf16[528,128]{1,0:T(8,128)(2,1)S(1)}, bf16[528,128]{1,0:T(8,128)(2,1)S(1)}, u32[]{:S(2)}, u32[]{:S(2)}) %collective-permute-start.13) | collective-permute-done | bytes 135200 | tf_op jit(solution)/shard_map/ppermute | solution.py:21
  174.3 3.3 %collective-permute-done.15 = bf16[528,128]{1,0:T(8,128)(2,1)S(1)} collective-permute-done((bf16[528,128]{1,0:T(8,128)(2,1)S(1)}, bf16[528,128]{1,0:T(8,128)(2,1)S(1)}, u32[]{:S(2)}, u32[]{:S(2)}) %collective-permute-start.15) | collective-permute-done | bytes 135200 | tf_op jit(solution)/shard_map/ppermute | solution.py:21
  177.5 4.0 %collective-permute-done.16 = bf16[528,128]{1,0:T(8,128)(2,1)S(1)} collective-permute-done((bf16[528,128]{1,0:T(8,128)(2,1)S(1)}, bf16[528,128]{1,0:T(8,128)(2,1)S(1)}, u32[]{:S(2)}, u32[]{:S(2)}) %collective-permute-start.16) | collective-permute-done | bytes 135200 | tf_op jit(solution)/shard_map/ppermute | solution.py:21
  184.3 10.3 %all-to-all-start = ((bf16[8,64,128]{2,1,0:T(8,128)(2,1)}), bf16[8,64,128]{2,1,0:T(8,128)(2,1)S(1)}, u32[]{:S(2)}, u32[]{:S(2)}) async-start(bf16[8,64,128]{2,1,0:T(8,128)(2,1)} %select_convert_fusion), calls=%async_computation | async-start | bytes 262144 | tf_op jit(solution)/shard_map/all_to_all | solution.py:291
  194.6 9.1 %all-to-all-done.refs_0_ = bf16[8,64,128]{2,1,0:T(8,128)(2,1)S(1)} async-done(((bf16[8,64,128]{2,1,0:T(8,128)(2,1)}), bf16[8,64,128]{2,1,0:T(8,128)(2,1)S(1)}, u32[]{:S(2)}, u32[]{:S(2)}) %all-to-all-start) | async-done | bytes 131104 | tf_op jit(solution)/shard_map/all_to_all | solution.py:291
  205.6 2.7 collective-permute-start.19
  208.3 4.4 %collective-permute-start.20 = (bf16[8,64,128]{2,1,0:T(8,128)(2,1)S(1)}, bf16[8,64,128]{2,1,0:T(8,128)(2,1)S(1)}, u32[]{:S(2)}, u32[]{:S(2)}) collective-permute-start(bf16[8,64,128]{2,1,0:T(8,128)(2,1)S(1)} %all-to-all-done.refs_0_), channel_id=1, source_target_pairs={{0,16},{16,32},{32,48},{48,0},{1,17},{17,33},{33,49},{49,1},{2,18}... | collective-permute-start | bytes 393224 | tf_op jit(solution)/shard_map/ppermute | solution.py:21
  214.0 2.5 collective-permute-done.20.refs_3_
  218.7 3.4 %shard_map.83 = bf16[8,256,256]{2,1,0:T(8,128)(2,1)S(1)} custom-call(s32[12]{0:T(128)S(1)} %pad_add_fusion.where_ref, bf16[8,64,128]{2,1,0:T(8,128)(2,1)S(1)} %all-to-all-done.refs_0_, bf16[8,64,128]{2,1,0:T(8,128)(2,1)S(1)} %collective-permute-done.18.refs_1_, bf16[8,64,128]{2,1,0:T(8,128)(2,1)S(1)} %collective-permute-done.19.refs_2_, ...), custom_call_target="tpu_custom_call" | custom-call | tf_op jit(solution)/shard_map/pallas_call | solution.py:194
  222.1 5.6 %collective-permute-start.27 = (bf16[256,256]{1,0:T(8,128)(2,1)S(1)}, bf16[256,256]{1,0:T(8,128)(2,1)S(1)}, u32[]{:S(2)}, u32[]{:S(2)}) collective-permute-start(bf16[256,256]{1,0:T(8,128)(2,1)S(1)} %get-tuple-element.14), channel_id=1, source_target_pairs={{0,448},{64,0},{128,64},{192,128},{256,192},{320,256},{384,320},{4... | collective-permute-start | bytes 393224 | tf_op jit(solution)/shard_map/ppermute | solution.py:21
  227.7 3.4 %collective-permute-start.26 = (bf16[256,256]{1,0:T(8,128)(2,1)S(1)}, bf16[256,256]{1,0:T(8,128)(2,1)S(1)}, u32[]{:S(2)}, u32[]{:S(2)}) collective-permute-start(bf16[256,256]{1,0:T(8,128)(2,1)S(1)} %get-tuple-element.15), channel_id=1, source_target_pairs={{0,384},{64,448},{128,0},{192,64},{256,128},{320,192},{384,256},{4... | collective-permute-start | bytes 393224 | tf_op jit(solution)/shard_map/ppermute | solution.py:21
  231.2 4.7 %collective-permute-start.25 = (bf16[256,256]{1,0:T(8,128)(2,1)S(1)}, bf16[256,256]{1,0:T(8,128)(2,1)S(1)}, u32[]{:S(2)}, u32[]{:S(2)}) collective-permute-start(bf16[256,256]{1,0:T(8,128)(2,1)S(1)} %get-tuple-element.16), channel_id=1, source_target_pairs={{0,320},{64,384},{128,448},{192,0},{256,64},{320,128},{384,192},{4... | collective-permute-start | bytes 393224 | tf_op jit(solution)/shard_map/ppermute | solution.py:21
  235.9 4.0 %collective-permute-start.24 = (bf16[256,256]{1,0:T(8,128)(2,1)S(1)}, bf16[256,256]{1,0:T(8,128)(2,1)S(1)}, u32[]{:S(2)}, u32[]{:S(2)}) collective-permute-start(bf16[256,256]{1,0:T(8,128)(2,1)S(1)} %get-tuple-element.17), channel_id=1, source_target_pairs={{0,256},{64,320},{128,384},{192,448},{256,0},{320,64},{384,128},{4... | collective-permute-start | bytes 393224 | tf_op jit(solution)/shard_map/ppermute | solution.py:21
  239.9 3.7 %collective-permute-start.23 = (bf16[256,256]{1,0:T(8,128)(2,1)S(1)}, bf16[256,256]{1,0:T(8,128)(2,1)S(1)}, u32[]{:S(2)}, u32[]{:S(2)}) collective-permute-start(bf16[256,256]{1,0:T(8,128)(2,1)S(1)} %get-tuple-element.18), channel_id=1, source_target_pairs={{0,192},{64,256},{128,320},{192,384},{256,448},{320,0},{384,64},{4... | collective-permute-start | bytes 393224 | tf_op jit(solution)/shard_map/ppermute | solution.py:21
  243.6 6.0 %collective-permute-start.22 = (bf16[256,256]{1,0:T(8,128)(2,1)S(1)}, bf16[256,256]{1,0:T(8,128)(2,1)S(1)}, u32[]{:S(2)}, u32[]{:S(2)}) collective-permute-start(bf16[256,256]{1,0:T(8,128)(2,1)S(1)} %get-tuple-element.19), channel_id=1, source_target_pairs={{0,128},{64,192},{128,256},{192,320},{256,384},{320,448},{384,0},{... | collective-permute-start | bytes 393224 | tf_op jit(solution)/shard_map/ppermute | solution.py:21
  254.6 6.7 %collective-permute-done.22 = bf16[256,256]{1,0:T(8,128)(2,1)S(1)} collective-permute-done((bf16[256,256]{1,0:T(8,128)(2,1)S(1)}, bf16[256,256]{1,0:T(8,128)(2,1)S(1)}, u32[]{:S(2)}, u32[]{:S(2)}) %collective-permute-start.22) | collective-permute-done | bytes 131104 | tf_op jit(solution)/shard_map/ppermute | solution.py:21
  (107 shorter events, 38.8 us)
Async XLA Ops:
  6.5 90.3 %all-gather.5.cloned.1.call-start = ((), (), s32[]{:S(2)}) async-start(), calls=%async_computation.2 | async-start | bytes 2359296 | tf_op jit(solution)/shard_map/all_gather | solution.py:244
  7.3 42.1 %all-to-all-start.1 = ((bf16[8,128,256]{2,1,0:T(8,128)(2,1)}), bf16[8,128,256]{2,1,0:T(8,128)(2,1)}, u32[]{:S(2)}, u32[]{:S(2)}) async-start(bf16[8,128,256]{2,1,0:T(8,128)(2,1)} %bitcast.116), calls=%async_computation.1 | async-start | bytes 1048576 | tf_op jit(solution)/shard_map/all_to_all | solution.py:246
  14.5 201.9 %all-gather.7.cloned.1.call-start = ((), (), s32[]{:S(2)}) async-start(), calls=%async_computation.3 | async-start | bytes 4718592 | tf_op jit(solution)/shard_map/all_gather | solution.py:247
  14.6 34.9 %collective-permute-start.4 = (bf16[16,256,128]{2,1,0:T(8,128)(2,1)S(1)}, bf16[16,256,128]{2,1,0:T(8,128)(2,1)S(1)}, u32[]{:S(2)}, u32[]{:S(2)}) collective-permute-start(bf16[16,256,128]{2,1,0:T(8,128)(2,1)S(1)} %copy-done.1), channel_id=1, source_target_pairs={{0,16},{16,32},{32,48},{48,0},{1,17},{17,33},{33,49},{49,1},{2,18}... | collective-permute-start | bytes 3145736 | tf_op jit(solution)/shard_map/ppermute | solution.py:21
  19.4 32.0 %collective-permute-start.6 = (bf16[16,256,128]{2,1,0:T(8,128)(2,1)}, bf16[16,256,128]{2,1,0:T(8,128)(2,1)}, u32[]{:S(2)}, u32[]{:S(2)}) collective-permute-start(bf16[16,256,128]{2,1,0:T(8,128)(2,1)} %refs_4_.1), channel_id=1, source_target_pairs={{0,48},{16,0},{32,16},{48,32},{1,49},{17,1},{33,17},{49,33},{2,50}... | collective-permute-start | bytes 3145736 | tf_op jit(solution)/shard_map/ppermute | solution.py:21
  21.4 75.4 %collective-permute-start.3 = (bf16[16,256,128]{2,1,0:T(8,128)(2,1)S(1)}, bf16[16,256,128]{2,1,0:T(8,128)(2,1)}, u32[]{:S(2)}, u32[]{:S(2)}) collective-permute-start(bf16[16,256,128]{2,1,0:T(8,128)(2,1)S(1)} %copy-done.1), channel_id=1, source_target_pairs={{0,48},{16,0},{32,16},{48,32},{1,49},{17,1},{33,17},{49,33},{2,50}... | collective-permute-start | bytes 3145736 | tf_op jit(solution)/shard_map/ppermute | solution.py:21
  23.3 73.5 %collective-permute-start.8 = (bf16[16,256,128]{2,1,0:T(8,128)(2,1)}, bf16[16,256,128]{2,1,0:T(8,128)(2,1)}, u32[]{:S(2)}, u32[]{:S(2)}) collective-permute-start(bf16[16,256,128]{2,1,0:T(8,128)(2,1)} %refs_4_.1), channel_id=1, source_target_pairs={{0,16},{16,32},{32,48},{48,0},{1,17},{17,33},{33,49},{49,1},{2,18}... | collective-permute-start | bytes 3145736 | tf_op jit(solution)/shard_map/ppermute | solution.py:21
  28.4 37.2 %collective-permute-start.2 = (s32[16]{0:T(128)S(1)}, s32[16]{0:T(128)S(1)}, u32[]{:S(2)}, u32[]{:S(2)}) collective-permute-start(s32[16]{0:T(128)S(1)} %copy-done.3), channel_id=1, source_target_pairs={{0,16},{16,32},{32,48},{48,0},{1,17},{17,33},{33,49},{49,1},{2,18}... | collective-permute-start | bytes 200 | tf_op jit(solution)/shard_map/ppermute | solution.py:21
  49.5 47.3 %collective-permute-start.5 = (bf16[16,256,128]{2,1,0:T(8,128)(2,1)S(1)}, bf16[16,256,128]{2,1,0:T(8,128)(2,1)}, u32[]{:S(2)}, u32[]{:S(2)}) collective-permute-start(bf16[16,256,128]{2,1,0:T(8,128)(2,1)S(1)} %collective-permute-done.4.refs_3_), channel_id=1, source_target_pairs={{0,16},{16,32},{32,48},{48,0},{1,17},{17,33},{33,49},{49,1},{2,18}... | collective-permute-start | bytes 3145736 | tf_op jit(solution)/shard_map/ppermute | solution.py:21
  51.4 45.4 %collective-permute-start.7 = (bf16[16,256,128]{2,1,0:T(8,128)(2,1)}, bf16[16,256,128]{2,1,0:T(8,128)(2,1)}, u32[]{:S(2)}, u32[]{:S(2)}) collective-permute-start(bf16[16,256,128]{2,1,0:T(8,128)(2,1)} %collective-permute-done.6.refs_5_), channel_id=1, source_target_pairs={{0,48},{16,0},{32,16},{48,32},{1,49},{17,1},{33,17},{49,33},{2,50}... | collective-permute-start | bytes 3145736 | tf_op jit(solution)/shard_map/ppermute | solution.py:21
  65.6 23.7 %collective-permute-start.1 = (s32[16]{0:T(128)S(1)}, s32[16]{0:T(128)S(1)}, u32[]{:S(2)}, u32[]{:S(2)}) collective-permute-start(s32[16]{0:T(128)S(1)} %copy-done.3), channel_id=1, source_target_pairs={{0,32},{16,48},{32,0},{48,16},{1,33},{17,49},{33,1},{49,17},{2,34}... | collective-permute-start | bytes 200 | tf_op jit(solution)/shard_map/ppermute | solution.py:21
  89.3 6.6 %collective-permute-start = (s32[16]{0:T(128)S(1)}, s32[16]{0:T(128)S(1)}, u32[]{:S(2)}, u32[]{:S(2)}) collective-permute-start(s32[16]{0:T(128)S(1)} %copy-done.3), channel_id=1, source_target_pairs={{0,48},{16,0},{32,16},{48,32},{1,49},{17,1},{33,17},{49,33},{2,50}... | collective-permute-start | bytes 200 | tf_op jit(solution)/shard_map/ppermute | solution.py:21
  108.5 6.3 %collective-permute-start.10 = (f32[8,8,64]{2,1,0:T(8,128)S(1)}, f32[8,8,64]{2,1,0:T(8,128)S(1)}, u32[]{:S(2)}, u32[]{:S(2)}) collective-permute-start(f32[8,8,64]{2,1,0:T(8,128)S(1)} %bitcast.122), channel_id=1, source_target_pairs={{0,8},{8,0},{1,9},{9,1},{2,10},{10,2},{3,11},{11,3},{4,12},{12,4},... | collective-permute-start | bytes 49160 | tf_op jit(solution)/shard_map/ppermute | solution.py:272
  112.3 4.7 %collective-permute-start.9 = (bf16[8,8,64,128]{3,2,1,0:T(8,128)(2,1)S(1)}, bf16[8,8,64,128]{3,2,1,0:T(8,128)(2,1)S(1)}, u32[]{:S(2)}, u32[]{:S(2)}) collective-permute-start(bf16[8,8,64,128]{3,2,1,0:T(8,128)(2,1)S(1)} %get-tuple-element.12), channel_id=1, source_target_pairs={{0,8},{8,0},{1,9},{9,1},{2,10},{10,2},{3,11},{11,3},{4,12},{12,4},... | collective-permute-start | bytes 3145736 | tf_op jit(solution)/shard_map/ppermute | solution.py:271
  118.3 47.0 %collective-permute-start.11 = (bf16[528,128]{1,0:T(8,128)(2,1)S(1)}, bf16[528,128]{1,0:T(8,128)(2,1)S(1)}, u32[]{:S(2)}, u32[]{:S(2)}) collective-permute-start(bf16[528,128]{1,0:T(8,128)(2,1)S(1)} %pad_maximum_fusion), channel_id=1, source_target_pairs={{0,64},{64,128},{128,192},{192,256},{256,320},{320,384},{384,448},... | collective-permute-start | bytes 405512 | tf_op jit(solution)/shard_map/ppermute | solution.py:21
  140.7 26.5 %collective-permute-start.12 = (bf16[528,128]{1,0:T(8,128)(2,1)S(1)}, bf16[528,128]{1,0:T(8,128)(2,1)S(1)}, u32[]{:S(2)}, u32[]{:S(2)}) collective-permute-start(bf16[528,128]{1,0:T(8,128)(2,1)S(1)} %pad_maximum_fusion.1), channel_id=1, source_target_pairs={{0,128},{64,192},{128,256},{192,320},{256,384},{320,448},{384,0},{... | collective-permute-start | bytes 405512 | tf_op jit(solution)/shard_map/ppermute | solution.py:21
  142.7 31.5 %collective-permute-start.13 = (bf16[528,128]{1,0:T(8,128)(2,1)S(1)}, bf16[528,128]{1,0:T(8,128)(2,1)S(1)}, u32[]{:S(2)}, u32[]{:S(2)}) collective-permute-start(bf16[528,128]{1,0:T(8,128)(2,1)S(1)} %pad_maximum_fusion.2), channel_id=1, source_target_pairs={{0,192},{64,256},{128,320},{192,384},{256,448},{320,0},{384,64},{4... | collective-permute-start | bytes 405512 | tf_op jit(solution)/shard_map/ppermute | solution.py:21
  151.8 22.4 %collective-permute-start.14 = (bf16[528,128]{1,0:T(8,128)(2,1)S(1)}, bf16[528,128]{1,0:T(8,128)(2,1)S(1)}, u32[]{:S(2)}, u32[]{:S(2)}) collective-permute-start(bf16[528,128]{1,0:T(8,128)(2,1)S(1)} %pad_maximum_fusion.3), channel_id=1, source_target_pairs={{0,256},{64,320},{128,384},{192,448},{256,0},{320,64},{384,128},{4... | collective-permute-start | bytes 405512 | tf_op jit(solution)/shard_map/ppermute | solution.py:21
  158.3 19.2 %collective-permute-start.15 = (bf16[528,128]{1,0:T(8,128)(2,1)S(1)}, bf16[528,128]{1,0:T(8,128)(2,1)S(1)}, u32[]{:S(2)}, u32[]{:S(2)}) collective-permute-start(bf16[528,128]{1,0:T(8,128)(2,1)S(1)} %pad_maximum_fusion.4), channel_id=1, source_target_pairs={{0,320},{64,384},{128,448},{192,0},{256,64},{320,128},{384,192},{4... | collective-permute-start | bytes 405512 | tf_op jit(solution)/shard_map/ppermute | solution.py:21
  165.3 16.3 %collective-permute-start.16 = (bf16[528,128]{1,0:T(8,128)(2,1)S(1)}, bf16[528,128]{1,0:T(8,128)(2,1)S(1)}, u32[]{:S(2)}, u32[]{:S(2)}) collective-permute-start(bf16[528,128]{1,0:T(8,128)(2,1)S(1)} %pad_maximum_fusion.5), channel_id=1, source_target_pairs={{0,384},{64,448},{128,0},{192,64},{256,128},{320,192},{384,256},{4... | collective-permute-start | bytes 405512 | tf_op jit(solution)/shard_map/ppermute | solution.py:21
  167.2 15.1 %collective-permute-start.17 = (bf16[528,128]{1,0:T(8,128)(2,1)S(1)}, bf16[528,128]{1,0:T(8,128)(2,1)S(1)}, u32[]{:S(2)}, u32[]{:S(2)}) collective-permute-start(bf16[528,128]{1,0:T(8,128)(2,1)S(1)} %pad_maximum_fusion.6), channel_id=1, source_target_pairs={{0,448},{64,0},{128,64},{192,128},{256,192},{320,256},{384,320},{4... | collective-permute-start | bytes 405512 | tf_op jit(solution)/shard_map/ppermute | solution.py:21
  184.3 19.4 %all-to-all-start = ((bf16[8,64,128]{2,1,0:T(8,128)(2,1)}), bf16[8,64,128]{2,1,0:T(8,128)(2,1)S(1)}, u32[]{:S(2)}, u32[]{:S(2)}) async-start(bf16[8,64,128]{2,1,0:T(8,128)(2,1)} %select_convert_fusion), calls=%async_computation | async-start | bytes 262144 | tf_op jit(solution)/shard_map/all_to_all | solution.py:291
  203.7 9.1 %collective-permute-start.18 = (bf16[8,64,128]{2,1,0:T(8,128)(2,1)S(1)}, bf16[8,64,128]{2,1,0:T(8,128)(2,1)S(1)}, u32[]{:S(2)}, u32[]{:S(2)}) collective-permute-start(bf16[8,64,128]{2,1,0:T(8,128)(2,1)S(1)} %all-to-all-done.refs_0_), channel_id=1, source_target_pairs={{0,48},{16,0},{32,16},{48,32},{1,49},{17,1},{33,17},{49,33},{2,50}... | collective-permute-start | bytes 393224 | tf_op jit(solution)/shard_map/ppermute | solution.py:21
  205.6 8.4 %collective-permute-start.19 = (bf16[8,64,128]{2,1,0:T(8,128)(2,1)S(1)}, bf16[8,64,128]{2,1,0:T(8,128)(2,1)S(1)}, u32[]{:S(2)}, u32[]{:S(2)}) collective-permute-start(bf16[8,64,128]{2,1,0:T(8,128)(2,1)S(1)} %all-to-all-done.refs_0_), channel_id=1, source_target_pairs={{0,32},{16,48},{32,0},{48,16},{1,33},{17,49},{33,1},{49,17},{2,34}... | collective-permute-start | bytes 393224 | tf_op jit(solution)/shard_map/ppermute | solution.py:21
  208.3 8.1 %collective-permute-start.20 = (bf16[8,64,128]{2,1,0:T(8,128)(2,1)S(1)}, bf16[8,64,128]{2,1,0:T(8,128)(2,1)S(1)}, u32[]{:S(2)}, u32[]{:S(2)}) collective-permute-start(bf16[8,64,128]{2,1,0:T(8,128)(2,1)S(1)} %all-to-all-done.refs_0_), channel_id=1, source_target_pairs={{0,16},{16,32},{32,48},{48,0},{1,17},{17,33},{33,49},{49,1},{2,18}... | collective-permute-start | bytes 393224 | tf_op jit(solution)/shard_map/ppermute | solution.py:21
  222.1 21.4 %collective-permute-start.27 = (bf16[256,256]{1,0:T(8,128)(2,1)S(1)}, bf16[256,256]{1,0:T(8,128)(2,1)S(1)}, u32[]{:S(2)}, u32[]{:S(2)}) collective-permute-start(bf16[256,256]{1,0:T(8,128)(2,1)S(1)} %get-tuple-element.14), channel_id=1, source_target_pairs={{0,448},{64,0},{128,64},{192,128},{256,192},{320,256},{384,320},{4... | collective-permute-start | bytes 393224 | tf_op jit(solution)/shard_map/ppermute | solution.py:21
  227.7 21.9 %collective-permute-start.26 = (bf16[256,256]{1,0:T(8,128)(2,1)S(1)}, bf16[256,256]{1,0:T(8,128)(2,1)S(1)}, u32[]{:S(2)}, u32[]{:S(2)}) collective-permute-start(bf16[256,256]{1,0:T(8,128)(2,1)S(1)} %get-tuple-element.15), channel_id=1, source_target_pairs={{0,384},{64,448},{128,0},{192,64},{256,128},{320,192},{384,256},{4... | collective-permute-start | bytes 393224 | tf_op jit(solution)/shard_map/ppermute | solution.py:21
  231.2 20.4 %collective-permute-start.25 = (bf16[256,256]{1,0:T(8,128)(2,1)S(1)}, bf16[256,256]{1,0:T(8,128)(2,1)S(1)}, u32[]{:S(2)}, u32[]{:S(2)}) collective-permute-start(bf16[256,256]{1,0:T(8,128)(2,1)S(1)} %get-tuple-element.16), channel_id=1, source_target_pairs={{0,320},{64,384},{128,448},{192,0},{256,64},{320,128},{384,192},{4... | collective-permute-start | bytes 393224 | tf_op jit(solution)/shard_map/ppermute | solution.py:21
  235.9 16.4 %collective-permute-start.24 = (bf16[256,256]{1,0:T(8,128)(2,1)S(1)}, bf16[256,256]{1,0:T(8,128)(2,1)S(1)}, u32[]{:S(2)}, u32[]{:S(2)}) collective-permute-start(bf16[256,256]{1,0:T(8,128)(2,1)S(1)} %get-tuple-element.17), channel_id=1, source_target_pairs={{0,256},{64,320},{128,384},{192,448},{256,0},{320,64},{384,128},{4... | collective-permute-start | bytes 393224 | tf_op jit(solution)/shard_map/ppermute | solution.py:21
  239.9 14.7 %collective-permute-start.23 = (bf16[256,256]{1,0:T(8,128)(2,1)S(1)}, bf16[256,256]{1,0:T(8,128)(2,1)S(1)}, u32[]{:S(2)}, u32[]{:S(2)}) collective-permute-start(bf16[256,256]{1,0:T(8,128)(2,1)S(1)} %get-tuple-element.18), channel_id=1, source_target_pairs={{0,192},{64,256},{128,320},{192,384},{256,448},{320,0},{384,64},{4... | collective-permute-start | bytes 393224 | tf_op jit(solution)/shard_map/ppermute | solution.py:21
  243.6 17.7 %collective-permute-start.22 = (bf16[256,256]{1,0:T(8,128)(2,1)S(1)}, bf16[256,256]{1,0:T(8,128)(2,1)S(1)}, u32[]{:S(2)}, u32[]{:S(2)}) collective-permute-start(bf16[256,256]{1,0:T(8,128)(2,1)S(1)} %get-tuple-element.19), channel_id=1, source_target_pairs={{0,128},{64,192},{128,256},{192,320},{256,384},{320,448},{384,0},{... | collective-permute-start | bytes 393224 | tf_op jit(solution)/shard_map/ppermute | solution.py:21
  249.6 12.9 %collective-permute-start.21 = (bf16[256,256]{1,0:T(8,128)(2,1)S(1)}, bf16[256,256]{1,0:T(8,128)(2,1)S(1)}, u32[]{:S(2)}, u32[]{:S(2)}) collective-permute-start(bf16[256,256]{1,0:T(8,128)(2,1)S(1)} %get-tuple-element.13), channel_id=1, source_target_pairs={{0,64},{64,128},{128,192},{192,256},{256,320},{320,384},{384,448},... | collective-permute-start | bytes 393224 | tf_op jit(solution)/shard_map/ppermute | solution.py:21
  (6 other events, 174.7 us)
Sparse Core Ops, SparseCore 0:
  9.5 47.9 all-gather.4
  59.5 58.6 all-gather.6

commit v3 on v2

--- a/solution.py
+++ b/solution.py
@@ -40,138 +40,177 @@
     return pieces
 
 
-def attend_kernel(scale, slot_ref, place_ref, q_ref, cos_ref, sin_ref, *refs):
-    key_refs, value_refs = refs[:4], refs[4:8]
-    out_ref, lse_ref, q_scr, k_scr, s_scr, m_scr, l_scr, acc_scr, used = refs[8:]
+def attend_kernel(scale, pieces, first, last, slot_ref, place_ref, q_ref, cos_ref, sin_ref, *refs):
+    key_refs, value_refs, refs = refs[:pieces], refs[pieces : 2 * pieces], refs[2 * pieces :]
+    if not first:
+        (before_ref, before_lse_ref), refs = refs[:2], refs[2:]
+    out_ref, lse_ref, q_scr, tile, k_scr, s_scr, m_scr, l_scr, acc_scr, used, entry = refs
     prompt = pl.program_id(0)
-    listed = cos_ref.shape[1]
-    rows, width = q_ref.shape[1], cos_ref.shape[2]
+    listed, width = cos_ref.shape[1:]
+    rows = q_ref.shape[1]
     group = q_ref.shape[2] // width
     total_rows = rows * group
-    held = key_refs[0].shape[0]
-    log2e = 1.4426950408889634
-    for g in range(group):
-        q_scr[g * rows : (g + 1) * rows] = q_ref[0, :, g * width : (g + 1) * width]
-    m_scr[...] = jnp.full_like(m_scr, EMPTY)
-    l_scr[...] = jnp.zeros_like(l_scr)
-    acc_scr[...] = jnp.zeros_like(acc_scr)
-
-    def score(k, count):
-        slot = slot_ref[prompt * listed + k]
-
-        @pl.when(slot >= 0)
-        def _():
-            piece, at = slot // held, slot % held
-            for d in range(4):
-
-                @pl.when(piece == d)
-                def _():
-                    k_scr[...] = key_refs[d][at]
-
-            used[count] = slot
-            keys = k_scr[...].astype(jnp.float32)
-            cosine = cos_ref[0, pl.ds(k, 1), :]
-            sine = sin_ref[0, pl.ds(k, 1), :]
-            turned = keys * cosine + pltpu.roll(keys, width // 2, 1) * sine
-            turned = turned.astype(jnp.bfloat16)
-            for r in range(0, total_rows, CHUNK):
-                s = lax.dot_general(
-                    q_scr[r : r + CHUNK],
-                    turned,
-                    (((1,), (1,)), ((), ())),
-                    preferred_element_type=jnp.float32,
-                )
-                s_scr[count, r : r + CHUNK] = s
-                highest = m_scr[r : r + CHUNK]
-                for t in range(0, s.shape[1], width):
-                    highest = jnp.maximum(highest, s[:, t : t + width])
-                m_scr[r : r + CHUNK] = highest
-
-        return count + jnp.where(slot >= 0, 1, 0)
-
-    count = lax.fori_loop(0, listed, score, 0)
-    for r in range(0, total_rows, CHUNK):
-        m = jnp.max(m_scr[r : r + CHUNK], axis=1, keepdims=True)
-        m_scr[r : r + CHUNK] = jnp.broadcast_to(m, (CHUNK, width))
-
-    def weigh(t, carry):
-        slot = used[t]
-        piece, at = slot // held, slot % held
-        for d in range(4):
-
-            @pl.when(piece == d)
-            def _():
-                k_scr[...] = value_refs[d][at]
-
-        for r in range(0, total_rows, CHUNK):
-            m = m_scr[r : r + CHUNK]
-            s = s_scr[t, r : r + CHUNK]
-            parts = [
-                jnp.exp2((s[:, u : u + width] - m) * (scale * log2e))
-                for u in range(0, s.shape[1], width)
-            ]
-            l_scr[r : r + CHUNK] += functools.reduce(jnp.add, parts)
-            weights = jnp.concatenate(parts, axis=1).astype(jnp.bfloat16)
-            acc_scr[r : r + CHUNK] += jnp.dot(
-                weights, k_scr[...], preferred_element_type=jnp.float32
-            )
-        return carry
-
-    lax.fori_loop(0, count, weigh, 0)
+    held, tokens = key_refs[0].shape[:2]
+    factor = scale * 1.4426950408889634
     row = lax.broadcasted_iota(jnp.int32, (rows, rows), 0)
     column = lax.broadcasted_iota(jnp.int32, (rows, rows), 1)
-    halves = out_ref.shape[0]
-    part = rows // halves
-    none = count == 0
+    chunks = [slice(r, r + CHUNK) for r in range(0, total_rows, CHUNK)]
+
+    for g in range(group):
+        span = slice(g * rows, (g + 1) * rows)
+        q_scr[span] = q_ref[0, :, g * width : (g + 1) * width]
+        if not first:
+            lse = jnp.sum(
+                jnp.where(row == column, before_lse_ref[0, g : g + 1, :], 0.0), axis=1, keepdims=True
+            )
+            lse = jnp.broadcast_to(lse * (1.0 / scale), (rows, width))
+            m_scr[span] = lse
+            l_scr[span] = lse
+    if first:
+        m_scr[...] = jnp.full_like(m_scr, EMPTY)
+
+    def note(k, count):
+        slot = slot_ref[prompt * listed + k]
+        used[count] = slot
+        entry[count] = k
+        return count + jnp.where(slot >= 0, 1, 0)
+
+    count = lax.fori_loop(0, listed, note, 0)
+    pairs = (count + 1) // 2
+
+    def fetch(refs, slot):
+        if pieces == 1:
+            return refs[0][slot]
+        for d in range(pieces):
+
+            @pl.when(slot // held == d)
+            def _():
+                tile[...] = refs[d][slot % held]
+
+        return tile[...]
+
+    def score(t, carry):
+        for b in range(2):
+            i = jnp.minimum(2 * t + b, count - 1)
+            keys = fetch(key_refs, used[i]).astype(jnp.float32)
+            cosine = cos_ref[0, pl.ds(entry[i], 1), :]
+            sine = sin_ref[0, pl.ds(entry[i], 1), :]
+            turned = keys * cosine + pltpu.roll(keys, width // 2, 1) * sine
+            k_scr[b * tokens : (b + 1) * tokens] = turned.astype(jnp.bfloat16)
+        both = 2 * t + 1 < count
+        for span in chunks:
+            s = lax.dot_general(
+                q_scr[span],
+                k_scr[...],
+                (((1,), (1,)), ((), ())),
+                preferred_element_type=jnp.float32,
+            )
+            highest = m_scr[span]
+            for u in range(0, 2 * tokens, width):
+                part = s[:, u : u + width]
+                if u >= tokens:
+                    part = jnp.where(both, part, EMPTY)
+                s_scr[t, span, u : u + width] = part
+                highest = jnp.maximum(highest, part)
+            m_scr[span] = highest
+        return carry
+
+    lax.fori_loop(0, pairs, score, 0)
+    lane = lax.broadcasted_iota(jnp.int32, (CHUNK, width), 1)
+    for span in chunks:
+        m = jnp.max(m_scr[span], axis=1, keepdims=True)
+        m = jnp.broadcast_to(m, (CHUNK, width))
+        m_scr[span] = m
+        if first:
+            l_scr[span] = jnp.zeros_like(m)
+            acc_scr[span] = jnp.zeros_like(m)
+        else:
+            weight = jnp.exp2((l_scr[span] - m) * factor)
+            l_scr[span] = jnp.where(lane == 0, weight, 0.0)
+            acc_scr[span] = before_ref[0, span] * weight
+
+    def weigh(t, carry):
+        for b in range(2):
+            i = jnp.minimum(2 * t + b, count - 1)
+            k_scr[b * tokens : (b + 1) * tokens] = fetch(value_refs, used[i])
+        for span in chunks:
+            m = m_scr[span]
+            parts = [
+                jnp.exp2((s_scr[t, span, u : u + width] - m) * factor)
+                for u in range(0, 2 * tokens, width)
+            ]
+            l_scr[span] += functools.reduce(jnp.add, parts)
+            weights = jnp.concatenate([p.astype(jnp.bfloat16) for p in parts], axis=1)
+            acc_scr[span] += jnp.dot(weights, k_scr[...], preferred_element_type=jnp.float32)
+        return carry
+
+    lax.fori_loop(0, pairs, weigh, 0)
     for g in range(group):
         span = slice(g * rows, (g + 1) * rows)
         total = jnp.sum(l_scr[span], axis=1, keepdims=True)
-        total = jnp.where(none, 1.0, total)
-        out = (acc_scr[span] / total).astype(out_ref.dtype)
-        for c in range(halves):
-            out_ref[c, place_ref[g], 0] = out[c * part : (c + 1) * part]
-        lse = jnp.where(none, EMPTY, m_scr[span] * scale + jnp.log(total))
-        lse_ref[0, pl.ds(place_ref[g], 1), :] = jnp.sum(
-            jnp.where(row == column, lse, 0.0), axis=0, keepdims=True
-        )
-
-
-def attend(slots, place, query, cosine, sine, keys, values, halves):
+        if first:
+            total = jnp.where(count == 0, 1.0, total)
+        out = acc_scr[span] * (1.0 / total)
+        lse = m_scr[span] * scale + jnp.log(total)
+        lse = jnp.sum(jnp.where(row == column, lse, 0.0), axis=0, keepdims=True)
+        if last:
+            halves = out_ref.shape[0]
+            part = rows // halves
+            for c in range(halves):
+                out_ref[c, place_ref[g], 0] = out[c * part : (c + 1) * part].astype(out_ref.dtype)
+            lse_ref[0, pl.ds(place_ref[g], 1), :] = lse
+        else:
+            out_ref[0, span] = out
+            lse_ref[0, g : g + 1, :] = lse
+
+
+def attend(slots, place, query, cosine, sine, keys, values, before, halves):
     prompts, rows, features = query.shape
     listed, width = cosine.shape[1:]
     group = features // width
     tokens = keys[0].shape[1]
     most = MOST * len(keys)
-    part = rows // halves
     whole = pl.BlockSpec(memory_space=pltpu.VMEM)
     table = pl.BlockSpec((1, listed, width), lambda j, s, p: (j, 0, 0))
+    state = [
+        pl.BlockSpec((1, rows * group, width), lambda j, s, p: (j, 0, 0)),
+        pl.BlockSpec((1, group, rows), lambda j, s, p: (j, 0, 0)),
+    ]
+    if halves:
+        part = rows // halves
+        out = jax.ShapeDtypeStruct((halves, group, prompts, part, width), jnp.bfloat16)
+        out_spec = pl.BlockSpec((halves, group, 1, part, width), lambda j, s, p: (0, 0, j, 0, 0))
+    else:
+        out = jax.ShapeDtypeStruct((prompts, rows * group, width), jnp.float32)
+        out_spec = state[0]
+    work = prompts * most // 2 * rows * group * tokens
     return pl.pallas_call(
-        functools.partial(attend_kernel, width**-0.5),
-        out_shape=(
-            jax.ShapeDtypeStruct((halves, group, prompts, part, width), jnp.bfloat16),
-            jax.ShapeDtypeStruct((prompts, group, rows), jnp.float32),
-        ),
+        functools.partial(attend_kernel, width**-0.5, len(keys), before is None, bool(halves)),
+        out_shape=(out, jax.ShapeDtypeStruct((prompts, group, rows), jnp.float32)),
         grid_spec=pltpu.PrefetchScalarGridSpec(
             num_scalar_prefetch=2,
             grid=(prompts,),
             in_specs=[pl.BlockSpec((1, rows, features), lambda j, s, p: (j, 0, 0)), table, table]
-            + [whole] * 8,
-            out_specs=(
-                pl.BlockSpec((halves, group, 1, part, width), lambda j, s, p: (0, 0, j, 0, 0)),
-                pl.BlockSpec((1, group, rows), lambda j, s, p: (j, 0, 0)),
-            ),
+            + [whole] * (2 * len(keys))
+            + (state if before else []),
+            out_specs=(out_spec, state[1]),
             scratch_shapes=[
                 pltpu.VMEM((rows * group, width), jnp.bfloat16),
                 pltpu.VMEM((tokens, width), jnp.bfloat16),
-                pltpu.VMEM((most, rows * group, tokens), jnp.float32),
+                pltpu.VMEM((2 * tokens, width), jnp.bfloat16),
+                pltpu.VMEM((most // 2, rows * group, 2 * tokens), jnp.float32),
                 pltpu.VMEM((rows * group, width), jnp.float32),
                 pltpu.VMEM((rows * group, width), jnp.float32),
                 pltpu.VMEM((rows * group, width), jnp.float32),
-                pltpu.SMEM((most,), jnp.int32),
+                pltpu.SMEM((most + 1,), jnp.int32),
+                pltpu.SMEM((most + 1,), jnp.int32),
             ],
         ),
+        cost_estimate=pl.CostEstimate(
+            flops=4 * work * width, bytes_accessed=8 * work, transcendentals=work
+        ),
         compiler_params=pltpu.CompilerParams(vmem_limit_bytes=48 * 1024 * 1024),
-    )(slots, place, query, cosine, sine, *keys, *values)
+    )(slots, place, query, cosine, sine, *keys, *values, *(before or ()))
 
 
 def project_kernel(columns, where_ref, *refs):
@@ -233,14 +272,17 @@
     halves = lax.axis_size("ctx")
     half_rows = prompt_rows // halves
 
-    keys = [passage_keys, shift(passage_keys, COL, -1), None, shift(passage_keys, COL, 1)]
-    values = [passage_values, shift(passage_values, COL, -1), None, shift(passage_values, COL, 1)]
+    near_offsets = gather_pieces(offsets, COL)
+    own_keys, own_values, near_offsets = lax.optimization_barrier(
+        (passage_keys, passage_values, near_offsets)
+    )
+    keys = [own_keys, shift(own_keys, COL, -1), None, shift(own_keys, COL, 1)]
+    values = [own_values, shift(own_values, COL, -1), None, shift(own_values, COL, 1)]
     keys[2] = shift(keys[3], COL, 1)
     values[2] = shift(values[1], COL, -1)
 
     asked = jnp.concatenate([passage_list, targets, row_counts[:, None]], axis=1)
     asked = lax.all_gather(asked, ROW, axis=0, tiled=True)
-    near_offsets = jnp.concatenate(gather_pieces(offsets, COL))
     query = lax.all_gather(queries, ROW, axis=0, tiled=True)
     weight = out_weight.reshape(group, width, -1)
     weight = lax.all_to_all(weight, ROW, split_axis=0, concat_axis=0, tiled=True)
@@ -250,10 +292,11 @@
     local = asked[:, :listed] - y * near
     mine = (local >= 0) & (local < near)
     ahead = (local // held - x) % columns
-    slots = jnp.where(mine, ahead * held + local % held, -1)
+    within = local % held
+    slots = jnp.where(mine, ahead * held + within, -1)
     same = slots[..., None] == jnp.arange(near, dtype=jnp.int32)
     delta = asked[:, listed : 2 * listed] - jnp.sum(
-        jnp.where(same, near_offsets, 0), axis=-1
+        jnp.where(same, jnp.concatenate(near_offsets), 0), axis=-1
     )
     half = width // 2
     inverse = theta_base ** (-2.0 * jnp.arange(half, dtype=jnp.float32) / width)
@@ -263,7 +306,16 @@
     sine = jnp.concatenate([-sine, sine], axis=-1)
 
     place = (jnp.arange(group, dtype=jnp.int32) - y) % rows_of
-    out, lse = attend(slots.reshape(-1), place, query, cosine, sine, keys, values, halves)
+    early = (0, 1, 3)
+    soon = jnp.where(mine & (ahead != 2), jnp.where(ahead == 3, 2, ahead) * held + within, -1)
+    late = jnp.where(mine & (ahead == 2), within, -1)
+    before = attend(
+        soon.reshape(-1), place, query, cosine, sine,
+        [keys[d] for d in early], [values[d] for d in early], None, 0,
+    )
+    out, lse = attend(
+        late.reshape(-1), place, query, cosine, sine, keys[2:3], values[2:3], before, halves
+    )
 
     lse = jnp.transpose(lse.reshape(rows_of, group, halves, half_rows), (2, 1, 0, 3))
     swap = [(i, 1 - i) for i in range(2)]

time: 273 us -> 268 us (0.982)
  starting transfers between devices: 141 us -> 116 us
  Pallas kernels: 14.9 us -> 36.9 us
    ppermute x26, starting transfers between devices: 119 us -> 93.8 us  [shift(): return lax.ppermute(value, axis, [(i, (i + by) % n) for i in range(n)])]
    pallas_call x1 -> x2, Pallas kernels: 11.5 us -> 33.5 us  [attend(): pl.pallas_call(functools.partial(attend_kernel, width ** (-0.5), len(keys...]
  transfers between devices with their start and end apart: 32 -> 32, of which waited for: 15 -> 13; matrix products, arithmetic and copies ran while one was open for 3% -> 2% of each run, Pallas kernels for 4% -> 13%
where the time goes in v3:
time: 268 us; the launch traced here: 265 us
  starting transfers between devices  116 us (43%)
  waiting for transfers between devices  71.2 us (27%)
  Pallas kernels  36.9 us (14%)
  blocking collectives  16.3 us (6%)
  between operations  14.7 us (5%)
  local copies, waits for them, and re-layouts  5.76 us (2%)
  other arithmetic  4.9 us (2%)
    ppermute x26, starting transfers between devices, shift(): return lax.ppermute(value, axis, [(i, (i + by) % n) for i in range(n)])  93.8 us
    ppermute x26, waiting for transfers between devices, shift(): return lax.ppermute(value, axis, [(i, (i + by) % n) for i in range(n)])  60.7 us
    pallas_call x2, Pallas kernels, attend(): pl.pallas_call(functools.partial(attend_kernel, width ** (-0.5), len(keys...  33.5 us
    all_gather x1, blocking collectives, body(): asked = lax.all_gather(asked, ROW, axis=0, tiled=True)  16.3 us
    all_to_all x1, starting transfers between devices, body(): lax.all_to_all(attended, 'head', split_axis=0, concat_axis=0, tiled=True)  10.3 us
    all_to_all x1, waiting for transfers between devices, body(): lax.all_to_all(attended, 'head', split_axis=0, concat_axis=0, tiled=True)  9.07 us
    all_to_all x1, starting transfers between devices, body(): lax.all_to_all(weight, ROW, split_axis=0, concat_axis=0, tiled=True)  7.11 us
  transfers between devices with their start and end apart: 32, of which 13 were waited for; matrix products, arithmetic and copies ran while one was open for 2% of the time, Pallas kernels for 13%

profile of v3, /device:TPU:6, one launch (start us, length us, event | category | flops | bytes accessed | tf_op | source)
XLA Modules:
  0.0 265.4 jit_solution(15427905117324180642)
XLA Ops:
  7.3 7.1 %all-to-all-start.1 = ((bf16[8,128,256]{2,1,0:T(8,128)(2,1)}), bf16[8,128,256]{2,1,0:T(8,128)(2,1)S(1)}, u32[]{:S(2)}, u32[]{:S(2)}) async-start(bf16[8,128,256]{2,1,0:T(8,128)(2,1)} %bitcast.116), calls=%async_computation.1 | async-start | bytes 1048576 | tf_op jit(solution)/shard_map/all_to_all | solution.py:288
  14.4 2.7 %collective-permute-start = (s32[16]{0:T(128)S(1)}, s32[16]{0:T(128)S(1)}, u32[]{:S(2)}, u32[]{:S(2)}) collective-permute-start(s32[16]{0:T(128)S(1)} %copy-done.4), channel_id=1, source_target_pairs={{0,48},{16,0},{32,16},{48,32},{1,49},{17,1},{33,17},{49,33},{2,50}... | collective-permute-start | bytes 200 | tf_op jit(solution)/shard_map/ppermute | solution.py:21
  17.2 4.8 %collective-permute-start.1 = (s32[16]{0:T(128)S(1)}, s32[16]{0:T(128)S(1)}, u32[]{:S(2)}, u32[]{:S(2)}) collective-permute-start(s32[16]{0:T(128)S(1)} %copy-done.4), channel_id=1, source_target_pairs={{0,32},{16,48},{32,0},{48,16},{1,33},{17,49},{33,1},{49,17},{2,34}... | collective-permute-start | bytes 200 | tf_op jit(solution)/shard_map/ppermute | solution.py:21
  24.2 3.2 %collective-permute-done.2 = s32[16]{0:T(128)S(1)} collective-permute-done((s32[16]{0:T(128)S(1)}, s32[16]{0:T(128)S(1)}, u32[]{:S(2)}, u32[]{:S(2)}) %collective-permute-start.2) | collective-permute-done | bytes 96 | tf_op jit(solution)/shard_map/ppermute | solution.py:21
  27.4 3.4 %collective-permute-start.3 = (bf16[16,256,128]{2,1,0:T(8,128)(2,1)S(1)}, bf16[16,256,128]{2,1,0:T(8,128)(2,1)}, u32[]{:S(2)}, u32[]{:S(2)}) collective-permute-start(bf16[16,256,128]{2,1,0:T(8,128)(2,1)S(1)} %copy-done.1), channel_id=1, source_target_pairs={{0,16},{16,32},{32,48},{48,0},{1,17},{17,33},{33,49},{49,1},{2,18}... | collective-permute-start | bytes 3145736 | tf_op jit(solution)/shard_map/ppermute | solution.py:21
  30.9 2.4 collective-permute-start.5
  34.0 16.3 %all-gather.1 = s32[8,1,33]{2,1,0:T(1,128)S(1)} all-gather(s32[1,1,33]{2,1,0:T(1,128)S(1)} %add_bitcast_fusion), channel_id=1, replica_groups=mesh['lib_0'=8,'lib_1'=4,'ctx'=2,'head'=8] {'lib_0'}, dimensions={0}, use_global_device_ids=true | all-gather | bytes 1188 | tf_op jit(solution)/shard_map/all_gather | solution.py:285
  52.8 4.7 %collective-permute-start.8 = (bf16[16,256,128]{2,1,0:T(8,128)(2,1)}, bf16[16,256,128]{2,1,0:T(8,128)(2,1)}, u32[]{:S(2)}, u32[]{:S(2)}) collective-permute-start(bf16[16,256,128]{2,1,0:T(8,128)(2,1)} %refs_3_), channel_id=1, source_target_pairs={{0,16},{16,32},{32,48},{48,0},{1,17},{17,33},{33,49},{49,1},{2,18}... | collective-permute-start | bytes 3145736 | tf_op jit(solution)/shard_map/ppermute | solution.py:21
  58.7 3.5 %collective-permute-start.4 = (bf16[16,256,128]{2,1,0:T(8,128)(2,1)}, bf16[16,256,128]{2,1,0:T(8,128)(2,1)S(1)}, u32[]{:S(2)}, u32[]{:S(2)}) collective-permute-start(bf16[16,256,128]{2,1,0:T(8,128)(2,1)} %collective-permute-done.3.refs_2_), channel_id=1, source_target_pairs={{0,16},{16,32},{32,48},{48,0},{1,17},{17,33},{33,49},{49,1},{2,18}... | collective-permute-start | bytes 3145736 | tf_op jit(solution)/shard_map/ppermute | solution.py:21
  65.4 17.4 %collective-permute-done.7.refs_1_ = bf16[16,256,128]{2,1,0:T(8,128)(2,1)} collective-permute-done((bf16[16,256,128]{2,1,0:T(8,128)(2,1)S(1)}, bf16[16,256,128]{2,1,0:T(8,128)(2,1)}, u32[]{:S(2)}, u32[]{:S(2)}) %collective-permute-start.7) | collective-permute-done | bytes 1048608 | tf_op jit(solution)/shard_map/ppermute | solution.py:21
  84.1 18.1 %shard_map.82 = (f32[8,1024,128]{2,1,0:T(8,128)}, f32[8,8,128]{2,1,0:T(8,128)S(1)}) custom-call(s32[128]{0:T(128)S(1)} %reshape.126.slot_ref, s32[8]{0:T(128)S(1)} %and_select_fusion.1.place_ref, bf16[8,128,1024]{2,1,0:T(8,128)(2,1)} %all-gather.5.cloned.1.call-done.q_ref, f32[8,16,128]{2,1,0:T(8,128)S(1)} %get-tuple-element.64.cos_ref, ...), custom_call_target="tpu_custom_call" | custom-call | flops 3221225472 | bytes 50331648 | tf_op jit(solution)/shard_map/pallas_call | solution.py:187
  102.2 15.4 %shard_map.83 = (bf16[2,8,8,64,128]{4,3,2,1,0:T(8,128)(2,1)S(1)}, f32[8,8,128]{2,1,0:T(8,128)S(1)}) custom-call(s32[128]{0:T(128)S(1)} %reshape.125.slot_ref, s32[8]{0:T(128)S(1)} %and_select_fusion.1.place_ref, bf16[8,128,1024]{2,1,0:T(8,128)(2,1)} %all-gather.5.cloned.1.call-done.q_ref, f32[8,16,128]{2,1,0:T(8,128)S(1)} %get-tuple-element.64.cos_ref, ...), custom_call_target="tpu_custom_call" | custom-call | flops 1073741824 | bytes 16777216 | tf_op jit(solution)/shard_map/pallas_call | solution.py:187
  120.0 2.4 collective-permute-start.10
  126.8 9.0 %collective-permute-start.16 = (bf16[528,128]{1,0:T(8,128)(2,1)S(1)}, bf16[528,128]{1,0:T(8,128)(2,1)S(1)}, u32[]{:S(2)}, u32[]{:S(2)}) collective-permute-start(bf16[528,128]{1,0:T(8,128)(2,1)S(1)} %pad_maximum_fusion.5), channel_id=1, source_target_pairs={{0,384},{64,448},{128,0},{192,64},{256,128},{320,192},{384,256},{4... | collective-permute-start | bytes 405512 | tf_op jit(solution)/shard_map/ppermute | solution.py:21
  135.8 6.1 %collective-permute-start.15 = (bf16[528,128]{1,0:T(8,128)(2,1)S(1)}, bf16[528,128]{1,0:T(8,128)(2,1)S(1)}, u32[]{:S(2)}, u32[]{:S(2)}) collective-permute-start(bf16[528,128]{1,0:T(8,128)(2,1)S(1)} %pad_maximum_fusion.4), channel_id=1, source_target_pairs={{0,320},{64,384},{128,448},{192,0},{256,64},{320,128},{384,192},{4... | collective-permute-start | bytes 405512 | tf_op jit(solution)/shard_map/ppermute | solution.py:21
  143.8 3.9 %collective-permute-start.11 = (bf16[528,128]{1,0:T(8,128)(2,1)S(1)}, bf16[528,128]{1,0:T(8,128)(2,1)S(1)}, u32[]{:S(2)}, u32[]{:S(2)}) collective-permute-start(bf16[528,128]{1,0:T(8,128)(2,1)S(1)} %pad_maximum_fusion), channel_id=1, source_target_pairs={{0,64},{64,128},{128,192},{192,256},{256,320},{320,384},{384,448},... | collective-permute-start | bytes 405512 | tf_op jit(solution)/shard_map/ppermute | solution.py:21
  147.8 5.3 %collective-permute-done.11 = bf16[528,128]{1,0:T(8,128)(2,1)S(1)} collective-permute-done((bf16[528,128]{1,0:T(8,128)(2,1)S(1)}, bf16[528,128]{1,0:T(8,128)(2,1)S(1)}, u32[]{:S(2)}, u32[]{:S(2)}) %collective-permute-start.11) | collective-permute-done | bytes 135200 | tf_op jit(solution)/shard_map/ppermute | solution.py:21
  153.1 4.9 %collective-permute-start.12 = (bf16[528,128]{1,0:T(8,128)(2,1)S(1)}, bf16[528,128]{1,0:T(8,128)(2,1)S(1)}, u32[]{:S(2)}, u32[]{:S(2)}) collective-permute-start(bf16[528,128]{1,0:T(8,128)(2,1)S(1)} %pad_maximum_fusion.1), channel_id=1, source_target_pairs={{0,128},{64,192},{128,256},{192,320},{256,384},{320,448},{384,0},{... | collective-permute-start | bytes 405512 | tf_op jit(solution)/shard_map/ppermute | solution.py:21
  158.0 9.1 %collective-permute-done.12 = bf16[528,128]{1,0:T(8,128)(2,1)S(1)} collective-permute-done((bf16[528,128]{1,0:T(8,128)(2,1)S(1)}, bf16[528,128]{1,0:T(8,128)(2,1)S(1)}, u32[]{:S(2)}, u32[]{:S(2)}) %collective-permute-start.12) | collective-permute-done | bytes 135200 | tf_op jit(solution)/shard_map/ppermute | solution.py:21
  167.1 2.7 %collective-permute-start.13 = (bf16[528,128]{1,0:T(8,128)(2,1)S(1)}, bf16[528,128]{1,0:T(8,128)(2,1)S(1)}, u32[]{:S(2)}, u32[]{:S(2)}) collective-permute-start(bf16[528,128]{1,0:T(8,128)(2,1)S(1)} %pad_maximum_fusion.2), channel_id=1, source_target_pairs={{0,192},{64,256},{128,320},{192,384},{256,448},{320,0},{384,64},{4... | collective-permute-start | bytes 405512 | tf_op jit(solution)/shard_map/ppermute | solution.py:21
  169.9 11.8 %collective-permute-done.13 = bf16[528,128]{1,0:T(8,128)(2,1)S(1)} collective-permute-done((bf16[528,128]{1,0:T(8,128)(2,1)S(1)}, bf16[528,128]{1,0:T(8,128)(2,1)S(1)}, u32[]{:S(2)}, u32[]{:S(2)}) %collective-permute-start.13) | collective-permute-done | bytes 135200 | tf_op jit(solution)/shard_map/ppermute | solution.py:21
  183.7 10.3 %all-to-all-start = ((bf16[8,64,128]{2,1,0:T(8,128)(2,1)}), bf16[8,64,128]{2,1,0:T(8,128)(2,1)S(1)}, u32[]{:S(2)}, u32[]{:S(2)}) async-start(bf16[8,64,128]{2,1,0:T(8,128)(2,1)} %select_convert_fusion), calls=%async_computation | async-start | bytes 262144 | tf_op jit(solution)/shard_map/all_to_all | solution.py:343
  194.0 9.1 %all-to-all-done.refs_0_ = bf16[8,64,128]{2,1,0:T(8,128)(2,1)S(1)} async-done(((bf16[8,64,128]{2,1,0:T(8,128)(2,1)}), bf16[8,64,128]{2,1,0:T(8,128)(2,1)S(1)}, u32[]{:S(2)}, u32[]{:S(2)}) %all-to-all-start) | async-done | bytes 131104 | tf_op jit(solution)/shard_map/all_to_all | solution.py:343
  207.1 5.0 %collective-permute-start.20 = (bf16[8,64,128]{2,1,0:T(8,128)(2,1)S(1)}, bf16[8,64,128]{2,1,0:T(8,128)(2,1)S(1)}, u32[]{:S(2)}, u32[]{:S(2)}) collective-permute-start(bf16[8,64,128]{2,1,0:T(8,128)(2,1)S(1)} %all-to-all-done.refs_0_), channel_id=1, source_target_pairs={{0,16},{16,32},{32,48},{48,0},{1,17},{17,33},{33,49},{49,1},{2,18}... | collective-permute-start | bytes 393224 | tf_op jit(solution)/shard_map/ppermute | solution.py:21
  218.1 3.4 %shard_map.84 = bf16[8,256,256]{2,1,0:T(8,128)(2,1)S(1)} custom-call(s32[12]{0:T(128)S(1)} %pad_add_fusion.where_ref, bf16[8,64,128]{2,1,0:T(8,128)(2,1)S(1)} %all-to-all-done.refs_0_, bf16[8,64,128]{2,1,0:T(8,128)(2,1)S(1)} %collective-permute-done.18.refs_1_, bf16[8,64,128]{2,1,0:T(8,128)(2,1)S(1)} %collective-permute-done.19.refs_2_, ...), custom_call_target="tpu_custom_call" | custom-call | tf_op jit(solution)/shard_map/pallas_call | solution.py:233
  223.4 3.3 %collective-permute-start.22 = (bf16[256,256]{1,0:T(8,128)(2,1)S(1)}, bf16[256,256]{1,0:T(8,128)(2,1)S(1)}, u32[]{:S(2)}, u32[]{:S(2)}) collective-permute-start(bf16[256,256]{1,0:T(8,128)(2,1)S(1)} %get-tuple-element.38), channel_id=1, source_target_pairs={{0,128},{64,192},{128,256},{192,320},{256,384},{320,448},{384,0},{... | collective-permute-start | bytes 393224 | tf_op jit(solution)/shard_map/ppermute | solution.py:21
  226.8 6.0 %collective-permute-start.23 = (bf16[256,256]{1,0:T(8,128)(2,1)S(1)}, bf16[256,256]{1,0:T(8,128)(2,1)S(1)}, u32[]{:S(2)}, u32[]{:S(2)}) collective-permute-start(bf16[256,256]{1,0:T(8,128)(2,1)S(1)} %get-tuple-element.37), channel_id=1, source_target_pairs={{0,192},{64,256},{128,320},{192,384},{256,448},{320,0},{384,64},{4... | collective-permute-start | bytes 393224 | tf_op jit(solution)/shard_map/ppermute | solution.py:21
  232.8 2.9 %collective-permute-start.24 = (bf16[256,256]{1,0:T(8,128)(2,1)S(1)}, bf16[256,256]{1,0:T(8,128)(2,1)S(1)}, u32[]{:S(2)}, u32[]{:S(2)}) collective-permute-start(bf16[256,256]{1,0:T(8,128)(2,1)S(1)} %get-tuple-element.36), channel_id=1, source_target_pairs={{0,256},{64,320},{128,384},{192,448},{256,0},{320,64},{384,128},{4... | collective-permute-start | bytes 393224 | tf_op jit(solution)/shard_map/ppermute | solution.py:21
  235.7 5.4 %collective-permute-start.25 = (bf16[256,256]{1,0:T(8,128)(2,1)S(1)}, bf16[256,256]{1,0:T(8,128)(2,1)S(1)}, u32[]{:S(2)}, u32[]{:S(2)}) collective-permute-start(bf16[256,256]{1,0:T(8,128)(2,1)S(1)} %get-tuple-element.35), channel_id=1, source_target_pairs={{0,320},{64,384},{128,448},{192,0},{256,64},{320,128},{384,192},{4... | collective-permute-start | bytes 393224 | tf_op jit(solution)/shard_map/ppermute | solution.py:21
  241.1 3.0 %collective-permute-start.26 = (bf16[256,256]{1,0:T(8,128)(2,1)S(1)}, bf16[256,256]{1,0:T(8,128)(2,1)S(1)}, u32[]{:S(2)}, u32[]{:S(2)}) collective-permute-start(bf16[256,256]{1,0:T(8,128)(2,1)S(1)} %get-tuple-element.34), channel_id=1, source_target_pairs={{0,384},{64,448},{128,0},{192,64},{256,128},{320,192},{384,256},{4... | collective-permute-start | bytes 393224 | tf_op jit(solution)/shard_map/ppermute | solution.py:21
  244.2 3.4 %collective-permute-start.27 = (bf16[256,256]{1,0:T(8,128)(2,1)S(1)}, bf16[256,256]{1,0:T(8,128)(2,1)S(1)}, u32[]{:S(2)}, u32[]{:S(2)}) collective-permute-start(bf16[256,256]{1,0:T(8,128)(2,1)S(1)} %get-tuple-element.33), channel_id=1, source_target_pairs={{0,448},{64,0},{128,64},{192,128},{256,192},{320,256},{384,320},{4... | collective-permute-start | bytes 393224 | tf_op jit(solution)/shard_map/ppermute | solution.py:21
  250.4 6.0 %collective-permute-done.26 = bf16[256,256]{1,0:T(8,128)(2,1)S(1)} collective-permute-done((bf16[256,256]{1,0:T(8,128)(2,1)S(1)}, bf16[256,256]{1,0:T(8,128)(2,1)S(1)}, u32[]{:S(2)}, u32[]{:S(2)}) %collective-permute-start.26) | collective-permute-done | bytes 131104 | tf_op jit(solution)/shard_map/ppermute | solution.py:21
  (112 shorter events, 38.7 us)
Async XLA Ops:
  6.5 76.3 %all-gather.5.cloned.1.call-start = ((), (), s32[]{:S(2)}) async-start(), calls=%async_computation.2 | async-start | bytes 2359296 | tf_op jit(solution)/shard_map/all_gather | solution.py:286
  7.3 50.2 %all-to-all-start.1 = ((bf16[8,128,256]{2,1,0:T(8,128)(2,1)}), bf16[8,128,256]{2,1,0:T(8,128)(2,1)S(1)}, u32[]{:S(2)}, u32[]{:S(2)}) async-start(bf16[8,128,256]{2,1,0:T(8,128)(2,1)} %bitcast.116), calls=%async_computation.1 | async-start | bytes 1048576 | tf_op jit(solution)/shard_map/all_to_all | solution.py:288
  14.4 201.5 %all-gather.7.cloned.1.call-start = ((), (), s32[]{:S(2)}) async-start(), calls=%async_computation.3 | async-start | bytes 4718592 | tf_op jit(solution)/shard_map/all_gather | solution.py:289
  14.4 9.8 %collective-permute-start = (s32[16]{0:T(128)S(1)}, s32[16]{0:T(128)S(1)}, u32[]{:S(2)}, u32[]{:S(2)}) collective-permute-start(s32[16]{0:T(128)S(1)} %copy-done.4), channel_id=1, source_target_pairs={{0,48},{16,0},{32,16},{48,32},{1,49},{17,1},{33,17},{49,33},{2,50}... | collective-permute-start | bytes 200 | tf_op jit(solution)/shard_map/ppermute | solution.py:21
  17.2 7.1 %collective-permute-start.1 = (s32[16]{0:T(128)S(1)}, s32[16]{0:T(128)S(1)}, u32[]{:S(2)}, u32[]{:S(2)}) collective-permute-start(s32[16]{0:T(128)S(1)} %copy-done.4), channel_id=1, source_target_pairs={{0,32},{16,48},{32,0},{48,16},{1,33},{17,49},{33,1},{49,17},{2,34}... | collective-permute-start | bytes 200 | tf_op jit(solution)/shard_map/ppermute | solution.py:21
  22.0 5.4 %collective-permute-start.2 = (s32[16]{0:T(128)S(1)}, s32[16]{0:T(128)S(1)}, u32[]{:S(2)}, u32[]{:S(2)}) collective-permute-start(s32[16]{0:T(128)S(1)} %copy-done.4), channel_id=1, source_target_pairs={{0,16},{16,32},{32,48},{48,0},{1,17},{17,33},{33,49},{49,1},{2,18}... | collective-permute-start | bytes 200 | tf_op jit(solution)/shard_map/ppermute | solution.py:21
  27.4 31.3 %collective-permute-start.3 = (bf16[16,256,128]{2,1,0:T(8,128)(2,1)S(1)}, bf16[16,256,128]{2,1,0:T(8,128)(2,1)}, u32[]{:S(2)}, u32[]{:S(2)}) collective-permute-start(bf16[16,256,128]{2,1,0:T(8,128)(2,1)S(1)} %copy-done.1), channel_id=1, source_target_pairs={{0,16},{16,32},{32,48},{48,0},{1,17},{17,33},{33,49},{49,1},{2,18}... | collective-permute-start | bytes 3145736 | tf_op jit(solution)/shard_map/ppermute | solution.py:21
  30.9 31.4 %collective-permute-start.5 = (bf16[16,256,128]{2,1,0:T(8,128)(2,1)}, bf16[16,256,128]{2,1,0:T(8,128)(2,1)}, u32[]{:S(2)}, u32[]{:S(2)}) collective-permute-start(bf16[16,256,128]{2,1,0:T(8,128)(2,1)} %refs_3_), channel_id=1, source_target_pairs={{0,48},{16,0},{32,16},{48,32},{1,49},{17,1},{33,17},{49,33},{2,50}... | collective-permute-start | bytes 3145736 | tf_op jit(solution)/shard_map/ppermute | solution.py:21
  50.4 32.5 %collective-permute-start.7 = (bf16[16,256,128]{2,1,0:T(8,128)(2,1)S(1)}, bf16[16,256,128]{2,1,0:T(8,128)(2,1)}, u32[]{:S(2)}, u32[]{:S(2)}) collective-permute-start(bf16[16,256,128]{2,1,0:T(8,128)(2,1)S(1)} %copy-done.1), channel_id=1, source_target_pairs={{0,48},{16,0},{32,16},{48,32},{1,49},{17,1},{33,17},{49,33},{2,50}... | collective-permute-start | bytes 3145736 | tf_op jit(solution)/shard_map/ppermute | solution.py:21
  52.8 30.1 %collective-permute-start.8 = (bf16[16,256,128]{2,1,0:T(8,128)(2,1)}, bf16[16,256,128]{2,1,0:T(8,128)(2,1)}, u32[]{:S(2)}, u32[]{:S(2)}) collective-permute-start(bf16[16,256,128]{2,1,0:T(8,128)(2,1)} %refs_3_), channel_id=1, source_target_pairs={{0,16},{16,32},{32,48},{48,0},{1,17},{17,33},{33,49},{49,1},{2,18}... | collective-permute-start | bytes 3145736 | tf_op jit(solution)/shard_map/ppermute | solution.py:21
  58.7 43.5 %collective-permute-start.4 = (bf16[16,256,128]{2,1,0:T(8,128)(2,1)}, bf16[16,256,128]{2,1,0:T(8,128)(2,1)S(1)}, u32[]{:S(2)}, u32[]{:S(2)}) collective-permute-start(bf16[16,256,128]{2,1,0:T(8,128)(2,1)} %collective-permute-done.3.refs_2_), channel_id=1, source_target_pairs={{0,16},{16,32},{32,48},{48,0},{1,17},{17,33},{33,49},{49,1},{2,18}... | collective-permute-start | bytes 3145736 | tf_op jit(solution)/shard_map/ppermute | solution.py:21
  62.2 40.0 %collective-permute-start.6 = (bf16[16,256,128]{2,1,0:T(8,128)(2,1)}, bf16[16,256,128]{2,1,0:T(8,128)(2,1)S(1)}, u32[]{:S(2)}, u32[]{:S(2)}) collective-permute-start(bf16[16,256,128]{2,1,0:T(8,128)(2,1)} %collective-permute-done.5.refs_4_), channel_id=1, source_target_pairs={{0,48},{16,0},{32,16},{48,32},{1,49},{17,1},{33,17},{49,33},{2,50}... | collective-permute-start | bytes 3145736 | tf_op jit(solution)/shard_map/ppermute | solution.py:21
  117.9 5.6 %collective-permute-start.9 = (bf16[8,8,64,128]{3,2,1,0:T(8,128)(2,1)S(1)}, bf16[8,8,64,128]{3,2,1,0:T(8,128)(2,1)S(1)}, u32[]{:S(2)}, u32[]{:S(2)}) collective-permute-start(bf16[8,8,64,128]{3,2,1,0:T(8,128)(2,1)S(1)} %get-tuple-element.31), channel_id=1, source_target_pairs={{0,8},{8,0},{1,9},{9,1},{2,10},{10,2},{3,11},{11,3},{4,12},{12,4},... | collective-permute-start | bytes 3145736 | tf_op jit(solution)/shard_map/ppermute | solution.py:323
  120.0 3.3 %collective-permute-start.10 = (f32[8,8,64]{2,1,0:T(8,128)S(1)}, f32[8,8,64]{2,1,0:T(8,128)S(1)}, u32[]{:S(2)}, u32[]{:S(2)}) collective-permute-start(f32[8,8,64]{2,1,0:T(8,128)S(1)} %bitcast.123), channel_id=1, source_target_pairs={{0,8},{8,0},{1,9},{9,1},{2,10},{10,2},{3,11},{11,3},{4,12},{12,4},... | collective-permute-start | bytes 49160 | tf_op jit(solution)/shard_map/ppermute | solution.py:324
  124.8 56.9 %collective-permute-start.17 = (bf16[528,128]{1,0:T(8,128)(2,1)S(1)}, bf16[528,128]{1,0:T(8,128)(2,1)S(1)}, u32[]{:S(2)}, u32[]{:S(2)}) collective-permute-start(bf16[528,128]{1,0:T(8,128)(2,1)S(1)} %pad_maximum_fusion.6), channel_id=1, source_target_pairs={{0,448},{64,0},{128,64},{192,128},{256,192},{320,256},{384,320},{4... | collective-permute-start | bytes 405512 | tf_op jit(solution)/shard_map/ppermute | solution.py:21
  126.8 54.9 %collective-permute-start.16 = (bf16[528,128]{1,0:T(8,128)(2,1)S(1)}, bf16[528,128]{1,0:T(8,128)(2,1)S(1)}, u32[]{:S(2)}, u32[]{:S(2)}) collective-permute-start(bf16[528,128]{1,0:T(8,128)(2,1)S(1)} %pad_maximum_fusion.5), channel_id=1, source_target_pairs={{0,384},{64,448},{128,0},{192,64},{256,128},{320,192},{384,256},{4... | collective-permute-start | bytes 405512 | tf_op jit(solution)/shard_map/ppermute | solution.py:21
  135.8 45.9 %collective-permute-start.15 = (bf16[528,128]{1,0:T(8,128)(2,1)S(1)}, bf16[528,128]{1,0:T(8,128)(2,1)S(1)}, u32[]{:S(2)}, u32[]{:S(2)}) collective-permute-start(bf16[528,128]{1,0:T(8,128)(2,1)S(1)} %pad_maximum_fusion.4), channel_id=1, source_target_pairs={{0,320},{64,384},{128,448},{192,0},{256,64},{320,128},{384,192},{4... | collective-permute-start | bytes 405512 | tf_op jit(solution)/shard_map/ppermute | solution.py:21
  141.9 39.8 %collective-permute-start.14 = (bf16[528,128]{1,0:T(8,128)(2,1)S(1)}, bf16[528,128]{1,0:T(8,128)(2,1)S(1)}, u32[]{:S(2)}, u32[]{:S(2)}) collective-permute-start(bf16[528,128]{1,0:T(8,128)(2,1)S(1)} %pad_maximum_fusion.3), channel_id=1, source_target_pairs={{0,256},{64,320},{128,384},{192,448},{256,0},{320,64},{384,128},{4... | collective-permute-start | bytes 405512 | tf_op jit(solution)/shard_map/ppermute | solution.py:21
  143.8 9.3 %collective-permute-start.11 = (bf16[528,128]{1,0:T(8,128)(2,1)S(1)}, bf16[528,128]{1,0:T(8,128)(2,1)S(1)}, u32[]{:S(2)}, u32[]{:S(2)}) collective-permute-start(bf16[528,128]{1,0:T(8,128)(2,1)S(1)} %pad_maximum_fusion), channel_id=1, source_target_pairs={{0,64},{64,128},{128,192},{192,256},{256,320},{320,384},{384,448},... | collective-permute-start | bytes 405512 | tf_op jit(solution)/shard_map/ppermute | solution.py:21
  153.1 14.0 %collective-permute-start.12 = (bf16[528,128]{1,0:T(8,128)(2,1)S(1)}, bf16[528,128]{1,0:T(8,128)(2,1)S(1)}, u32[]{:S(2)}, u32[]{:S(2)}) collective-permute-start(bf16[528,128]{1,0:T(8,128)(2,1)S(1)} %pad_maximum_fusion.1), channel_id=1, source_target_pairs={{0,128},{64,192},{128,256},{192,320},{256,384},{320,448},{384,0},{... | collective-permute-start | bytes 405512 | tf_op jit(solution)/shard_map/ppermute | solution.py:21
  167.1 14.5 %collective-permute-start.13 = (bf16[528,128]{1,0:T(8,128)(2,1)S(1)}, bf16[528,128]{1,0:T(8,128)(2,1)S(1)}, u32[]{:S(2)}, u32[]{:S(2)}) collective-permute-start(bf16[528,128]{1,0:T(8,128)(2,1)S(1)} %pad_maximum_fusion.2), channel_id=1, source_target_pairs={{0,192},{64,256},{128,320},{192,384},{256,448},{320,0},{384,64},{4... | collective-permute-start | bytes 405512 | tf_op jit(solution)/shard_map/ppermute | solution.py:21
  183.7 19.4 %all-to-all-start = ((bf16[8,64,128]{2,1,0:T(8,128)(2,1)}), bf16[8,64,128]{2,1,0:T(8,128)(2,1)S(1)}, u32[]{:S(2)}, u32[]{:S(2)}) async-start(bf16[8,64,128]{2,1,0:T(8,128)(2,1)} %select_convert_fusion), calls=%async_computation | async-start | bytes 262144 | tf_op jit(solution)/shard_map/all_to_all | solution.py:343
  203.1 9.1 %collective-permute-start.18 = (bf16[8,64,128]{2,1,0:T(8,128)(2,1)S(1)}, bf16[8,64,128]{2,1,0:T(8,128)(2,1)S(1)}, u32[]{:S(2)}, u32[]{:S(2)}) collective-permute-start(bf16[8,64,128]{2,1,0:T(8,128)(2,1)S(1)} %all-to-all-done.refs_0_), channel_id=1, source_target_pairs={{0,48},{16,0},{32,16},{48,32},{1,49},{17,1},{33,17},{49,33},{2,50}... | collective-permute-start | bytes 393224 | tf_op jit(solution)/shard_map/ppermute | solution.py:21
  205.1 8.4 %collective-permute-start.19 = (bf16[8,64,128]{2,1,0:T(8,128)(2,1)S(1)}, bf16[8,64,128]{2,1,0:T(8,128)(2,1)S(1)}, u32[]{:S(2)}, u32[]{:S(2)}) collective-permute-start(bf16[8,64,128]{2,1,0:T(8,128)(2,1)S(1)} %all-to-all-done.refs_0_), channel_id=1, source_target_pairs={{0,32},{16,48},{32,0},{48,16},{1,33},{17,49},{33,1},{49,17},{2,34}... | collective-permute-start | bytes 393224 | tf_op jit(solution)/shard_map/ppermute | solution.py:21
  207.1 8.8 %collective-permute-start.20 = (bf16[8,64,128]{2,1,0:T(8,128)(2,1)S(1)}, bf16[8,64,128]{2,1,0:T(8,128)(2,1)S(1)}, u32[]{:S(2)}, u32[]{:S(2)}) collective-permute-start(bf16[8,64,128]{2,1,0:T(8,128)(2,1)S(1)} %all-to-all-done.refs_0_), channel_id=1, source_target_pairs={{0,16},{16,32},{32,48},{48,0},{1,17},{17,33},{33,49},{49,1},{2,18}... | collective-permute-start | bytes 393224 | tf_op jit(solution)/shard_map/ppermute | solution.py:21
  221.5 19.6 %collective-permute-start.21 = (bf16[256,256]{1,0:T(8,128)(2,1)S(1)}, bf16[256,256]{1,0:T(8,128)(2,1)S(1)}, u32[]{:S(2)}, u32[]{:S(2)}) collective-permute-start(bf16[256,256]{1,0:T(8,128)(2,1)S(1)} %get-tuple-element.32), channel_id=1, source_target_pairs={{0,64},{64,128},{128,192},{192,256},{256,320},{320,384},{384,448},... | collective-permute-start | bytes 393224 | tf_op jit(solution)/shard_map/ppermute | solution.py:21
  223.4 20.7 %collective-permute-start.22 = (bf16[256,256]{1,0:T(8,128)(2,1)S(1)}, bf16[256,256]{1,0:T(8,128)(2,1)S(1)}, u32[]{:S(2)}, u32[]{:S(2)}) collective-permute-start(bf16[256,256]{1,0:T(8,128)(2,1)S(1)} %get-tuple-element.38), channel_id=1, source_target_pairs={{0,128},{64,192},{128,256},{192,320},{256,384},{320,448},{384,0},{... | collective-permute-start | bytes 393224 | tf_op jit(solution)/shard_map/ppermute | solution.py:21
  226.8 22.0 %collective-permute-start.23 = (bf16[256,256]{1,0:T(8,128)(2,1)S(1)}, bf16[256,256]{1,0:T(8,128)(2,1)S(1)}, u32[]{:S(2)}, u32[]{:S(2)}) collective-permute-start(bf16[256,256]{1,0:T(8,128)(2,1)S(1)} %get-tuple-element.37), channel_id=1, source_target_pairs={{0,192},{64,256},{128,320},{192,384},{256,448},{320,0},{384,64},{4... | collective-permute-start | bytes 393224 | tf_op jit(solution)/shard_map/ppermute | solution.py:21
  232.8 15.9 %collective-permute-start.24 = (bf16[256,256]{1,0:T(8,128)(2,1)S(1)}, bf16[256,256]{1,0:T(8,128)(2,1)S(1)}, u32[]{:S(2)}, u32[]{:S(2)}) collective-permute-start(bf16[256,256]{1,0:T(8,128)(2,1)S(1)} %get-tuple-element.36), channel_id=1, source_target_pairs={{0,256},{64,320},{128,384},{192,448},{256,0},{320,64},{384,128},{4... | collective-permute-start | bytes 393224 | tf_op jit(solution)/shard_map/ppermute | solution.py:21
  235.7 14.7 %collective-permute-start.25 = (bf16[256,256]{1,0:T(8,128)(2,1)S(1)}, bf16[256,256]{1,0:T(8,128)(2,1)S(1)}, u32[]{:S(2)}, u32[]{:S(2)}) collective-permute-start(bf16[256,256]{1,0:T(8,128)(2,1)S(1)} %get-tuple-element.35), channel_id=1, source_target_pairs={{0,320},{64,384},{128,448},{192,0},{256,64},{320,128},{384,192},{4... | collective-permute-start | bytes 393224 | tf_op jit(solution)/shard_map/ppermute | solution.py:21
  241.1 15.3 %collective-permute-start.26 = (bf16[256,256]{1,0:T(8,128)(2,1)S(1)}, bf16[256,256]{1,0:T(8,128)(2,1)S(1)}, u32[]{:S(2)}, u32[]{:S(2)}) collective-permute-start(bf16[256,256]{1,0:T(8,128)(2,1)S(1)} %get-tuple-element.34), channel_id=1, source_target_pairs={{0,384},{64,448},{128,0},{192,64},{256,128},{320,192},{384,256},{4... | collective-permute-start | bytes 393224 | tf_op jit(solution)/shard_map/ppermute | solution.py:21
  244.2 13.6 %collective-permute-start.27 = (bf16[256,256]{1,0:T(8,128)(2,1)S(1)}, bf16[256,256]{1,0:T(8,128)(2,1)S(1)}, u32[]{:S(2)}, u32[]{:S(2)}) collective-permute-start(bf16[256,256]{1,0:T(8,128)(2,1)S(1)} %get-tuple-element.33), channel_id=1, source_target_pairs={{0,448},{64,0},{128,64},{192,128},{256,192},{320,256},{384,320},{4... | collective-permute-start | bytes 393224 | tf_op jit(solution)/shard_map/ppermute | solution.py:21
  (7 other events, 87.8 us)
Sparse Core Ops, SparseCore 0:
  9.5 47.9 all-gather.4
  59.5 58.5 all-gather.6

commit v4 on v3

v4 whole, which is shorter than its diff:
```python
import functools

import jax
import jax.numpy as jnp
from jax import lax
from jax.experimental import pallas as pl
from jax.experimental.pallas import tpu as pltpu
from jax.sharding import Mesh
from jax.sharding import PartitionSpec as P

ROW, COL = "lib_0", "lib_1"
LIB = (ROW, COL)
theta_base = 500000.0
EMPTY = -1e30
CHUNK = 256
MOST = 2


def shift(value, axis, by):
    n = lax.axis_size(axis)
    return lax.ppermute(value, axis, [(i, (i + by) % n) for i in range(n)])


def far_first(n):
    return sorted(range(1, n), key=lambda d: -min(d, n - d))


def coded(integers):
    return (integers // 128).astype(jnp.bfloat16), (integers % 128).astype(jnp.bfloat16)


def decoded(high, low):
    return high.astype(jnp.int32) * 128 + low.astype(jnp.int32)


def gather_pieces(value, axis):
    n = lax.axis_size(axis)
    pieces = [value] * n
    for d in far_first(n):
        pieces[d] = shift(value, axis, -d)
    return pieces


def attend_kernel(scale, pieces, first, last, slot_ref, q_ref, cos_ref, sin_ref, *refs):
    key_refs, value_refs, refs = refs[:pieces], refs[pieces : 2 * pieces], refs[2 * pieces :]
    if not first:
        (before_ref, before_lse_ref), refs = refs[:2], refs[2:]
    out_ref, lse_ref, q_scr, tile, k_scr, v_scr, s_scr, m_scr, acc_scr, used, entry = refs
    prompt = pl.program_id(0)
    listed, width = cos_ref.shape[1:]
    rows = q_ref.shape[1]
    group = q_ref.shape[2] // width
    total_rows = rows * group
    tokens = tile.shape[0]
    held = key_refs[0].shape[0] // tokens
    factor = scale * 1.4426950408889634
    chunks = [slice(r, r + CHUNK) for r in range(0, total_rows, CHUNK)]

    @pl.when(prompt == 0)
    def _():
        v_scr[:, width:] = jnp.ones((2 * tokens, width), v_scr.dtype)

    for g in range(group):
        q_scr[g * rows : (g + 1) * rows] = q_ref[0, :, g * width : (g + 1) * width]
    for span in chunks:
        if first:
            m_scr[span] = jnp.full((CHUNK, width), EMPTY, jnp.float32)
        else:
            m_scr[span] = before_lse_ref[0, span] * (1.0 / scale)

    def note(k, count):
        slot = slot_ref[prompt * listed + k]
        used[count] = slot
        entry[count] = k
        return count + jnp.where(slot >= 0, 1, 0)

    count = lax.fori_loop(0, listed, note, 0)
    pairs = (count + 1) // 2

    def fetch(refs, slot):
        def at(index):
            return pl.ds(pl.multiple_of(index * tokens, tokens), tokens)

        if pieces == 1:
            return refs[0][at(slot)]
        for d in range(pieces):

            @pl.when(slot // held == d)
            def _():
                tile[...] = refs[d][at(slot % held)]

        return tile[...]

    def score(t, carry):
        for b in range(2):
            i = jnp.minimum(2 * t + b, count - 1)
            keys = fetch(key_refs, used[i]).astype(jnp.float32)
            cosine = cos_ref[0, pl.ds(entry[i], 1), :]
            sine = sin_ref[0, pl.ds(entry[i], 1), :]
            turned = keys * cosine + pltpu.roll(keys, width // 2, 1) * sine
            k_scr[b * tokens : (b + 1) * tokens] = turned.astype(jnp.bfloat16)
        both = 2 * t + 1 < count
        for span in chunks:
            s = lax.dot_general(
                q_scr[span],
                k_scr[...],
                (((1,), (1,)), ((), ())),
                preferred_element_type=jnp.float32,
            )
            highest = m_scr[span]
            for u in range(0, 2 * tokens, width):
                part = s[:, u : u + width]
                if u >= tokens:
                    part = jnp.where(both, part, EMPTY)
                s_scr[t, span, u : u + width] = part
                highest = jnp.maximum(highest, part)
            m_scr[span] = highest
        return carry

    lax.fori_loop(0, pairs, score, 0)
    for span in chunks:
        m = jnp.broadcast_to(jnp.max(m_scr[span], axis=1, keepdims=True), (CHUNK, width))
        m_scr[span] = m
        if first:
            acc_scr[span] = jnp.zeros((CHUNK, 2 * width), jnp.float32)
        else:
            weight = jnp.exp2((before_lse_ref[0, span] * (1.0 / scale) - m) * factor)
            acc_scr[span, :width] = before_ref[0, span] * weight
            acc_scr[span, width:] = weight

    def weigh(t, carry):
        for b in range(2):
            i = jnp.minimum(2 * t + b, count - 1)
            v_scr[b * tokens : (b + 1) * tokens, :width] = fetch(value_refs, used[i])
        for span in chunks:
            m = m_scr[span]
            parts = [
                jnp.exp2((s_scr[t, span, u : u + width] - m) * factor)
                for u in range(0, 2 * tokens, width)
            ]
            weights = jnp.concatenate([p.astype(jnp.bfloat16) for p in parts], axis=1)
            acc_scr[span] += jnp.dot(weights, v_scr[...], preferred_element_type=jnp.float32)
        return carry

    lax.fori_loop(0, pairs, weigh, 0)
    row = lax.broadcasted_iota(jnp.int32, (rows, rows), 0)
    column = lax.broadcasted_iota(jnp.int32, (rows, rows), 1)
    for g in range(group):
        span = slice(g * rows, (g + 1) * rows)
        total = acc_scr[span, width:]
        if first:
            total = jnp.where(count == 0, 1.0, total)
        out = acc_scr[span, :width] / total
        lse = m_scr[span] * scale + jnp.log(total)
        if last:
            halves = out_ref.shape[0]
            part = rows // halves
            for c in range(halves):
                out_ref[c, g, 0] = out[c * part : (c + 1) * part].astype(out_ref.dtype)
            lse_ref[0, g : g + 1, :] = jnp.sum(
                jnp.where(row == column, lse, 0.0), axis=0, keepdims=True
            )
        else:
            out_ref[0, span] = out
            lse_ref[0, span] = lse


def attend(slots, query, cosine, sine, keys, values, before, halves, rows, tokens):
    prompts, _, features = query.shape
    listed, width = cosine.shape[1:]
    group = features // width
    most = MOST * len(keys)
    whole = pl.BlockSpec(memory_space=pltpu.VMEM)
    table = pl.BlockSpec((1, listed, width), lambda j, s: (j, 0, 0))
    state = pl.BlockSpec((1, rows * group, width), lambda j, s: (j, 0, 0))
    if halves:
        part = rows // halves
        out = (
            jax.ShapeDtypeStruct((halves, group, prompts, part, width), jnp.bfloat16),
            jax.ShapeDtypeStruct((prompts, group, rows), jnp.float32),
        )
        out_specs = (
            pl.BlockSpec((halves, group, 1, part, width), lambda j, s: (0, 0, j, 0, 0)),
            pl.BlockSpec((1, group, rows), lambda j, s: (j, 0, 0)),
        )
    else:
        out = (jax.ShapeDtypeStruct((prompts, rows * group, width), jnp.float32),) * 2
        out_specs = (state, state)
    work = prompts * most // 2 * rows * group * tokens
    return pl.pallas_call(
        functools.partial(attend_kernel, width**-0.5, len(keys), before is None, bool(halves)),
        out_shape=out,
        grid_spec=pltpu.PrefetchScalarGridSpec(
            num_scalar_prefetch=1,
            grid=(prompts,),
            in_specs=[pl.BlockSpec((1, rows, features), lambda j, s: (j, 0, 0)), table, table]
            + [whole] * (2 * len(keys))
            + ([state, state] if before else []),
            out_specs=out_specs,
            scratch_shapes=[
                pltpu.VMEM((rows * group, width), jnp.bfloat16),
                pltpu.VMEM((tokens, width), jnp.bfloat16),
                pltpu.VMEM((2 * tokens, width), jnp.bfloat16),
                pltpu.VMEM((2 * tokens, 2 * width), jnp.bfloat16),
                pltpu.VMEM((most // 2, rows * group, 2 * tokens), jnp.float32),
                pltpu.VMEM((rows * group, width), jnp.float32),
                pltpu.VMEM((rows * group, 2 * width), jnp.float32),
                pltpu.SMEM((most + 1,), jnp.int32),
                pltpu.SMEM((most + 1,), jnp.int32),
            ],
        ),
        cost_estimate=pl.CostEstimate(
            flops=4 * work * width, bytes_accessed=8 * work, transcendentals=work
        ),
        compiler_params=pltpu.CompilerParams(vmem_limit_bytes=48 * 1024 * 1024),
    )(slots, query, cosine, sine, *keys, *values, *(before or ()))


def project_kernel(columns, where_ref, *refs):
    pieces, weight_ref, out_ref = refs[:columns], refs[columns], refs[columns + 1]
    heads, rows = pieces[0].shape[:2]
    left = jnp.concatenate(
        [jnp.concatenate([p[h] for h in range(heads)], axis=1) for p in pieces], axis=0
    )
    right = jnp.concatenate([weight_ref[h, 0] for h in range(heads)], axis=0)
    term = jnp.dot(left, right, preferred_element_type=jnp.float32).astype(out_ref.dtype)
    for d in range(columns):
        at = pl.multiple_of(where_ref[d] * rows, rows)
        out_ref[0, pl.ds(at, rows), :] = term[d * rows : (d + 1) * rows]


def project(where, pieces, weight):
    columns = len(pieces)
    heads, rows, width = pieces[0].shape
    owners, out_columns = weight.shape[1], weight.shape[3]
    return pl.pallas_call(
        functools.partial(project_kernel, columns),
        out_shape=jax.ShapeDtypeStruct((owners, columns * rows, out_columns), jnp.bfloat16),
        grid_spec=pltpu.PrefetchScalarGridSpec(
            num_scalar_prefetch=1,
            grid=(owners,),
            in_specs=[pl.BlockSpec((heads, rows, width), lambda s, w: (0, 0, 0))] * columns
            + [pl.BlockSpec((heads, 1, width, out_columns), lambda s, w: (0, s, 0, 0))],
            out_specs=pl.BlockSpec((1, columns * rows, out_columns), lambda s, w: (s, 0, 0)),
        ),
        compiler_params=pltpu.CompilerParams(vmem_limit_bytes=32 * 1024 * 1024),
    )(where, *pieces, weight)


def merged(outs, lses):
    top = jnp.max(lses, axis=0)
    share = jnp.exp(lses - top)
    total = jnp.sum(share, axis=0)
    share = share / total
    out = jnp.sum(outs.astype(jnp.float32) * share[..., None], axis=0)
    return out, top + jnp.log(total)


def three_parts(value):
    first = lax.reduce_precision(value, 8, 7)
    rest = value - first
    second = lax.reduce_precision(rest, 8, 7)
    return jnp.stack([first, second, rest - second]).astype(jnp.bfloat16)


def turns(delta, width):
    half = width // 2
    inverse = theta_base ** (-2.0 * jnp.arange(half, dtype=jnp.float32) / width)
    angle = delta.astype(jnp.float32)[..., None] * inverse
    cosine, sine = jnp.cos(angle), jnp.sin(angle)
    return jnp.concatenate([cosine, cosine], axis=-1), jnp.concatenate([-sine, sine], axis=-1)


def body(
    queries, passage_keys, passage_values, offsets, out_weight, passage_list, targets, row_counts
):
    rows_of, columns = lax.axis_size(ROW), lax.axis_size(COL)
    y, x, c = lax.axis_index(ROW), lax.axis_index(COL), lax.axis_index("ctx")
    z = lax.axis_index("head")
    held, tokens, width = passage_keys.shape
    listed = passage_list.shape[1]
    prompt_rows, features = queries.shape[1:]
    group = features // width
    halves = lax.axis_size("ctx")
    half_rows = prompt_rows // halves

    behind = jnp.pad(jnp.stack(coded(offsets)), ((0, 14), (0, width - held)))
    own_keys = jnp.concatenate([passage_keys.reshape(-1, width), behind], axis=0)
    own_values = passage_values.reshape(-1, width)
    keys = [own_keys, shift(own_keys, COL, -1), None, shift(own_keys, COL, 1)]
    values = [own_values, shift(own_values, COL, -1), None, shift(own_values, COL, 1)]
    keys[2] = shift(keys[3], COL, 1)
    values[2] = shift(values[1], COL, -1)

    asked = jnp.concatenate([passage_list[0], targets[0], row_counts])
    asked = jnp.stack(coded(asked))
    asked = jnp.pad(asked, ((0, 14), (0, features - asked.shape[1])))
    query = jnp.concatenate([queries, asked[None]], axis=1)
    query = lax.all_gather(query, ROW, axis=0, tiled=True)
    asked = decoded(query[:, prompt_rows], query[:, prompt_rows + 1])
    weight = out_weight.reshape(group, width, -1)
    weight = lax.all_to_all(weight, ROW, split_axis=0, concat_axis=0, tiled=True)
    weight = lax.all_gather(weight[None], "head", axis=0, tiled=True)

    local = asked[:, :listed] - y * columns * held
    mine = (local >= 0) & (local < columns * held)
    ahead = (local // held - x) % columns
    within = local % held

    def tables(order, pieces):
        slots = jnp.full_like(within, -1)
        for at, d in enumerate(order):
            slots = jnp.where(mine & (ahead == d), at * held + within, slots)
        tails = jnp.stack([p[held * tokens : held * tokens + 2, :held] for p in pieces])
        near = decoded(tails[:, 0], tails[:, 1]).reshape(-1)
        same = slots[..., None] == jnp.arange(len(order) * held, dtype=jnp.int32)
        moved = asked[:, listed : 2 * listed] - jnp.sum(jnp.where(same, near, 0), axis=-1)
        return (slots.reshape(-1), *turns(moved, width))

    before = None
    for order, laid_out in (((0, 1, 3), 0), ((2,), halves)):
        pieces = [keys[d] for d in order]
        if before is not None:
            before, pieces = lax.optimization_barrier((before, pieces))
        slots, cosine, sine = tables(order, pieces)
        before = attend(
            slots, query, cosine, sine, pieces, [values[d] for d in order], before, laid_out,
            prompt_rows, tokens,
        )
    out, lse = before

    lse = jnp.transpose(lse.reshape(rows_of, group, halves, half_rows), (2, 1, 0, 3))
    swap = [(i, 1 - i) for i in range(2)]
    pick = functools.partial(lax.dynamic_index_in_dim, axis=0, keepdims=False)
    other = lax.ppermute(pick(out, 1 - c), "ctx", swap)
    other_lse = lax.ppermute(pick(lse, 1 - c), "ctx", swap)
    out, lse = merged(
        jnp.stack([pick(out, c), other]), jnp.stack([pick(lse, c), other_lse])
    )

    out = out.astype(jnp.bfloat16).reshape(group * rows_of, half_rows, width)
    parts = jnp.moveaxis(three_parts(lse.reshape(group * rows_of, half_rows)), 0, 1)
    parts = jnp.pad(parts, ((0, 0), (0, 5), (0, width - half_rows)))
    sent = jnp.concatenate([out, parts], axis=1)
    got = lax.all_to_all(sent, (ROW, "head"), split_axis=0, concat_axis=0, tiled=True)
    got = got.reshape(rows_of, -1, half_rows + 8, width)
    lses = got[:, :, half_rows : half_rows + 3, :half_rows].astype(jnp.float32)
    attended, _ = merged(got[:, :, :half_rows], jnp.sum(lses, axis=2))
    count = lax.dynamic_index_in_dim(asked[:, 2 * listed], z, keepdims=False)
    live = c * half_rows + jnp.arange(half_rows, dtype=jnp.int32) < count
    attended = jnp.where(live[:, None], attended, 0.0).astype(jnp.bfloat16)

    where = (x + jnp.arange(columns, dtype=jnp.int32)) % columns
    terms = project(where, gather_pieces(attended, COL), weight)
    terms = lax.all_to_all(terms, ROW, split_axis=0, concat_axis=0, tiled=True)
    total = jnp.sum(terms.astype(jnp.float32), axis=0)
    return total.astype(jnp.bfloat16)[None]


def solution(mesh):
    finer = Mesh(
        mesh.devices.reshape(8, 4, mesh.shape["ctx"], mesh.shape["head"]),
        ("lib_0", "lib_1", "ctx", "head"),
    )
    return jax.shard_map(
        body,
        mesh=finer,
        in_specs=(
            P(LIB, None, "head"),
            P(LIB, "ctx", "head"),
            P(LIB, "ctx", "head"),
            P(LIB),
            P("head", LIB),
            P(LIB, None),
            P(LIB, None),
            P(LIB),
        ),
        out_specs=P("ctx", "head", LIB),
        check_vma=False,
    )
```

time: 268 us -> 231 us (0.86)
  starting transfers between devices: 116 us -> 57.6 us
  blocking collectives: 16.3 us -> 33.3 us
  other arithmetic: 4.9 us -> 11.3 us
  Pallas kernels: 36.9 us -> 33.5 us
    ppermute x26 -> x9, starting transfers between devices: 93.8 us -> 34.1 us  [shift(): return lax.ppermute(value, axis, [(i, (i + by) % n) for i in range(n)])]
    ppermute x26 -> x9, waiting for transfers between devices: 60.7 us -> 24.6 us  [shift(): return lax.ppermute(value, axis, [(i, (i + by) % n) for i in range(n)])]
    all_to_all x0 -> x1, blocking collectives: none -> 33.3 us  [body(): terms = lax.all_to_all(terms, ROW, split_axis=0, concat_axis=0, tiled=True)]
    all_to_all x1, waiting for transfers between devices: 9.07 us -> 30.9 us  [body(): lax.all_to_all(sent, (ROW, 'head'), split_axis=0, concat_axis=0, tiled=True)]
    all_gather x1 -> x0, blocking collectives: 16.3 us -> none  [body(): asked = lax.all_gather(asked, ROW, axis=0, tiled=True)]
    all_to_all x1, waiting for transfers between devices: 0.01 us -> 14.3 us  [body(): lax.all_to_all(weight, ROW, split_axis=0, concat_axis=0, tiled=True)]
    all_to_all x1, starting transfers between devices: 10.3 us -> 15.6 us  [body(): lax.all_to_all(sent, (ROW, 'head'), split_axis=0, concat_axis=0, tiled=True)]
    concatenate x10 -> x6, other arithmetic: 0.34 us -> 4.39 us  [the longest x1 1.7 us: body(): query = jnp.concatenate([queries, asked[None]], axis=1)]
  transfers between devices with their start and end apart: 32 -> 15, of which waited for: 13 -> 7; matrix products, arithmetic and copies ran while one was open for 2% -> 5% of each run, Pallas kernels for 13% -> 13%
where the time goes in v4:
time: 231 us; the launch traced here: 230 us
  waiting for transfers between devices  71.9 us (31%)
  starting transfers between devices  57.6 us (25%)
  Pallas kernels  33.5 us (15%)
  blocking collectives  33.3 us (14%)
  between operations  14.5 us (6%)
  other arithmetic  11.3 us (5%)
  local copies, waits for them, and re-layouts  8.16 us (4%)
    ppermute x9, starting transfers between devices, shift(): return lax.ppermute(value, axis, [(i, (i + by) % n) for i in range(n)])  34.1 us
    all_to_all x1, blocking collectives, body(): terms = lax.all_to_all(terms, ROW, split_axis=0, concat_axis=0, tiled=True)  33.3 us
    all_to_all x1, waiting for transfers between devices, body(): lax.all_to_all(sent, (ROW, 'head'), split_axis=0, concat_axis=0, tiled=True)  30.9 us
    pallas_call x2, Pallas kernels, attend(): pl.pallas_call(functools.partial(attend_kernel, width ** (-0.5), len(keys...  30.1 us
    ppermute x9, waiting for transfers between devices, shift(): return lax.ppermute(value, axis, [(i, (i + by) % n) for i in range(n)])  24.6 us
    all_to_all x1, starting transfers between devices, body(): lax.all_to_all(sent, (ROW, 'head'), split_axis=0, concat_axis=0, tiled=True)  15.6 us
    all_to_all x1, waiting for transfers between devices, body(): lax.all_to_all(weight, ROW, split_axis=0, concat_axis=0, tiled=True)  14.3 us
    unnamed x11, local copies, waits for them, and re-layouts  5.24 us
  transfers between devices with their start and end apart: 15, of which 7 were waited for; matrix products, arithmetic and copies ran while one was open for 5% of the time, Pallas kernels for 13%

profile of v4, /device:TPU:6, one launch (start us, length us, event | category | flops | bytes accessed | tf_op | source)
XLA Modules:
  0.0 230.1 jit_solution(15808098879160267155)
XLA Ops:
  8.0 1.7 pad_maximum_fusion
  10.4 1.3 fusion.3.refs_0_
  11.7 7.8 %collective-permute-start.1 = (bf16[4112,128]{1,0:T(8,128)(2,1)S(1)}, bf16[4112,128]{1,0:T(8,128)(2,1)}, u32[]{:S(2)}, u32[]{:S(2)}) collective-permute-start(bf16[4112,128]{1,0:T(8,128)(2,1)S(1)} %fusion.3.refs_0_), channel_id=1, source_target_pairs={{0,16},{16,32},{32,48},{48,0},{1,17},{17,33},{33,49},{49,1},{2,18}... | collective-permute-start | bytes 3158024 | tf_op jit(solution)/shard_map/ppermute | solution.py:21
  19.5 1.9 collective-permute-start.2
  21.4 3.5 %all-to-all-start.1 = ((bf16[8,128,256]{2,1,0:T(8,128)(2,1)}), bf16[8,128,256]{2,1,0:T(8,128)(2,1)S(1)}, u32[]{:S(2)}, u32[]{:S(2)}) async-start(bf16[8,128,256]{2,1,0:T(8,128)(2,1)} %bitcast.26), calls=%async_computation.1 | async-start | bytes 1048576 | tf_op jit(solution)/shard_map/all_to_all | solution.py:302
  25.0 2.5 %collective-permute-start = (bf16[4112,128]{1,0:T(8,128)(2,1)S(1)}, bf16[4112,128]{1,0:T(8,128)(2,1)S(1)}, u32[]{:S(2)}, u32[]{:S(2)}) collective-permute-start(bf16[4112,128]{1,0:T(8,128)(2,1)S(1)} %fusion.3.refs_0_), channel_id=1, source_target_pairs={{0,48},{16,0},{32,16},{48,32},{1,49},{17,1},{33,17},{49,33},{2,50}... | collective-permute-start | bytes 3158024 | tf_op jit(solution)/shard_map/ppermute | solution.py:21
  27.5 4.6 %collective-permute-start.3 = (bf16[4096,128]{1,0:T(8,128)(2,1)}, bf16[4096,128]{1,0:T(8,128)(2,1)}, u32[]{:S(2)}, u32[]{:S(2)}) collective-permute-start(bf16[4096,128]{1,0:T(8,128)(2,1)} %bitcast.10.refs_3_), channel_id=1, source_target_pairs={{0,16},{16,32},{32,48},{48,0},{1,17},{17,33},{33,49},{49,1},{2,18}... | collective-permute-start | bytes 3145736 | tf_op jit(solution)/shard_map/ppermute | solution.py:21
  32.1 14.3 %all-to-all-done.1 = bf16[8,128,256]{2,1,0:T(8,128)(2,1)S(1)} async-done(((bf16[8,128,256]{2,1,0:T(8,128)(2,1)}), bf16[8,128,256]{2,1,0:T(8,128)(2,1)S(1)}, u32[]{:S(2)}, u32[]{:S(2)}) %all-to-all-start.1) | async-done | bytes 524320 | tf_op jit(solution)/shard_map/all_to_all | solution.py:302
  47.2 1.8 collective-permute-done.2.refs_4_
  49.0 1.9 collective-permute-start.5
  51.6 19.8 %collective-permute-done.refs_1_ = bf16[4112,128]{1,0:T(8,128)(2,1)S(1)} collective-permute-done((bf16[4112,128]{1,0:T(8,128)(2,1)S(1)}, bf16[4112,128]{1,0:T(8,128)(2,1)S(1)}, u32[]{:S(2)}, u32[]{:S(2)}) %collective-permute-start) | collective-permute-done | bytes 1052704 | tf_op jit(solution)/shard_map/ppermute | solution.py:21
  71.4 1.0 copy-done.1
  72.5 1.9 collective-permute-start.4
  74.5 1.0 fusion.32
  76.5 1.2 copy-done.2
  77.7 19.3 %shard_map.82 = (f32[8,1024,128]{2,1,0:T(8,128)}, f32[8,1024,128]{2,1,0:T(8,128)}) custom-call(s32[128]{0:T(128)S(1)} %reshape.427.slot_ref, bf16[8,144,1024]{2,1,0:T(8,128)(2,1)} %all-gather.4.cloned.1.call-done.q_ref, f32[8,16,128]{2,1,0:T(8,128)S(1)} %get-tuple-element.43.cos_ref, f32[8,16,128]{2,1,0:T(8,128)S(1)} %get-tuple-element.44.sin_ref, ...), custom_call_target="tpu_custom_call" | custom-call | flops 3221225472 | bytes 50331648 | tf_op jit(solution)/shard_map/pallas_call | solution.py:190
  98.0 10.8 %shard_map.83 = (bf16[2,8,8,64,128]{4,3,2,1,0:T(8,128)(2,1)S(1)}, f32[8,8,128]{2,1,0:T(8,128)S(1)}) custom-call(s32[128]{0:T(128)S(1)} %reshape.426.slot_ref, bf16[8,144,1024]{2,1,0:T(8,128)(2,1)} %all-gather.4.cloned.1.call-done.q_ref, f32[8,16,128]{2,1,0:T(8,128)S(1)} %pad_maximum_fusion.3.cos_ref, f32[8,16,128]{2,1,0:T(8,128)S(1)} %pad_maximum_fusion.4.sin_ref, ...), custom_call_target="tpu_custom_call" | custom-call | flops 1073741824 | bytes 16777216 | tf_op jit(solution)/shard_map/pallas_call | solution.py:190
  109.0 1.9 collective-permute-start.7
  111.1 2.4 %collective-permute-start.6 = (bf16[8,8,64,128]{3,2,1,0:T(8,128)(2,1)S(1)}, bf16[8,8,64,128]{3,2,1,0:T(8,128)(2,1)S(1)}, u32[]{:S(2)}, u32[]{:S(2)}) collective-permute-start(bf16[8,8,64,128]{3,2,1,0:T(8,128)(2,1)S(1)} %get-tuple-element.28), channel_id=1, source_target_pairs={{0,8},{8,0},{1,9},{9,1},{2,10},{10,2},{3,11},{11,3},{4,12},{12,4},... | collective-permute-start | bytes 3145736 | tf_op jit(solution)/shard_map/ppermute | solution.py:335
  113.8 2.0 collective-permute-done.6
  115.8 1.5 multiply_reduce_fusion
  117.3 1.1 fusion.2
  118.4 15.6 %all-to-all-start = ((bf16[64,72,128]{2,1,0:T(8,128)(2,1)}), bf16[64,72,128]{2,1,0:T(8,128)(2,1)S(1)}, u32[]{:S(2)}, u32[]{:S(2)}) async-start(bf16[64,72,128]{2,1,0:T(8,128)(2,1)} %fusion.2), calls=%async_computation | async-start | bytes 2359296 | tf_op jit(solution)/shard_map/all_to_all | solution.py:345
  135.2 30.9 %all-to-all-done = bf16[64,72,128]{2,1,0:T(8,128)(2,1)S(1)} async-done(((bf16[64,72,128]{2,1,0:T(8,128)(2,1)}), bf16[64,72,128]{2,1,0:T(8,128)(2,1)S(1)}, u32[]{:S(2)}, u32[]{:S(2)}) %all-to-all-start) | async-done | bytes 1179680 | tf_op jit(solution)/shard_map/all_to_all | solution.py:345
  167.1 5.8 %collective-permute-start.10 = (bf16[8,64,128]{2,1,0:T(8,128)(2,1)S(1)}, bf16[8,64,128]{2,1,0:T(8,128)(2,1)S(1)}, u32[]{:S(2)}, u32[]{:S(2)}) collective-permute-start(bf16[8,64,128]{2,1,0:T(8,128)(2,1)S(1)} %select_convert_fusion.refs_0_), channel_id=1, source_target_pairs={{0,16},{16,32},{32,48},{48,0},{1,17},{17,33},{33,49},{49,1},{2,18}... | collective-permute-start | bytes 393224 | tf_op jit(solution)/shard_map/ppermute | solution.py:21
  172.9 1.9 collective-permute-start.8
  174.9 5.9 %collective-permute-start.9 = (bf16[8,64,128]{2,1,0:T(8,128)(2,1)S(1)}, bf16[8,64,128]{2,1,0:T(8,128)(2,1)S(1)}, u32[]{:S(2)}, u32[]{:S(2)}) collective-permute-start(bf16[8,64,128]{2,1,0:T(8,128)(2,1)S(1)} %select_convert_fusion.refs_0_), channel_id=1, source_target_pairs={{0,32},{16,48},{32,0},{48,16},{1,33},{17,49},{33,1},{49,17},{2,34}... | collective-permute-start | bytes 393224 | tf_op jit(solution)/shard_map/ppermute | solution.py:21
  180.8 1.2 collective-permute-done.8.refs_1_
  181.9 1.7 collective-permute-done.9.refs_2_
  183.7 2.2 copy-done
  185.9 3.3 %shard_map.84 = bf16[8,256,256]{2,1,0:T(8,128)(2,1)S(1)} custom-call(s32[4]{0:T(128)S(1)} %and_select_fusion.5.where_ref, bf16[8,64,128]{2,1,0:T(8,128)(2,1)S(1)} %select_convert_fusion.refs_0_, bf16[8,64,128]{2,1,0:T(8,128)(2,1)S(1)} %collective-permute-done.8.refs_1_, bf16[8,64,128]{2,1,0:T(8,128)(2,1)S(1)} %collective-permute-done.9.refs_2_, ...), custom_call_target="tpu_custom_call" | custom-call | tf_op jit(solution)/shard_map/pallas_call | solution.py:236
  189.2 33.3 %all_to_all.15 = bf16[8,256,256]{2,1,0:T(8,128)(2,1)S(1)} all-to-all(bf16[8,256,256]{2,1,0:T(8,128)(2,1)S(1)} %shard_map.84), channel_id=1, replica_groups=mesh['lib_0'=8,'lib_1'=4,'ctx'=2,'head'=8] {'lib_0'}, dimensions={0} | all-to-all | bytes 2097152 | tf_op jit(solution)/shard_map/all_to_all | solution.py:355
  (68 shorter events, 8.5 us)
Async XLA Ops:
  6.5 67.9 %all-gather.4.cloned.1.call-start = ((), (), s32[]{:S(2)}) async-start(), calls=%async_computation.3 | async-start | bytes 2654208 | tf_op jit(solution)/shard_map/all_gather | solution.py:299
  11.7 39.2 %collective-permute-start.1 = (bf16[4112,128]{1,0:T(8,128)(2,1)S(1)}, bf16[4112,128]{1,0:T(8,128)(2,1)}, u32[]{:S(2)}, u32[]{:S(2)}) collective-permute-start(bf16[4112,128]{1,0:T(8,128)(2,1)S(1)} %fusion.3.refs_0_), channel_id=1, source_target_pairs={{0,16},{16,32},{32,48},{48,0},{1,17},{17,33},{33,49},{49,1},{2,18}... | collective-permute-start | bytes 3158024 | tf_op jit(solution)/shard_map/ppermute | solution.py:21
  19.5 29.5 %collective-permute-start.2 = (bf16[4096,128]{1,0:T(8,128)(2,1)}, bf16[4096,128]{1,0:T(8,128)(2,1)}, u32[]{:S(2)}, u32[]{:S(2)}) collective-permute-start(bf16[4096,128]{1,0:T(8,128)(2,1)} %bitcast.10.refs_3_), channel_id=1, source_target_pairs={{0,48},{16,0},{32,16},{48,32},{1,49},{17,1},{33,17},{49,33},{2,50}... | collective-permute-start | bytes 3145736 | tf_op jit(solution)/shard_map/ppermute | solution.py:21
  21.4 25.0 %all-to-all-start.1 = ((bf16[8,128,256]{2,1,0:T(8,128)(2,1)}), bf16[8,128,256]{2,1,0:T(8,128)(2,1)S(1)}, u32[]{:S(2)}, u32[]{:S(2)}) async-start(bf16[8,128,256]{2,1,0:T(8,128)(2,1)} %bitcast.26), calls=%async_computation.1 | async-start | bytes 1048576 | tf_op jit(solution)/shard_map/all_to_all | solution.py:302
  24.9 158.8 %all-gather.6.cloned.1.call-start = ((), (), s32[]{:S(2)}) async-start(), calls=%async_computation.4 | async-start | bytes 4718592 | tf_op jit(solution)/shard_map/all_gather | solution.py:303
  25.0 46.5 %collective-permute-start = (bf16[4112,128]{1,0:T(8,128)(2,1)S(1)}, bf16[4112,128]{1,0:T(8,128)(2,1)S(1)}, u32[]{:S(2)}, u32[]{:S(2)}) collective-permute-start(bf16[4112,128]{1,0:T(8,128)(2,1)S(1)} %fusion.3.refs_0_), channel_id=1, source_target_pairs={{0,48},{16,0},{32,16},{48,32},{1,49},{17,1},{33,17},{49,33},{2,50}... | collective-permute-start | bytes 3158024 | tf_op jit(solution)/shard_map/ppermute | solution.py:21
  27.5 49.0 %collective-permute-start.3 = (bf16[4096,128]{1,0:T(8,128)(2,1)}, bf16[4096,128]{1,0:T(8,128)(2,1)}, u32[]{:S(2)}, u32[]{:S(2)}) collective-permute-start(bf16[4096,128]{1,0:T(8,128)(2,1)} %bitcast.10.refs_3_), channel_id=1, source_target_pairs={{0,16},{16,32},{32,48},{48,0},{1,17},{17,33},{33,49},{49,1},{2,18}... | collective-permute-start | bytes 3145736 | tf_op jit(solution)/shard_map/ppermute | solution.py:21
  46.3 0.8 copy-start.3
  49.0 49.0 %collective-permute-start.5 = (bf16[4096,128]{1,0:T(8,128)(2,1)}, bf16[4096,128]{1,0:T(8,128)(2,1)}, u32[]{:S(2)}, u32[]{:S(2)}) collective-permute-start(bf16[4096,128]{1,0:T(8,128)(2,1)} %collective-permute-done.2.refs_4_), channel_id=1, source_target_pairs={{0,48},{16,0},{32,16},{48,32},{1,49},{17,1},{33,17},{49,33},{2,50}... | collective-permute-start | bytes 3145736 | tf_op jit(solution)/shard_map/ppermute | solution.py:21
  71.4 1.0 copy-start.1
  72.5 24.5 %collective-permute-start.4 = (bf16[4112,128]{1,0:T(8,128)(2,1)}, bf16[4112,128]{1,0:T(8,128)(2,1)S(1)}, u32[]{:S(2)}, u32[]{:S(2)}) collective-permute-start(bf16[4112,128]{1,0:T(8,128)(2,1)} %collective-permute-done.1.refs_2_), channel_id=1, source_target_pairs={{0,16},{16,32},{32,48},{48,0},{1,17},{17,33},{33,49},{49,1},{2,18}... | collective-permute-start | bytes 3158024 | tf_op jit(solution)/shard_map/ppermute | solution.py:21
  76.4 1.2 copy-start.2
  109.0 4.6 %collective-permute-start.7 = (f32[8,8,64]{2,1,0:T(8,128)S(1)}, f32[8,8,64]{2,1,0:T(8,128)S(1)}, u32[]{:S(2)}, u32[]{:S(2)}) collective-permute-start(f32[8,8,64]{2,1,0:T(8,128)S(1)} %bitcast.69), channel_id=1, source_target_pairs={{0,8},{8,0},{1,9},{9,1},{2,10},{10,2},{3,11},{11,3},{4,12},{12,4},... | collective-permute-start | bytes 49160 | tf_op jit(solution)/shard_map/ppermute | solution.py:336
  111.1 4.7 %collective-permute-start.6 = (bf16[8,8,64,128]{3,2,1,0:T(8,128)(2,1)S(1)}, bf16[8,8,64,128]{3,2,1,0:T(8,128)(2,1)S(1)}, u32[]{:S(2)}, u32[]{:S(2)}) collective-permute-start(bf16[8,8,64,128]{3,2,1,0:T(8,128)(2,1)S(1)} %get-tuple-element.28), channel_id=1, source_target_pairs={{0,8},{8,0},{1,9},{9,1},{2,10},{10,2},{3,11},{11,3},{4,12},{12,4},... | collective-permute-start | bytes 3145736 | tf_op jit(solution)/shard_map/ppermute | solution.py:335
  118.4 47.8 %all-to-all-start = ((bf16[64,72,128]{2,1,0:T(8,128)(2,1)}), bf16[64,72,128]{2,1,0:T(8,128)(2,1)S(1)}, u32[]{:S(2)}, u32[]{:S(2)}) async-start(bf16[64,72,128]{2,1,0:T(8,128)(2,1)} %fusion.2), calls=%async_computation | async-start | bytes 2359296 | tf_op jit(solution)/shard_map/all_to_all | solution.py:345
  167.1 13.6 %collective-permute-start.10 = (bf16[8,64,128]{2,1,0:T(8,128)(2,1)S(1)}, bf16[8,64,128]{2,1,0:T(8,128)(2,1)S(1)}, u32[]{:S(2)}, u32[]{:S(2)}) collective-permute-start(bf16[8,64,128]{2,1,0:T(8,128)(2,1)S(1)} %select_convert_fusion.refs_0_), channel_id=1, source_target_pairs={{0,16},{16,32},{32,48},{48,0},{1,17},{17,33},{33,49},{49,1},{2,18}... | collective-permute-start | bytes 393224 | tf_op jit(solution)/shard_map/ppermute | solution.py:21
  172.9 9.0 %collective-permute-start.8 = (bf16[8,64,128]{2,1,0:T(8,128)(2,1)S(1)}, bf16[8,64,128]{2,1,0:T(8,128)(2,1)S(1)}, u32[]{:S(2)}, u32[]{:S(2)}) collective-permute-start(bf16[8,64,128]{2,1,0:T(8,128)(2,1)S(1)} %select_convert_fusion.refs_0_), channel_id=1, source_target_pairs={{0,48},{16,0},{32,16},{48,32},{1,49},{17,1},{33,17},{49,33},{2,50}... | collective-permute-start | bytes 393224 | tf_op jit(solution)/shard_map/ppermute | solution.py:21
  174.9 8.8 %collective-permute-start.9 = (bf16[8,64,128]{2,1,0:T(8,128)(2,1)S(1)}, bf16[8,64,128]{2,1,0:T(8,128)(2,1)S(1)}, u32[]{:S(2)}, u32[]{:S(2)}) collective-permute-start(bf16[8,64,128]{2,1,0:T(8,128)(2,1)S(1)} %select_convert_fusion.refs_0_), channel_id=1, source_target_pairs={{0,32},{16,48},{32,0},{48,16},{1,33},{17,49},{33,1},{49,17},{2,34}... | collective-permute-start | bytes 393224 | tf_op jit(solution)/shard_map/ppermute | solution.py:21
  183.7 2.2 copy-start
Sparse Core Ops, SparseCore 0:
  9.8 55.1 all-gather.3
  67.1 59.5 all-gather.5

commit v5 on v4

--- a/solution.py
+++ b/solution.py
@@ -21,10 +21,6 @@
     return lax.ppermute(value, axis, [(i, (i + by) % n) for i in range(n)])
 
 
-def far_first(n):
-    return sorted(range(1, n), key=lambda d: -min(d, n - d))
-
-
 def coded(integers):
     return (integers // 128).astype(jnp.bfloat16), (integers % 128).astype(jnp.bfloat16)
 
@@ -33,18 +29,15 @@
     return high.astype(jnp.int32) * 128 + low.astype(jnp.int32)
 
 
-def gather_pieces(value, axis):
-    n = lax.axis_size(axis)
-    pieces = [value] * n
-    for d in far_first(n):
-        pieces[d] = shift(value, axis, -d)
-    return pieces
-
-
-def attend_kernel(scale, pieces, first, last, slot_ref, q_ref, cos_ref, sin_ref, *refs):
-    key_refs, value_refs, refs = refs[:pieces], refs[pieces : 2 * pieces], refs[2 * pieces :]
+def attend_kernel(scale, pieces, first, last, values_at, slot_ref, q_ref, cos_ref, sin_ref, *refs):
+    key_refs, refs = refs[:pieces], refs[pieces:]
+    value_refs = key_refs
+    if last:
+        value_refs, refs = refs[:pieces], refs[pieces:]
     if not first:
         (before_ref, before_lse_ref), refs = refs[:2], refs[2:]
+    if last:
+        other_ref, refs = refs[1], refs[:1] + refs[2:]
     out_ref, lse_ref, q_scr, tile, k_scr, v_scr, s_scr, m_scr, acc_scr, used, entry = refs
     prompt = pl.program_id(0)
     listed, width = cos_ref.shape[1:]
@@ -52,7 +45,7 @@
     group = q_ref.shape[2] // width
     total_rows = rows * group
     tokens = tile.shape[0]
-    held = key_refs[0].shape[0] // tokens
+    held = key_refs[0].shape[0] // tokens if last else values_at // tokens
     factor = scale * 1.4426950408889634
     chunks = [slice(r, r + CHUNK) for r in range(0, total_rows, CHUNK)]
 
@@ -77,9 +70,9 @@
     count = lax.fori_loop(0, listed, note, 0)
     pairs = (count + 1) // 2
 
-    def fetch(refs, slot):
+    def fetch(refs, slot, start):
         def at(index):
-            return pl.ds(pl.multiple_of(index * tokens, tokens), tokens)
+            return pl.ds(pl.multiple_of(index * tokens + start, 16), tokens)
 
         if pieces == 1:
             return refs[0][at(slot)]
@@ -94,7 +87,7 @@
     def score(t, carry):
         for b in range(2):
             i = jnp.minimum(2 * t + b, count - 1)
-            keys = fetch(key_refs, used[i]).astype(jnp.float32)
+            keys = fetch(key_refs, used[i], 0).astype(jnp.float32)
             cosine = cos_ref[0, pl.ds(entry[i], 1), :]
             sine = sin_ref[0, pl.ds(entry[i], 1), :]
             turned = keys * cosine + pltpu.roll(keys, width // 2, 1) * sine
@@ -131,7 +124,7 @@
     def weigh(t, carry):
         for b in range(2):
             i = jnp.minimum(2 * t + b, count - 1)
-            v_scr[b * tokens : (b + 1) * tokens, :width] = fetch(value_refs, used[i])
+            v_scr[b * tokens : (b + 1) * tokens, :width] = fetch(value_refs, used[i], 0 if last else values_at)
         for span in chunks:
             m = m_scr[span]
             parts = [
@@ -143,6 +136,8 @@
         return carry
 
     lax.fori_loop(0, pairs, weigh, 0)
+    if last:
+        core = slot_ref[pl.num_programs(0) * listed]
     row = lax.broadcasted_iota(jnp.int32, (rows, rows), 0)
     column = lax.broadcasted_iota(jnp.int32, (rows, rows), 1)
     for g in range(group):
@@ -153,10 +148,15 @@
         out = acc_scr[span, :width] / total
         lse = m_scr[span] * scale + jnp.log(total)
         if last:
-            halves = out_ref.shape[0]
-            part = rows // halves
-            for c in range(halves):
-                out_ref[c, g, 0] = out[c * part : (c + 1) * part].astype(out_ref.dtype)
+            out = out.astype(out_ref.dtype)
+            part = rows // 2
+            for c in range(2):
+
+                @pl.when(core == c)
+                def _():
+                    out_ref[g, 0] = out[c * part : (c + 1) * part]
+                    other_ref[g, 0] = out[(1 - c) * part : (2 - c) * part]
+
             lse_ref[0, g : g + 1, :] = jnp.sum(
                 jnp.where(row == column, lse, 0.0), axis=0, keepdims=True
             )
@@ -165,7 +165,7 @@
             lse_ref[0, span] = lse
 
 
-def attend(slots, query, cosine, sine, keys, values, before, halves, rows, tokens):
+def attend(slots, query, cosine, sine, keys, values, before, rows, tokens, values_at):
     prompts, _, features = query.shape
     listed, width = cosine.shape[1:]
     group = features // width
@@ -173,28 +173,25 @@
     whole = pl.BlockSpec(memory_space=pltpu.VMEM)
     table = pl.BlockSpec((1, listed, width), lambda j, s: (j, 0, 0))
     state = pl.BlockSpec((1, rows * group, width), lambda j, s: (j, 0, 0))
-    if halves:
-        part = rows // halves
-        out = (
-            jax.ShapeDtypeStruct((halves, group, prompts, part, width), jnp.bfloat16),
-            jax.ShapeDtypeStruct((prompts, group, rows), jnp.float32),
-        )
-        out_specs = (
-            pl.BlockSpec((halves, group, 1, part, width), lambda j, s: (0, 0, j, 0, 0)),
-            pl.BlockSpec((1, group, rows), lambda j, s: (j, 0, 0)),
-        )
+    if before:
+        half = jax.ShapeDtypeStruct((group, prompts, rows // 2, width), jnp.bfloat16)
+        half_spec = pl.BlockSpec((group, 1, rows // 2, width), lambda j, s: (0, j, 0, 0))
+        out = (half, half, jax.ShapeDtypeStruct((prompts, group, rows), jnp.float32))
+        out_specs = (half_spec, half_spec, pl.BlockSpec((1, group, rows), lambda j, s: (j, 0, 0)))
     else:
         out = (jax.ShapeDtypeStruct((prompts, rows * group, width), jnp.float32),) * 2
         out_specs = (state, state)
     work = prompts * most // 2 * rows * group * tokens
     return pl.pallas_call(
-        functools.partial(attend_kernel, width**-0.5, len(keys), before is None, bool(halves)),
+        functools.partial(
+            attend_kernel, width**-0.5, len(keys), before is None, before is not None, values_at
+        ),
         out_shape=out,
         grid_spec=pltpu.PrefetchScalarGridSpec(
             num_scalar_prefetch=1,
             grid=(prompts,),
             in_specs=[pl.BlockSpec((1, rows, features), lambda j, s: (j, 0, 0)), table, table]
-            + [whole] * (2 * len(keys))
+            + [whole] * (len(keys) + len(values))
             + ([state, state] if before else []),
             out_specs=out_specs,
             scratch_shapes=[
@@ -216,35 +213,33 @@
     )(slots, query, cosine, sine, *keys, *values, *(before or ()))
 
 
-def project_kernel(columns, where_ref, *refs):
-    pieces, weight_ref, out_ref = refs[:columns], refs[columns], refs[columns + 1]
-    heads, rows = pieces[0].shape[:2]
+def project_kernel(rows_ref, weight_ref, out_ref):
+    columns, heads = rows_ref.shape[:2]
     left = jnp.concatenate(
-        [jnp.concatenate([p[h] for h in range(heads)], axis=1) for p in pieces], axis=0
+        [
+            jnp.concatenate([rows_ref[d, h] for h in range(heads)], axis=1)
+            for d in range(columns)
+        ],
+        axis=0,
     )
     right = jnp.concatenate([weight_ref[h, 0] for h in range(heads)], axis=0)
-    term = jnp.dot(left, right, preferred_element_type=jnp.float32).astype(out_ref.dtype)
-    for d in range(columns):
-        at = pl.multiple_of(where_ref[d] * rows, rows)
-        out_ref[0, pl.ds(at, rows), :] = term[d * rows : (d + 1) * rows]
-
-
-def project(where, pieces, weight):
-    columns = len(pieces)
-    heads, rows, width = pieces[0].shape
+    out_ref[0] = jnp.dot(left, right, preferred_element_type=jnp.float32).astype(out_ref.dtype)
+
+
+def project(rows_in, weight):
+    columns, heads, rows, width = rows_in.shape
     owners, out_columns = weight.shape[1], weight.shape[3]
     return pl.pallas_call(
-        functools.partial(project_kernel, columns),
+        project_kernel,
         out_shape=jax.ShapeDtypeStruct((owners, columns * rows, out_columns), jnp.bfloat16),
-        grid_spec=pltpu.PrefetchScalarGridSpec(
-            num_scalar_prefetch=1,
-            grid=(owners,),
-            in_specs=[pl.BlockSpec((heads, rows, width), lambda s, w: (0, 0, 0))] * columns
-            + [pl.BlockSpec((heads, 1, width, out_columns), lambda s, w: (0, s, 0, 0))],
-            out_specs=pl.BlockSpec((1, columns * rows, out_columns), lambda s, w: (s, 0, 0)),
-        ),
-        compiler_params=pltpu.CompilerParams(vmem_limit_bytes=32 * 1024 * 1024),
-    )(where, *pieces, weight)
+        grid=(owners,),
+        in_specs=[
+            pl.BlockSpec((columns, heads, rows, width), lambda s: (0, 0, 0, 0)),
+            pl.BlockSpec((heads, 1, width, out_columns), lambda s: (0, s, 0, 0)),
+        ],
+        out_specs=pl.BlockSpec((1, columns * rows, out_columns), lambda s: (s, 0, 0)),
+        compiler_params=pltpu.CompilerParams(vmem_limit_bytes=60 * 1024 * 1024),
+    )(rows_in, weight)
 
 
 def merged(outs, lses):
@@ -284,19 +279,23 @@
     halves = lax.axis_size("ctx")
     half_rows = prompt_rows // halves
 
-    behind = jnp.pad(jnp.stack(coded(offsets)), ((0, 14), (0, width - held)))
-    own_keys = jnp.concatenate([passage_keys.reshape(-1, width), behind], axis=0)
-    own_values = passage_values.reshape(-1, width)
-    keys = [own_keys, shift(own_keys, COL, -1), None, shift(own_keys, COL, 1)]
-    values = [own_values, shift(own_values, COL, -1), None, shift(own_values, COL, 1)]
-    keys[2] = shift(keys[3], COL, 1)
-    values[2] = shift(values[1], COL, -1)
+    tail = jnp.pad(jnp.stack(coded(offsets)), ((0, 14), (0, width - held)))
+    own = jnp.concatenate(
+        [passage_keys.reshape(-1, width), tail, passage_values.reshape(-1, width)], axis=0
+    )
+    values_at = held * tokens + 16
+    pieces = {0: own, 1: shift(own, COL, -1), 3: shift(own, COL, 1)}
+    opposite = (
+        shift(pieces[3][:values_at], COL, 1),
+        shift(pieces[1][values_at:], COL, -1),
+    )
 
     asked = jnp.concatenate([passage_list[0], targets[0], row_counts])
     asked = jnp.stack(coded(asked))
     asked = jnp.pad(asked, ((0, 14), (0, features - asked.shape[1])))
     query = jnp.concatenate([queries, asked[None]], axis=1)
     query = lax.all_gather(query, ROW, axis=0, tiled=True)
+    query, pieces = lax.optimization_barrier((query, pieces))
     asked = decoded(query[:, prompt_rows], query[:, prompt_rows + 1])
     weight = out_weight.reshape(group, width, -1)
     weight = lax.all_to_all(weight, ROW, split_axis=0, concat_axis=0, tiled=True)
@@ -317,41 +316,40 @@
         moved = asked[:, listed : 2 * listed] - jnp.sum(jnp.where(same, near, 0), axis=-1)
         return (slots.reshape(-1), *turns(moved, width))
 
-    before = None
-    for order, laid_out in (((0, 1, 3), 0), ((2,), halves)):
-        pieces = [keys[d] for d in order]
-        if before is not None:
-            before, pieces = lax.optimization_barrier((before, pieces))
-        slots, cosine, sine = tables(order, pieces)
-        before = attend(
-            slots, query, cosine, sine, pieces, [values[d] for d in order], before, laid_out,
-            prompt_rows, tokens,
-        )
-    out, lse = before
+    early = (0, 1, 3)
+    pieces = [pieces[d] for d in early]
+    slots, cosine, sine = tables(early, pieces)
+    sizes = (prompt_rows, tokens, values_at)
+    before = attend(slots, query, cosine, sine, pieces, [], None, *sizes)
+    before, opposite = lax.optimization_barrier((before, opposite))
+    slots, cosine, sine = tables((2,), opposite[:1])
+    slots = jnp.concatenate([slots, c[None]])
+    out, other, lse = attend(
+        slots, query, cosine, sine, opposite[:1], opposite[1:], before, *sizes
+    )
 
     lse = jnp.transpose(lse.reshape(rows_of, group, halves, half_rows), (2, 1, 0, 3))
     swap = [(i, 1 - i) for i in range(2)]
     pick = functools.partial(lax.dynamic_index_in_dim, axis=0, keepdims=False)
-    other = lax.ppermute(pick(out, 1 - c), "ctx", swap)
+    other = lax.ppermute(other, "ctx", swap)
     other_lse = lax.ppermute(pick(lse, 1 - c), "ctx", swap)
-    out, lse = merged(
-        jnp.stack([pick(out, c), other]), jnp.stack([pick(lse, c), other_lse])
-    )
+    out, lse = merged(jnp.stack([out, other]), jnp.stack([pick(lse, c), other_lse]))
 
     out = out.astype(jnp.bfloat16).reshape(group * rows_of, half_rows, width)
     parts = jnp.moveaxis(three_parts(lse.reshape(group * rows_of, half_rows)), 0, 1)
     parts = jnp.pad(parts, ((0, 0), (0, 5), (0, width - half_rows)))
     sent = jnp.concatenate([out, parts], axis=1)
+    count = lax.dynamic_index_in_dim(asked[:, 2 * listed], z, keepdims=False)
+    live = c * half_rows + jnp.arange(half_rows, dtype=jnp.int32) < count
+    sent, live = lax.optimization_barrier((sent, live))
     got = lax.all_to_all(sent, (ROW, "head"), split_axis=0, concat_axis=0, tiled=True)
     got = got.reshape(rows_of, -1, half_rows + 8, width)
     lses = got[:, :, half_rows : half_rows + 3, :half_rows].astype(jnp.float32)
     attended, _ = merged(got[:, :, :half_rows], jnp.sum(lses, axis=2))
-    count = lax.dynamic_index_in_dim(asked[:, 2 * listed], z, keepdims=False)
-    live = c * half_rows + jnp.arange(half_rows, dtype=jnp.int32) < count
     attended = jnp.where(live[:, None], attended, 0.0).astype(jnp.bfloat16)
 
-    where = (x + jnp.arange(columns, dtype=jnp.int32)) % columns
-    terms = project(where, gather_pieces(attended, COL), weight)
+    rows_in = lax.all_gather(attended[None], COL, axis=0, tiled=True)
+    terms = project(rows_in, weight)
     terms = lax.all_to_all(terms, ROW, split_axis=0, concat_axis=0, tiled=True)
     total = jnp.sum(terms.astype(jnp.float32), axis=0)
     return total.astype(jnp.bfloat16)[None]

time: 231 us -> 245 us (1.061)
  blocking collectives: 33.3 us -> 107 us
  waiting for transfers between devices: 71.9 us -> 36.4 us
  starting transfers between devices: 57.6 us -> 23.4 us
  other arithmetic: 11.3 us -> 15.1 us
  Pallas kernels: 33.5 us -> 37 us
  local copies, waits for them, and re-layouts: 8.16 us -> 11.1 us
    all_to_all x0 -> x1, blocking collectives: none -> 61.7 us  [body(): lax.all_to_all(sent, (ROW, 'head'), split_axis=0, concat_axis=0, tiled=True)]
    all_to_all x1 -> x0, waiting for transfers between devices: 30.9 us -> none  [body(): lax.all_to_all(sent, (ROW, 'head'), split_axis=0, concat_axis=0, tiled=True)]
    ppermute x9 -> x4, starting transfers between devices: 34.1 us -> 15.5 us  [shift(): return lax.ppermute(value, axis, [(i, (i + by) % n) for i in range(n)])]
    all_to_all x1 -> x0, starting transfers between devices: 15.6 us -> none  [body(): lax.all_to_all(sent, (ROW, 'head'), split_axis=0, concat_axis=0, tiled=True)]
    all_gather x0 -> x1, blocking collectives: none -> 13.9 us  [body(): rows_in = lax.all_gather(attended[None], COL, axis=0, tiled=True)]
    ppermute x9 -> x4, waiting for transfers between devices: 24.6 us -> 12.4 us  [shift(): return lax.ppermute(value, axis, [(i, (i + by) % n) for i in range(n)])]
    all_to_all x1, waiting for transfers between devices: 14.3 us -> 22.9 us  [body(): lax.all_to_all(weight, ROW, split_axis=0, concat_axis=0, tiled=True)]
    concatenate x1 -> x2, other arithmetic: 1.29 us -> 6.17 us  [the longest x1 6.16 us: body(): jnp.concatenate([passage_keys.reshape(-1, width), tail, passage_values.re...]
  transfers between devices with their start and end apart: 15 -> 9, of which waited for: 7 -> 3; matrix products, arithmetic and copies ran while one was open for 5% -> 9% of each run, Pallas kernels for 13% -> 12%
where the time goes in v5:
time: 245 us; the launch traced here: 244 us
  blocking collectives  107 us (44%)
  Pallas kernels  37 us (15%)
  waiting for transfers between devices  36.4 us (15%)
  starting transfers between devices  23.4 us (10%)
  other arithmetic  15.1 us (6%)
  between operations  14.4 us (6%)
  local copies, waits for them, and re-layouts  11.1 us (5%)
    all_to_all x1, blocking collectives, body(): lax.all_to_all(sent, (ROW, 'head'), split_axis=0, concat_axis=0, tiled=True)  61.7 us
    all_to_all x1, blocking collectives, body(): terms = lax.all_to_all(terms, ROW, split_axis=0, concat_axis=0, tiled=True)  31.1 us
    pallas_call x2, Pallas kernels, attend(): pl.pallas_call(functools.partial(attend_kernel, width ** (-0.5), len(keys...  29.9 us
    all_to_all x1, waiting for transfers between devices, body(): lax.all_to_all(weight, ROW, split_axis=0, concat_axis=0, tiled=True)  22.9 us
    ppermute x4, starting transfers between devices, shift(): return lax.ppermute(value, axis, [(i, (i + by) % n) for i in range(n)])  15.5 us
    all_gather x1, blocking collectives, body(): rows_in = lax.all_gather(attended[None], COL, axis=0, tiled=True)  13.9 us
    ppermute x4, waiting for transfers between devices, shift(): return lax.ppermute(value, axis, [(i, (i + by) % n) for i in range(n)])  12.4 us
    pallas_call x1, Pallas kernels, project(): pl.pallas_call(project_kernel, out_shape=jax.ShapeDtypeStruct((owners, co...  7.09 us
  transfers between devices with their start and end apart: 9, of which 3 were waited for; matrix products, arithmetic and copies ran while one was open for 9% of the time, Pallas kernels for 12%

profile of v5, /device:TPU:6, one launch (start us, length us, event | category | flops | bytes accessed | tf_op | source)
XLA Modules:
  0.0 244.2 jit_solution(10240712098504531046)
XLA Ops:
  7.2 0.8 fusion.34
  8.0 1.7 pad_maximum_fusion.1
  9.7 0.7 convert_bitcast_fusion
  10.4 6.2 %pad_maximum_fusion.refs_0_ = bf16[8208,128]{1,0:T(8,128)(2,1)S(1)} fusion(bf16[4096,128]{1,0:T(8,128)(2,1)} %bitcast.69, bf16[16,128]{1,0:T(8,128)(2,1)S(1)} %fusion.26, bf16[4096,128]{1,0:T(8,128)(2,1)} %bitcast.70), kind=kLoop, calls=%fused_computation.3 | loop fusion | flops 6303744 | bytes 4202496 | tf_op jit(solution)/shard_map/concatenate | solution.py:283
  16.5 7.8 %collective-permute-start.1 = (bf16[8208,128]{1,0:T(8,128)(2,1)S(1)}, bf16[8208,128]{1,0:T(8,128)(2,1)}, u32[]{:S(2)}, u32[]{:S(2)}) collective-permute-start(bf16[8208,128]{1,0:T(8,128)(2,1)S(1)} %pad_maximum_fusion.refs_0_), channel_id=1, source_target_pairs={{0,16},{16,32},{32,48},{48,0},{1,17},{17,33},{33,49},{49,1},{2,18}... | collective-permute-start | bytes 6303752 | tf_op jit(solution)/shard_map/ppermute | solution.py:21
  24.3 1.9 collective-permute-start
  26.2 3.5 %all-to-all-start.1 = ((bf16[8,128,256]{2,1,0:T(8,128)(2,1)}), bf16[8,128,256]{2,1,0:T(8,128)(2,1)S(1)}, u32[]{:S(2)}, u32[]{:S(2)}) async-start(bf16[8,128,256]{2,1,0:T(8,128)(2,1)} %bitcast.28), calls=%async_computation.1 | async-start | bytes 1048576 | tf_op jit(solution)/shard_map/all_to_all | solution.py:301
  29.8 22.9 %all-to-all-done.1 = bf16[8,128,256]{2,1,0:T(8,128)(2,1)S(1)} async-done(((bf16[8,128,256]{2,1,0:T(8,128)(2,1)}), bf16[8,128,256]{2,1,0:T(8,128)(2,1)S(1)}, u32[]{:S(2)}, u32[]{:S(2)}) %all-to-all-start.1) | async-done | bytes 524320 | tf_op jit(solution)/shard_map/all_to_all | solution.py:301
  52.7 0.8 copy-done.1
  53.6 12.4 %collective-permute-done.1.refs_2_ = bf16[8208,128]{1,0:T(8,128)(2,1)} collective-permute-done((bf16[8208,128]{1,0:T(8,128)(2,1)S(1)}, bf16[8208,128]{1,0:T(8,128)(2,1)}, u32[]{:S(2)}, u32[]{:S(2)}) %collective-permute-start.1) | collective-permute-done | bytes 2101280 | tf_op jit(solution)/shard_map/ppermute | solution.py:21
  66.0 2.3 slice.75
  68.2 3.4 %collective-permute-start.2 = (bf16[4112,128]{1,0:T(8,128)(2,1)}, bf16[4112,128]{1,0:T(8,128)(2,1)S(1)}, u32[]{:S(2)}, u32[]{:S(2)}) collective-permute-start(bf16[4112,128]{1,0:T(8,128)(2,1)} %slice.75), channel_id=1, source_target_pairs={{0,16},{16,32},{32,48},{48,0},{1,17},{17,33},{33,49},{49,1},{2,18}... | collective-permute-start | bytes 3158024 | tf_op jit(solution)/shard_map/ppermute | solution.py:21
  71.7 2.3 slice.76
  73.9 2.4 collective-permute-start.3
  76.4 0.7 slice_bitcast_fusion.1
  77.2 3.0 %copy.30 = bf16[8,144,1024]{2,0,1:T(8,128)(2,1)S(1)} copy(bf16[8,144,1024]{2,1,0:T(8,128)(2,1)} %all-gather.4.cloned.1.call-done.q_ref) | data formatting | bytes 4718592 | tf_op jit(solution)/shard_map/optimization_barrier | solution.py:298
  81.2 19.6 %shard_map.82 = (f32[8,1024,128]{2,1,0:T(8,128)}, f32[8,1024,128]{2,1,0:T(8,128)}) custom-call(s32[128]{0:T(128)S(1)} %reshape.439.slot_ref, bf16[8,144,1024]{2,1,0:T(8,128)(2,1)} %all-gather.4.cloned.1.call-done.q_ref, f32[8,16,128]{2,1,0:T(8,128)S(1)} %pad_maximum_fusion.2.cos_ref, f32[8,16,128]{2,1,0:T(8,128)S(1)} %pad_maximum_fusion.3.sin_ref, ...), custom_call_target="tpu_custom_call" | custom-call | flops 3221225472 | bytes 50331648 | tf_op jit(solution)/shard_map/pallas_call | solution.py:185
  101.3 0.3 fusion.18
  101.8 10.4 %shard_map.83 = (bf16[8,8,64,128]{3,2,1,0:T(8,128)(2,1)S(1)}, bf16[8,8,64,128]{3,2,1,0:T(8,128)(2,1)S(1)}, f32[8,8,128]{2,1,0:T(8,128)S(1)}) custom-call(s32[129]{0:T(256)S(1)} %pad_add_fusion.slot_ref, bf16[8,144,1024]{2,1,0:T(8,128)(2,1)} %all-gather.4.cloned.1.call-done.q_ref, f32[8,16,128]{2,1,0:T(8,128)S(1)} %pad_maximum_fusion.4.cos_ref, ...), custom_call_target="tpu_custom_call" | custom-call | flops 1073741824 | bytes 16777216 | tf_op jit(solution)/shard_map/pallas_call | solution.py:185
  112.2 1.0 copy-done
  113.3 1.9 collective-permute-start.5
  115.3 2.4 collective-permute-start.4
  117.7 0.5 constant_dynamic-slice_fusion
  118.2 0.7 add_compare_fusion
  119.1 1.1 collective-permute-done.4
  120.2 1.5 multiply_reduce_fusion
  121.8 61.7 %all_to_all.15 = bf16[64,72,128]{2,1,0:T(8,128)(2,1)S(1)} all-to-all(bf16[64,72,128]{2,1,0:T(8,128)(2,1)S(1)} %fusion.1), channel_id=1, replica_groups=mesh['lib_0'=8,'lib_1'=4,'ctx'=2,'head'=8] {'lib_0','head'}, dimensions={0} | all-to-all | bytes 2359296 | tf_op jit(solution)/shard_map/all_to_all | solution.py:345
  183.5 0.7 multiply_reduce_fusion.1
  184.4 13.9 %all_gather.10.rows_ref = bf16[4,8,64,128]{3,2,1,0:T(8,128)(2,1)} all-gather(bf16[1,8,64,128]{3,2,1,0:T(8,128)(2,1)S(1)} %fusion.2), channel_id=1, replica_groups=mesh['lib_0'=8,'lib_1'=4,'ctx'=2,'head'=8] {'lib_1'}, dimensions={0}, use_global_device_ids=true | all-gather | bytes 655360 | tf_op jit(solution)/shard_map/all_gather | solution.py:351
  198.3 7.1 %shard_map.84 = bf16[8,256,256]{2,1,0:T(8,128)(2,1)} custom-call(bf16[4,8,64,128]{3,2,1,0:T(8,128)(2,1)} %all_gather.10.rows_ref, bf16[8,8,128,256]{3,2,1,0:T(8,128)(2,1)} %bitcast.67), custom_call_target="tpu_custom_call" | custom-call | tf_op jit(solution)/shard_map/pallas_call | solution.py:232
  205.4 31.1 %all_to_all.16 = bf16[8,256,256]{2,1,0:T(8,128)(2,1)S(1)} all-to-all(bf16[8,256,256]{2,1,0:T(8,128)(2,1)} %shard_map.84), channel_id=1, replica_groups=mesh['lib_0'=8,'lib_1'=4,'ctx'=2,'head'=8] {'lib_0'}, dimensions={0} | all-to-all | bytes 2097152 | tf_op jit(solution)/shard_map/all_to_all | solution.py:353
  236.5 0.8 reduce_sum.85
  (55 shorter events, 2.5 us)
Async XLA Ops:
  6.5 69.8 %all-gather.4.cloned.1.call-start = ((), (), s32[]{:S(2)}) async-start(), calls=%async_computation.3 | async-start | bytes 2654208 | tf_op jit(solution)/shard_map/all_gather | solution.py:297
  16.5 49.5 %collective-permute-start.1 = (bf16[8208,128]{1,0:T(8,128)(2,1)S(1)}, bf16[8208,128]{1,0:T(8,128)(2,1)}, u32[]{:S(2)}, u32[]{:S(2)}) collective-permute-start(bf16[8208,128]{1,0:T(8,128)(2,1)S(1)} %pad_maximum_fusion.refs_0_), channel_id=1, source_target_pairs={{0,16},{16,32},{32,48},{48,0},{1,17},{17,33},{33,49},{49,1},{2,18}... | collective-permute-start | bytes 6303752 | tf_op jit(solution)/shard_map/ppermute | solution.py:21
  24.3 47.4 %collective-permute-start = (bf16[8208,128]{1,0:T(8,128)(2,1)S(1)}, bf16[8208,128]{1,0:T(8,128)(2,1)}, u32[]{:S(2)}, u32[]{:S(2)}) collective-permute-start(bf16[8208,128]{1,0:T(8,128)(2,1)S(1)} %pad_maximum_fusion.refs_0_), channel_id=1, source_target_pairs={{0,48},{16,0},{32,16},{48,32},{1,49},{17,1},{33,17},{49,33},{2,50}... | collective-permute-start | bytes 6303752 | tf_op jit(solution)/shard_map/ppermute | solution.py:21
  26.2 26.5 %all-to-all-start.1 = ((bf16[8,128,256]{2,1,0:T(8,128)(2,1)}), bf16[8,128,256]{2,1,0:T(8,128)(2,1)S(1)}, u32[]{:S(2)}, u32[]{:S(2)}) async-start(bf16[8,128,256]{2,1,0:T(8,128)(2,1)} %bitcast.28), calls=%async_computation.1 | async-start | bytes 1048576 | tf_op jit(solution)/shard_map/all_to_all | solution.py:301
  29.7 168.5 %all-gather.6.cloned.1.call-start = ((), (), s32[]{:S(2)}) async-start(), calls=%async_computation.4 | async-start | bytes 4718592 | tf_op jit(solution)/shard_map/all_gather | solution.py:302
  52.7 0.8 copy-start.1
  68.2 32.6 %collective-permute-start.2 = (bf16[4112,128]{1,0:T(8,128)(2,1)}, bf16[4112,128]{1,0:T(8,128)(2,1)S(1)}, u32[]{:S(2)}, u32[]{:S(2)}) collective-permute-start(bf16[4112,128]{1,0:T(8,128)(2,1)} %slice.75), channel_id=1, source_target_pairs={{0,16},{16,32},{32,48},{48,0},{1,17},{17,33},{33,49},{49,1},{2,18}... | collective-permute-start | bytes 3158024 | tf_op jit(solution)/shard_map/ppermute | solution.py:21
  73.9 26.9 %collective-permute-start.3 = (bf16[4096,128]{1,0:T(8,128)(2,1)}, bf16[4096,128]{1,0:T(8,128)(2,1)}, u32[]{:S(2)}, u32[]{:S(2)}) collective-permute-start(bf16[4096,128]{1,0:T(8,128)(2,1)} %slice.76), channel_id=1, source_target_pairs={{0,48},{16,0},{32,16},{48,32},{1,49},{17,1},{33,17},{49,33},{2,50}... | collective-permute-start | bytes 3145736 | tf_op jit(solution)/shard_map/ppermute | solution.py:21
  112.2 1.0 copy-start
  113.3 5.5 %collective-permute-start.5 = (f32[8,8,64]{2,1,0:T(8,128)S(1)}, f32[8,8,64]{2,1,0:T(8,128)S(1)}, u32[]{:S(2)}, u32[]{:S(2)}) collective-permute-start(f32[8,8,64]{2,1,0:T(8,128)S(1)} %bitcast.75), channel_id=1, source_target_pairs={{0,8},{8,0},{1,9},{9,1},{2,10},{10,2},{3,11},{11,3},{4,12},{12,4},... | collective-permute-start | bytes 49160 | tf_op jit(solution)/shard_map/ppermute | solution.py:335
  115.3 4.9 %collective-permute-start.4 = (bf16[8,8,64,128]{3,2,1,0:T(8,128)(2,1)}, bf16[8,8,64,128]{3,2,1,0:T(8,128)(2,1)S(1)}, u32[]{:S(2)}, u32[]{:S(2)}) collective-permute-start(bf16[8,8,64,128]{3,2,1,0:T(8,128)(2,1)} %copy-done), channel_id=1, source_target_pairs={{0,8},{8,0},{1,9},{9,1},{2,10},{10,2},{3,11},{11,3},{4,12},{12,4},... | collective-permute-start | bytes 3145736 | tf_op jit(solution)/shard_map/ppermute | solution.py:334
Sparse Core Ops, SparseCore 0:
  9.8 58.6 all-gather.3
  70.6 57.0 all-gather.5

commit v6 on v4

--- a/solution.py
+++ b/solution.py
@@ -21,24 +21,12 @@
     return lax.ppermute(value, axis, [(i, (i + by) % n) for i in range(n)])
 
 
-def far_first(n):
-    return sorted(range(1, n), key=lambda d: -min(d, n - d))
-
-
 def coded(integers):
     return (integers // 128).astype(jnp.bfloat16), (integers % 128).astype(jnp.bfloat16)
 
 
 def decoded(high, low):
     return high.astype(jnp.int32) * 128 + low.astype(jnp.int32)
-
-
-def gather_pieces(value, axis):
-    n = lax.axis_size(axis)
-    pieces = [value] * n
-    for d in far_first(n):
-        pieces[d] = shift(value, axis, -d)
-    return pieces
 
 
 def attend_kernel(scale, pieces, first, last, slot_ref, q_ref, cos_ref, sin_ref, *refs):
@@ -216,35 +204,33 @@
     )(slots, query, cosine, sine, *keys, *values, *(before or ()))
 
 
-def project_kernel(columns, where_ref, *refs):
-    pieces, weight_ref, out_ref = refs[:columns], refs[columns], refs[columns + 1]
-    heads, rows = pieces[0].shape[:2]
+def project_kernel(rows_ref, weight_ref, out_ref):
+    columns, heads = rows_ref.shape[:2]
     left = jnp.concatenate(
-        [jnp.concatenate([p[h] for h in range(heads)], axis=1) for p in pieces], axis=0
+        [
+            jnp.concatenate([rows_ref[d, h] for h in range(heads)], axis=1)
+            for d in range(columns)
+        ],
+        axis=0,
     )
     right = jnp.concatenate([weight_ref[h, 0] for h in range(heads)], axis=0)
-    term = jnp.dot(left, right, preferred_element_type=jnp.float32).astype(out_ref.dtype)
-    for d in range(columns):
-        at = pl.multiple_of(where_ref[d] * rows, rows)
-        out_ref[0, pl.ds(at, rows), :] = term[d * rows : (d + 1) * rows]
-
-
-def project(where, pieces, weight):
-    columns = len(pieces)
-    heads, rows, width = pieces[0].shape
+    out_ref[0] = jnp.dot(left, right, preferred_element_type=jnp.float32).astype(out_ref.dtype)
+
+
+def project(rows_in, weight):
+    columns, heads, rows, width = rows_in.shape
     owners, out_columns = weight.shape[1], weight.shape[3]
     return pl.pallas_call(
-        functools.partial(project_kernel, columns),
+        project_kernel,
         out_shape=jax.ShapeDtypeStruct((owners, columns * rows, out_columns), jnp.bfloat16),
-        grid_spec=pltpu.PrefetchScalarGridSpec(
-            num_scalar_prefetch=1,
-            grid=(owners,),
-            in_specs=[pl.BlockSpec((heads, rows, width), lambda s, w: (0, 0, 0))] * columns
-            + [pl.BlockSpec((heads, 1, width, out_columns), lambda s, w: (0, s, 0, 0))],
-            out_specs=pl.BlockSpec((1, columns * rows, out_columns), lambda s, w: (s, 0, 0)),
-        ),
+        grid=(owners,),
+        in_specs=[
+            pl.BlockSpec((columns, heads, rows, width), lambda s: (0, 0, 0, 0)),
+            pl.BlockSpec((heads, 1, width, out_columns), lambda s: (0, s, 0, 0)),
+        ],
+        out_specs=pl.BlockSpec((1, columns * rows, out_columns), lambda s: (s, 0, 0)),
         compiler_params=pltpu.CompilerParams(vmem_limit_bytes=32 * 1024 * 1024),
-    )(where, *pieces, weight)
+    )(rows_in, weight)
 
 
 def merged(outs, lses):
@@ -294,14 +280,18 @@
 
     asked = jnp.concatenate([passage_list[0], targets[0], row_counts])
     asked = jnp.stack(coded(asked))
-    asked = jnp.pad(asked, ((0, 14), (0, features - asked.shape[1])))
-    query = jnp.concatenate([queries, asked[None]], axis=1)
+    padded = jnp.pad(asked, ((0, 14), (0, features - asked.shape[1])))
+    query = jnp.concatenate([queries, padded[None]], axis=1)
     query = lax.all_gather(query, ROW, axis=0, tiled=True)
-    asked = decoded(query[:, prompt_rows], query[:, prompt_rows + 1])
-    weight = out_weight.reshape(group, width, -1)
+    asked = query[:, prompt_rows : prompt_rows + 2, : asked.shape[1]]
+    asked, keys[1], near_keys = lax.optimization_barrier((asked, keys[1], keys[3]))
+    asked = decoded(asked[:, 0], asked[:, 1])
+    weight, _ = lax.optimization_barrier((out_weight, keys[3]))
+    weight = weight.reshape(group, width, -1)
     weight = lax.all_to_all(weight, ROW, split_axis=0, concat_axis=0, tiled=True)
     weight = lax.all_gather(weight[None], "head", axis=0, tiled=True)
 
+    keys[3] = near_keys
     local = asked[:, :listed] - y * columns * held
     mine = (local >= 0) & (local < columns * held)
     ahead = (local // held - x) % columns
@@ -342,16 +332,18 @@
     parts = jnp.moveaxis(three_parts(lse.reshape(group * rows_of, half_rows)), 0, 1)
     parts = jnp.pad(parts, ((0, 0), (0, 5), (0, width - half_rows)))
     sent = jnp.concatenate([out, parts], axis=1)
+    count = lax.dynamic_index_in_dim(asked[:, 2 * listed], z, keepdims=False)
+    live = c * half_rows + jnp.arange(half_rows, dtype=jnp.int32) < count
+    sent, live = lax.optimization_barrier((sent, live))
     got = lax.all_to_all(sent, (ROW, "head"), split_axis=0, concat_axis=0, tiled=True)
+    got, weight = lax.optimization_barrier((got, weight))
     got = got.reshape(rows_of, -1, half_rows + 8, width)
     lses = got[:, :, half_rows : half_rows + 3, :half_rows].astype(jnp.float32)
     attended, _ = merged(got[:, :, :half_rows], jnp.sum(lses, axis=2))
-    count = lax.dynamic_index_in_dim(asked[:, 2 * listed], z, keepdims=False)
-    live = c * half_rows + jnp.arange(half_rows, dtype=jnp.int32) < count
     attended = jnp.where(live[:, None], attended, 0.0).astype(jnp.bfloat16)
 
-    where = (x + jnp.arange(columns, dtype=jnp.int32)) % columns
-    terms = project(where, gather_pieces(attended, COL), weight)
+    rows_in = lax.all_gather(attended[None], COL, axis=0, tiled=True)
+    terms = project(rows_in, weight)
     terms = lax.all_to_all(terms, ROW, split_axis=0, concat_axis=0, tiled=True)
     total = jnp.sum(terms.astype(jnp.float32), axis=0)
     return total.astype(jnp.bfloat16)[None]

time: 231 us -> 226 us (0.978)
  blocking collectives: 33.3 us -> 87.7 us
  waiting for transfers between devices: 71.9 us -> 32 us
  starting transfers between devices: 57.6 us -> 33.7 us
  Pallas kernels: 33.5 us -> 41.4 us
  local copies, waits for them, and re-layouts: 8.16 us -> 5.66 us
    all_to_all x0 -> x1, blocking collectives: none -> 43.6 us  [body(): lax.all_to_all(sent, (ROW, 'head'), split_axis=0, concat_axis=0, tiled=True)]
    all_to_all x1 -> x0, waiting for transfers between devices: 30.9 us -> none  [body(): lax.all_to_all(sent, (ROW, 'head'), split_axis=0, concat_axis=0, tiled=True)]
    all_to_all x1 -> x0, starting transfers between devices: 15.6 us -> none  [body(): lax.all_to_all(sent, (ROW, 'head'), split_axis=0, concat_axis=0, tiled=True)]
    all_to_all x1, waiting for transfers between devices: 14.3 us -> 0.01 us  [body(): lax.all_to_all(weight, ROW, split_axis=0, concat_axis=0, tiled=True)]
    all_gather x0 -> x1, blocking collectives: none -> 13.4 us  [body(): rows_in = lax.all_gather(attended[None], COL, axis=0, tiled=True)]
    ppermute x9 -> x6, starting transfers between devices: 34.1 us -> 22.2 us  [shift(): return lax.ppermute(value, axis, [(i, (i + by) % n) for i in range(n)])]
    pallas_call x2, Pallas kernels: 30.1 us -> 38.6 us  [attend(): pl.pallas_call(functools.partial(attend_kernel, width ** (-0.5), len(keys...]
    ppermute x9 -> x6, waiting for transfers between devices: 24.6 us -> 31 us  [shift(): return lax.ppermute(value, axis, [(i, (i + by) % n) for i in range(n)])]
  transfers between devices with their start and end apart: 15 -> 11, of which waited for: 7 -> 3; matrix products, arithmetic and copies ran while one was open for 5% -> 4% of each run, Pallas kernels for 13% -> 17%
where the time goes in v6:
time: 226 us; the launch traced here: 225 us
  blocking collectives  87.7 us (39%)
  Pallas kernels  41.4 us (18%)
  starting transfers between devices  33.7 us (15%)
  waiting for transfers between devices  32 us (14%)
  between operations  14.4 us (6%)
  other arithmetic  10.3 us (5%)
  local copies, waits for them, and re-layouts  5.66 us (3%)
    all_to_all x1, blocking collectives, body(): lax.all_to_all(sent, (ROW, 'head'), split_axis=0, concat_axis=0, tiled=True)  43.6 us
    pallas_call x2, Pallas kernels, attend(): pl.pallas_call(functools.partial(attend_kernel, width ** (-0.5), len(keys...  38.6 us
    ppermute x6, waiting for transfers between devices, shift(): return lax.ppermute(value, axis, [(i, (i + by) % n) for i in range(n)])  31 us
    all_to_all x1, blocking collectives, body(): terms = lax.all_to_all(terms, ROW, split_axis=0, concat_axis=0, tiled=True)  30.7 us
    ppermute x6, starting transfers between devices, shift(): return lax.ppermute(value, axis, [(i, (i + by) % n) for i in range(n)])  22.2 us
    all_gather x1, blocking collectives, body(): rows_in = lax.all_gather(attended[None], COL, axis=0, tiled=True)  13.4 us
    all_to_all x1, starting transfers between devices, body(): lax.all_to_all(weight, ROW, split_axis=0, concat_axis=0, tiled=True)  7.1 us
  transfers between devices with their start and end apart: 11, of which 3 were waited for; matrix products, arithmetic and copies ran while one was open for 4% of the time, Pallas kernels for 17%

profile of v6, /device:TPU:6, one launch (start us, length us, event | category | flops | bytes accessed | tf_op | source)
XLA Modules:
  0.0 225.1 jit_solution(3397158444031137456)
XLA Ops:
  7.2 0.8 fusion.30
  8.0 1.7 pad_maximum_fusion
  9.7 0.7 convert_bitcast_fusion
  10.4 1.3 fusion.3.refs_0_
  11.7 7.8 %collective-permute-start.1 = (bf16[4112,128]{1,0:T(8,128)(2,1)S(1)}, bf16[4112,128]{1,0:T(8,128)(2,1)}, u32[]{:S(2)}, u32[]{:S(2)}) collective-permute-start(bf16[4112,128]{1,0:T(8,128)(2,1)S(1)} %fusion.3.refs_0_), channel_id=1, source_target_pairs={{0,16},{16,32},{32,48},{48,0},{1,17},{17,33},{33,49},{49,1},{2,18}... | collective-permute-start | bytes 3158024 | tf_op jit(solution)/shard_map/ppermute | solution.py:21
  19.4 1.9 collective-permute-start
  21.4 1.9 collective-permute-start.2
  23.3 15.4 %collective-permute-done.1.refs_2_ = bf16[4112,128]{1,0:T(8,128)(2,1)} collective-permute-done((bf16[4112,128]{1,0:T(8,128)(2,1)S(1)}, bf16[4112,128]{1,0:T(8,128)(2,1)}, u32[]{:S(2)}, u32[]{:S(2)}) %collective-permute-start.1) | collective-permute-done | bytes 1052704 | tf_op jit(solution)/shard_map/ppermute | solution.py:21
  38.6 7.1 %all-to-all-start.1 = ((bf16[8,128,256]{2,1,0:T(8,128)(2,1)}), bf16[8,128,256]{2,1,0:T(8,128)(2,1)S(1)}, u32[]{:S(2)}, u32[]{:S(2)}) async-start(bf16[8,128,256]{2,1,0:T(8,128)(2,1)} %bitcast.25), calls=%async_computation.1 | async-start | bytes 1048576 | tf_op jit(solution)/shard_map/all_to_all | solution.py:291
  45.8 3.6 %collective-permute-start.3 = (bf16[4096,128]{1,0:T(8,128)(2,1)}, bf16[4096,128]{1,0:T(8,128)(2,1)}, u32[]{:S(2)}, u32[]{:S(2)}) collective-permute-start(bf16[4096,128]{1,0:T(8,128)(2,1)} %bitcast.9.refs_3_), channel_id=1, source_target_pairs={{0,16},{16,32},{32,48},{48,0},{1,17},{17,33},{33,49},{49,1},{2,18}... | collective-permute-start | bytes 3145736 | tf_op jit(solution)/shard_map/ppermute | solution.py:21
  49.4 15.7 %collective-permute-done.2.refs_4_ = bf16[4096,128]{1,0:T(8,128)(2,1)} collective-permute-done((bf16[4096,128]{1,0:T(8,128)(2,1)}, bf16[4096,128]{1,0:T(8,128)(2,1)}, u32[]{:S(2)}, u32[]{:S(2)}) %collective-permute-start.2) | collective-permute-done | bytes 1048608 | tf_op jit(solution)/shard_map/ppermute | solution.py:21
  65.1 1.9 collective-permute-start.5
  67.0 5.1 %collective-permute-start.4 = (bf16[4112,128]{1,0:T(8,128)(2,1)}, bf16[4112,128]{1,0:T(8,128)(2,1)S(1)}, u32[]{:S(2)}, u32[]{:S(2)}) collective-permute-start(bf16[4112,128]{1,0:T(8,128)(2,1)} %collective-permute-done.1.refs_2_), channel_id=1, source_target_pairs={{0,16},{16,32},{32,48},{48,0},{1,17},{17,33},{33,49},{49,1},{2,18}... | collective-permute-start | bytes 3158024 | tf_op jit(solution)/shard_map/ppermute | solution.py:21
  72.2 0.8 copy-done.1
  73.0 0.7 slice.62
  73.8 0.7 slice_bitcast_fusion.1
  75.6 27.9 %shard_map.82 = (f32[8,1024,128]{2,1,0:T(8,128)}, f32[8,1024,128]{2,1,0:T(8,128)}) custom-call(s32[128]{0:T(128)S(1)} %reshape.438.slot_ref, bf16[8,144,1024]{2,1,0:T(8,128)(2,1)} %all-gather.4.cloned.1.call-done.q_ref, f32[8,16,128]{2,1,0:T(8,128)S(1)} %pad_maximum_fusion.1.cos_ref, f32[8,16,128]{2,1,0:T(8,128)S(1)} %pad_maximum_fusion.2.sin_ref, ...), custom_call_target="tpu_custom_call" | custom-call | flops 3221225472 | bytes 50331648 | tf_op jit(solution)/shard_map/pallas_call | solution.py:178
  104.0 0.3 fusion.20
  104.5 10.7 %shard_map.83 = (bf16[2,8,8,64,128]{4,3,2,1,0:T(8,128)(2,1)S(1)}, f32[8,8,128]{2,1,0:T(8,128)S(1)}) custom-call(s32[128]{0:T(128)S(1)} %reshape.437.slot_ref, bf16[8,144,1024]{2,1,0:T(8,128)(2,1)} %all-gather.4.cloned.1.call-done.q_ref, f32[8,16,128]{2,1,0:T(8,128)S(1)} %pad_maximum_fusion.3.cos_ref, f32[8,16,128]{2,1,0:T(8,128)S(1)} %pad_maximum_fusion.4.sin_ref, ...), custom_call_target="tpu_custom_call" | custom-call | flops 1073741824 | bytes 16777216 | tf_op jit(solution)/shard_map/pallas_call | solution.py:178
  115.4 1.9 collective-permute-start.7
  117.5 2.4 %collective-permute-start.6 = (bf16[8,8,64,128]{3,2,1,0:T(8,128)(2,1)S(1)}, bf16[8,8,64,128]{3,2,1,0:T(8,128)(2,1)S(1)}, u32[]{:S(2)}, u32[]{:S(2)}) collective-permute-start(bf16[8,8,64,128]{3,2,1,0:T(8,128)(2,1)S(1)} %get-tuple-element.42), channel_id=1, source_target_pairs={{0,8},{8,0},{1,9},{9,1},{2,10},{10,2},{3,11},{11,3},{4,12},{12,4},... | collective-permute-start | bytes 3145736 | tf_op jit(solution)/shard_map/ppermute | solution.py:325
  119.9 0.5 constant_dynamic-slice_fusion
  120.4 0.7 add_compare_fusion
  121.3 0.9 collective-permute-done.6
  122.2 1.5 multiply_reduce_fusion
  123.8 43.6 %all_to_all.15 = bf16[64,72,128]{2,1,0:T(8,128)(2,1)S(1)} all-to-all(bf16[64,72,128]{2,1,0:T(8,128)(2,1)S(1)} %fusion.2), channel_id=1, replica_groups=mesh['lib_0'=8,'lib_1'=4,'ctx'=2,'head'=8] {'lib_0','head'}, dimensions={0} | all-to-all | bytes 2359296 | tf_op jit(solution)/shard_map/all_to_all | solution.py:338
  167.5 0.7 multiply_reduce_fusion.1
  168.3 13.4 %all_gather.11.rows_ref = bf16[4,8,64,128]{3,2,1,0:T(8,128)(2,1)S(1)} all-gather(bf16[1,8,64,128]{3,2,1,0:T(8,128)(2,1)S(1)} %fusion.4), channel_id=1, replica_groups=mesh['lib_0'=8,'lib_1'=4,'ctx'=2,'head'=8] {'lib_1'}, dimensions={0}, use_global_device_ids=true | all-gather | bytes 655360 | tf_op jit(solution)/shard_map/all_gather | solution.py:345
  181.8 2.2 copy-done
  184.0 2.8 %shard_map.84 = bf16[8,256,256]{2,1,0:T(8,128)(2,1)S(1)} custom-call(bf16[4,8,64,128]{3,2,1,0:T(8,128)(2,1)S(1)} %all_gather.11.rows_ref, bf16[8,8,128,256]{3,2,1,0:T(8,128)(2,1)S(1)} %bitcast.63), custom_call_target="tpu_custom_call" | custom-call | tf_op jit(solution)/shard_map/pallas_call | solution.py:223
  186.8 30.7 %all_to_all.16 = bf16[8,256,256]{2,1,0:T(8,128)(2,1)S(1)} all-to-all(bf16[8,256,256]{2,1,0:T(8,128)(2,1)S(1)} %shard_map.84), channel_id=1, replica_groups=mesh['lib_0'=8,'lib_1'=4,'ctx'=2,'head'=8] {'lib_0'}, dimensions={0} | all-to-all | bytes 2097152 | tf_op jit(solution)/shard_map/all_to_all | solution.py:347
  217.4 0.8 reduce_sum.85
  (58 shorter events, 2.7 us)
Async XLA Ops:
  6.5 66.5 %all-gather.4.cloned.1.call-start = ((), (), s32[]{:S(2)}) async-start(), calls=%async_computation.3 | async-start | bytes 2654208 | tf_op jit(solution)/shard_map/all_gather | solution.py:285
  11.7 27.0 %collective-permute-start.1 = (bf16[4112,128]{1,0:T(8,128)(2,1)S(1)}, bf16[4112,128]{1,0:T(8,128)(2,1)}, u32[]{:S(2)}, u32[]{:S(2)}) collective-permute-start(bf16[4112,128]{1,0:T(8,128)(2,1)S(1)} %fusion.3.refs_0_), channel_id=1, source_target_pairs={{0,16},{16,32},{32,48},{48,0},{1,17},{17,33},{33,49},{49,1},{2,18}... | collective-permute-start | bytes 3158024 | tf_op jit(solution)/shard_map/ppermute | solution.py:21
  19.4 54.3 %collective-permute-start = (bf16[4112,128]{1,0:T(8,128)(2,1)S(1)}, bf16[4112,128]{1,0:T(8,128)(2,1)}, u32[]{:S(2)}, u32[]{:S(2)}) collective-permute-start(bf16[4112,128]{1,0:T(8,128)(2,1)S(1)} %fusion.3.refs_0_), channel_id=1, source_target_pairs={{0,48},{16,0},{32,16},{48,32},{1,49},{17,1},{33,17},{49,33},{2,50}... | collective-permute-start | bytes 3158024 | tf_op jit(solution)/shard_map/ppermute | solution.py:21
  21.4 43.8 %collective-permute-start.2 = (bf16[4096,128]{1,0:T(8,128)(2,1)}, bf16[4096,128]{1,0:T(8,128)(2,1)}, u32[]{:S(2)}, u32[]{:S(2)}) collective-permute-start(bf16[4096,128]{1,0:T(8,128)(2,1)} %bitcast.9.refs_3_), channel_id=1, source_target_pairs={{0,48},{16,0},{32,16},{48,32},{1,49},{17,1},{33,17},{49,33},{2,50}... | collective-permute-start | bytes 3145736 | tf_op jit(solution)/shard_map/ppermute | solution.py:21
  38.6 33.5 %all-to-all-start.1 = ((bf16[8,128,256]{2,1,0:T(8,128)(2,1)}), bf16[8,128,256]{2,1,0:T(8,128)(2,1)S(1)}, u32[]{:S(2)}, u32[]{:S(2)}) async-start(bf16[8,128,256]{2,1,0:T(8,128)(2,1)} %bitcast.25), calls=%async_computation.1 | async-start | bytes 1048576 | tf_op jit(solution)/shard_map/all_to_all | solution.py:291
  45.8 121.6 %all-gather.6.cloned.1.call-start = ((), (), s32[]{:S(2)}) async-start(), calls=%async_computation.4 | async-start | bytes 4718592 | tf_op jit(solution)/shard_map/all_gather | solution.py:292
  45.8 29.8 %collective-permute-start.3 = (bf16[4096,128]{1,0:T(8,128)(2,1)}, bf16[4096,128]{1,0:T(8,128)(2,1)}, u32[]{:S(2)}, u32[]{:S(2)}) collective-permute-start(bf16[4096,128]{1,0:T(8,128)(2,1)} %bitcast.9.refs_3_), channel_id=1, source_target_pairs={{0,16},{16,32},{32,48},{48,0},{1,17},{17,33},{33,49},{49,1},{2,18}... | collective-permute-start | bytes 3145736 | tf_op jit(solution)/shard_map/ppermute | solution.py:21
  65.1 39.4 %collective-permute-start.5 = (bf16[4096,128]{1,0:T(8,128)(2,1)}, bf16[4096,128]{1,0:T(8,128)(2,1)}, u32[]{:S(2)}, u32[]{:S(2)}) collective-permute-start(bf16[4096,128]{1,0:T(8,128)(2,1)} %collective-permute-done.2.refs_4_), channel_id=1, source_target_pairs={{0,48},{16,0},{32,16},{48,32},{1,49},{17,1},{33,17},{49,33},{2,50}... | collective-permute-start | bytes 3145736 | tf_op jit(solution)/shard_map/ppermute | solution.py:21
  67.0 36.4 %collective-permute-start.4 = (bf16[4112,128]{1,0:T(8,128)(2,1)}, bf16[4112,128]{1,0:T(8,128)(2,1)S(1)}, u32[]{:S(2)}, u32[]{:S(2)}) collective-permute-start(bf16[4112,128]{1,0:T(8,128)(2,1)} %collective-permute-done.1.refs_2_), channel_id=1, source_target_pairs={{0,16},{16,32},{32,48},{48,0},{1,17},{17,33},{33,49},{49,1},{2,18}... | collective-permute-start | bytes 3158024 | tf_op jit(solution)/shard_map/ppermute | solution.py:21
  72.2 0.8 copy-start.1
  115.4 5.7 %collective-permute-start.7 = (f32[8,8,64]{2,1,0:T(8,128)S(1)}, f32[8,8,64]{2,1,0:T(8,128)S(1)}, u32[]{:S(2)}, u32[]{:S(2)}) collective-permute-start(f32[8,8,64]{2,1,0:T(8,128)S(1)} %bitcast.73), channel_id=1, source_target_pairs={{0,8},{8,0},{1,9},{9,1},{2,10},{10,2},{3,11},{11,3},{4,12},{12,4},... | collective-permute-start | bytes 49160 | tf_op jit(solution)/shard_map/ppermute | solution.py:326
  117.5 4.7 %collective-permute-start.6 = (bf16[8,8,64,128]{3,2,1,0:T(8,128)(2,1)S(1)}, bf16[8,8,64,128]{3,2,1,0:T(8,128)(2,1)S(1)}, u32[]{:S(2)}, u32[]{:S(2)}) collective-permute-start(bf16[8,8,64,128]{3,2,1,0:T(8,128)(2,1)S(1)} %get-tuple-element.42), channel_id=1, source_target_pairs={{0,8},{8,0},{1,9},{9,1},{2,10},{10,2},{3,11},{11,3},{4,12},{12,4},... | collective-permute-start | bytes 3145736 | tf_op jit(solution)/shard_map/ppermute | solution.py:325
  181.8 2.2 copy-start
Sparse Core Ops, SparseCore 0:
  9.8 57.9 all-gather.3
  73.1 61.8 all-gather.5

commit v7 on v6

--- a/solution.py
+++ b/solution.py
@@ -32,8 +32,10 @@
 def attend_kernel(scale, pieces, first, last, slot_ref, q_ref, cos_ref, sin_ref, *refs):
     key_refs, value_refs, refs = refs[:pieces], refs[pieces : 2 * pieces], refs[2 * pieces :]
     if not first:
-        (before_ref, before_lse_ref), refs = refs[:2], refs[2:]
+        (before_ref, before_top_ref), refs = refs[:2], refs[2:]
     out_ref, lse_ref, q_scr, tile, k_scr, v_scr, s_scr, m_scr, acc_scr, used, entry = refs
+    if not last:
+        acc_scr, m_scr = out_ref.at[0], lse_ref.at[0]
     prompt = pl.program_id(0)
     listed, width = cos_ref.shape[1:]
     rows = q_ref.shape[1]
@@ -54,7 +56,7 @@
         if first:
             m_scr[span] = jnp.full((CHUNK, width), EMPTY, jnp.float32)
         else:
-            m_scr[span] = before_lse_ref[0, span] * (1.0 / scale)
+            m_scr[span] = before_top_ref[0, span]
 
     def note(k, count):
         slot = slot_ref[prompt * listed + k]
@@ -112,9 +114,9 @@
         if first:
             acc_scr[span] = jnp.zeros((CHUNK, 2 * width), jnp.float32)
         else:
-            weight = jnp.exp2((before_lse_ref[0, span] * (1.0 / scale) - m) * factor)
-            acc_scr[span, :width] = before_ref[0, span] * weight
-            acc_scr[span, width:] = weight
+            weight = jnp.exp2((before_top_ref[0, span] - m) * factor)
+            for u in (0, width):
+                acc_scr[span, u : u + width] = before_ref[0, span, u : u + width] * weight
 
     def weigh(t, carry):
         for b in range(2):
@@ -131,26 +133,27 @@
         return carry
 
     lax.fori_loop(0, pairs, weigh, 0)
+    if not last:
+        return
+    halves = out_ref.shape[0]
+    part = rows // halves
     row = lax.broadcasted_iota(jnp.int32, (rows, rows), 0)
     column = lax.broadcasted_iota(jnp.int32, (rows, rows), 1)
+
+    def line(value):
+        return jnp.sum(jnp.where(row == column, value, 0.0), axis=0, keepdims=True)
+
+    tops, totals = [], []
     for g in range(group):
         span = slice(g * rows, (g + 1) * rows)
-        total = acc_scr[span, width:]
-        if first:
-            total = jnp.where(count == 0, 1.0, total)
-        out = acc_scr[span, :width] / total
-        lse = m_scr[span] * scale + jnp.log(total)
-        if last:
-            halves = out_ref.shape[0]
-            part = rows // halves
-            for c in range(halves):
-                out_ref[c, g, 0] = out[c * part : (c + 1) * part].astype(out_ref.dtype)
-            lse_ref[0, g : g + 1, :] = jnp.sum(
-                jnp.where(row == column, lse, 0.0), axis=0, keepdims=True
-            )
-        else:
-            out_ref[0, span] = out
-            lse_ref[0, span] = lse
+        total = jnp.maximum(acc_scr[span, width:], 1.0)
+        out = (acc_scr[span, :width] / total).astype(out_ref.dtype)
+        for c in range(halves):
+            out_ref[c, g, 0] = out[c * part : (c + 1) * part]
+        tops.append(line(m_scr[span]))
+        totals.append(line(total))
+    tops, totals = jnp.concatenate(tops, axis=0), jnp.concatenate(totals, axis=0)
+    lse_ref[0] = tops * scale + jnp.log(totals)
 
 
 def attend(slots, query, cosine, sine, keys, values, before, halves, rows, tokens):
@@ -160,7 +163,9 @@
     most = MOST * len(keys)
     whole = pl.BlockSpec(memory_space=pltpu.VMEM)
     table = pl.BlockSpec((1, listed, width), lambda j, s: (j, 0, 0))
-    state = pl.BlockSpec((1, rows * group, width), lambda j, s: (j, 0, 0))
+    state = [
+        pl.BlockSpec((1, rows * group, w * width), lambda j, s: (j, 0, 0)) for w in (2, 1)
+    ]
     if halves:
         part = rows // halves
         out = (
@@ -172,8 +177,10 @@
             pl.BlockSpec((1, group, rows), lambda j, s: (j, 0, 0)),
         )
     else:
-        out = (jax.ShapeDtypeStruct((prompts, rows * group, width), jnp.float32),) * 2
-        out_specs = (state, state)
+        out = tuple(
+            jax.ShapeDtypeStruct((prompts, rows * group, w * width), jnp.float32) for w in (2, 1)
+        )
+        out_specs = tuple(state)
     work = prompts * most // 2 * rows * group * tokens
     return pl.pallas_call(
         functools.partial(attend_kernel, width**-0.5, len(keys), before is None, bool(halves)),
@@ -183,7 +190,7 @@
             grid=(prompts,),
             in_specs=[pl.BlockSpec((1, rows, features), lambda j, s: (j, 0, 0)), table, table]
             + [whole] * (2 * len(keys))
-            + ([state, state] if before else []),
+            + (state if before else []),
             out_specs=out_specs,
             scratch_shapes=[
                 pltpu.VMEM((rows * group, width), jnp.bfloat16),
@@ -275,8 +282,10 @@
     own_values = passage_values.reshape(-1, width)
     keys = [own_keys, shift(own_keys, COL, -1), None, shift(own_keys, COL, 1)]
     values = [own_values, shift(own_values, COL, -1), None, shift(own_values, COL, 1)]
-    keys[2] = shift(keys[3], COL, 1)
-    values[2] = shift(values[1], COL, -1)
+    second = lax.optimization_barrier((keys[3], values[3]))[0]
+    keys[2] = shift(second, COL, 1)
+    second = lax.optimization_barrier((values[1], keys[1]))[0]
+    values[2] = shift(second, COL, -1)
 
     asked = jnp.concatenate([passage_list[0], targets[0], row_counts])
     asked = jnp.stack(coded(asked))

time: 226 us -> 227 us (level)
  blocking collectives: 87.7 us -> 100 us
  Pallas kernels: 41.4 us -> 33 us
  starting transfers between devices: 33.7 us -> 31.1 us
  waiting for transfers between devices: 32 us -> 29.7 us
    all_to_all x1, blocking collectives: 43.6 us -> 56.2 us  [body(): lax.all_to_all(sent, (ROW, 'head'), split_axis=0, concat_axis=0, tiled=True)]
    pallas_call x2, Pallas kernels: 38.6 us -> 30.2 us  [attend(): pl.pallas_call(functools.partial(attend_kernel, width ** (-0.5), len(keys...]
    all_to_all x1, starting transfers between devices: 7.1 us -> 4.16 us  [body(): lax.all_to_all(weight, ROW, split_axis=0, concat_axis=0, tiled=True)]
    ppermute x6, waiting for transfers between devices: 31 us -> 28.3 us  [shift(): return lax.ppermute(value, axis, [(i, (i + by) % n) for i in range(n)])]
  transfers between devices with their start and end apart: 11 -> 11, of which waited for: 3 -> 4; matrix products, arithmetic and copies ran while one was open for 4% -> 4% of each run, Pallas kernels for 17% -> 13%
where the time goes in v7:
time: 227 us; the launch traced here: 226 us
  blocking collectives  100 us (44%)
  Pallas kernels  33 us (15%)
  starting transfers between devices  31.1 us (14%)
  waiting for transfers between devices  29.7 us (13%)
  between operations  14.4 us (6%)
  other arithmetic  10.3 us (5%)
  local copies, waits for them, and re-layouts  7.13 us (3%)
    all_to_all x1, blocking collectives, body(): lax.all_to_all(sent, (ROW, 'head'), split_axis=0, concat_axis=0, tiled=True)  56.2 us
    all_to_all x1, blocking collectives, body(): terms = lax.all_to_all(terms, ROW, split_axis=0, concat_axis=0, tiled=True)  31.1 us
    pallas_call x2, Pallas kernels, attend(): pl.pallas_call(functools.partial(attend_kernel, width ** (-0.5), len(keys...  30.2 us
    ppermute x6, waiting for transfers between devices, shift(): return lax.ppermute(value, axis, [(i, (i + by) % n) for i in range(n)])  28.3 us
    ppermute x6, starting transfers between devices, shift(): return lax.ppermute(value, axis, [(i, (i + by) % n) for i in range(n)])  22.6 us
    all_gather x1, blocking collectives, body(): rows_in = lax.all_gather(attended[None], COL, axis=0, tiled=True)  12.8 us
  transfers between devices with their start and end apart: 11, of which 4 were waited for; matrix products, arithmetic and copies ran while one was open for 4% of the time, Pallas kernels for 13%

profile of v7, /device:TPU:6, one launch (start us, length us, event | category | flops | bytes accessed | tf_op | source)
XLA Modules:
  0.0 225.7 jit_solution(16905606753652959901)
XLA Ops:
  7.2 0.8 fusion.30
  8.0 1.7 pad_maximum_fusion
  9.7 0.7 convert_bitcast_fusion
  10.4 1.3 fusion.3.refs_0_
  11.7 7.8 %collective-permute-start.1 = (bf16[4112,128]{1,0:T(8,128)(2,1)S(1)}, bf16[4112,128]{1,0:T(8,128)(2,1)}, u32[]{:S(2)}, u32[]{:S(2)}) collective-permute-start(bf16[4112,128]{1,0:T(8,128)(2,1)S(1)} %fusion.3.refs_0_), channel_id=1, source_target_pairs={{0,16},{16,32},{32,48},{48,0},{1,17},{17,33},{33,49},{49,1},{2,18}... | collective-permute-start | bytes 3158024 | tf_op jit(solution)/shard_map/ppermute | solution.py:21
  19.4 1.9 collective-permute-start
  21.4 5.1 %collective-permute-start.3 = (bf16[4096,128]{1,0:T(8,128)(2,1)}, bf16[4096,128]{1,0:T(8,128)(2,1)S(1)}, u32[]{:S(2)}, u32[]{:S(2)}) collective-permute-start(bf16[4096,128]{1,0:T(8,128)(2,1)} %bitcast.9.refs_3_), channel_id=1, source_target_pairs={{0,16},{16,32},{32,48},{48,0},{1,17},{17,33},{33,49},{49,1},{2,18}... | collective-permute-start | bytes 3145736 | tf_op jit(solution)/shard_map/ppermute | solution.py:21
  26.5 1.9 collective-permute-start.2
  28.4 14.7 %collective-permute-done.1.refs_2_ = bf16[4112,128]{1,0:T(8,128)(2,1)} collective-permute-done((bf16[4112,128]{1,0:T(8,128)(2,1)S(1)}, bf16[4112,128]{1,0:T(8,128)(2,1)}, u32[]{:S(2)}, u32[]{:S(2)}) %collective-permute-start.1) | collective-permute-done | bytes 1052704 | tf_op jit(solution)/shard_map/ppermute | solution.py:21
  43.1 4.2 %all-to-all-start.1 = ((bf16[8,128,256]{2,1,0:T(8,128)(2,1)}), bf16[8,128,256]{2,1,0:T(8,128)(2,1)}, u32[]{:S(2)}, u32[]{:S(2)}) async-start(bf16[8,128,256]{2,1,0:T(8,128)(2,1)} %bitcast.25), calls=%async_computation.1 | async-start | bytes 1048576 | tf_op jit(solution)/shard_map/all_to_all | solution.py:300
  47.4 13.6 %collective-permute-done.3.refs_5_ = bf16[4096,128]{1,0:T(8,128)(2,1)S(1)} collective-permute-done((bf16[4096,128]{1,0:T(8,128)(2,1)}, bf16[4096,128]{1,0:T(8,128)(2,1)S(1)}, u32[]{:S(2)}, u32[]{:S(2)}) %collective-permute-start.3) | collective-permute-done | bytes 1048608 | tf_op jit(solution)/shard_map/ppermute | solution.py:21
  61.0 1.0 copy-done.1
  62.1 3.4 %collective-permute-start.4 = (bf16[4112,128]{1,0:T(8,128)(2,1)}, bf16[4112,128]{1,0:T(8,128)(2,1)S(1)}, u32[]{:S(2)}, u32[]{:S(2)}) collective-permute-start(bf16[4112,128]{1,0:T(8,128)(2,1)} %collective-permute-done.1.refs_2_), channel_id=1, source_target_pairs={{0,16},{16,32},{32,48},{48,0},{1,17},{17,33},{33,49},{49,1},{2,18}... | collective-permute-start | bytes 3158024 | tf_op jit(solution)/shard_map/ppermute | solution.py:21
  65.5 2.4 %collective-permute-start.5 = (bf16[4096,128]{1,0:T(8,128)(2,1)}, bf16[4096,128]{1,0:T(8,128)(2,1)}, u32[]{:S(2)}, u32[]{:S(2)}) collective-permute-start(bf16[4096,128]{1,0:T(8,128)(2,1)} %collective-permute-done.2.refs_4_), channel_id=1, source_target_pairs={{0,48},{16,0},{32,16},{48,32},{1,49},{17,1},{33,17},{49,33},{2,50}... | collective-permute-start | bytes 3145736 | tf_op jit(solution)/shard_map/ppermute | solution.py:21
  68.4 0.7 slice.62
  69.1 0.7 slice_bitcast_fusion.1
  70.9 1.2 copy-done.2
  72.1 19.6 %shard_map.82 = (f32[8,1024,256]{2,1,0:T(8,128)}, f32[8,1024,128]{2,1,0:T(8,128)}) custom-call(s32[128]{0:T(128)S(1)} %reshape.438.slot_ref, bf16[8,144,1024]{2,1,0:T(8,128)(2,1)} %all-gather.4.cloned.1.call-done.q_ref, f32[8,16,128]{2,1,0:T(8,128)S(1)} %pad_maximum_fusion.1.cos_ref, f32[8,16,128]{2,1,0:T(8,128)S(1)} %pad_maximum_fusion.2.sin_ref, ...), custom_call_target="tpu_custom_call" | custom-call | flops 3221225472 | bytes 50331648 | tf_op jit(solution)/shard_map/pallas_call | solution.py:185
  92.8 10.6 %shard_map.83 = (bf16[2,8,8,64,128]{4,3,2,1,0:T(8,128)(2,1)S(1)}, f32[8,8,128]{2,1,0:T(8,128)S(1)}) custom-call(s32[128]{0:T(128)S(1)} %reshape.437.slot_ref, bf16[8,144,1024]{2,1,0:T(8,128)(2,1)} %all-gather.4.cloned.1.call-done.q_ref, f32[8,16,128]{2,1,0:T(8,128)S(1)} %pad_maximum_fusion.3.cos_ref, f32[8,16,128]{2,1,0:T(8,128)S(1)} %pad_maximum_fusion.4.sin_ref, ...), custom_call_target="tpu_custom_call" | custom-call | flops 1073741824 | bytes 16777216 | tf_op jit(solution)/shard_map/pallas_call | solution.py:185
  103.6 1.9 collective-permute-start.7
  105.7 2.4 %collective-permute-start.6 = (bf16[8,8,64,128]{3,2,1,0:T(8,128)(2,1)S(1)}, bf16[8,8,64,128]{3,2,1,0:T(8,128)(2,1)S(1)}, u32[]{:S(2)}, u32[]{:S(2)}) collective-permute-start(bf16[8,8,64,128]{3,2,1,0:T(8,128)(2,1)S(1)} %get-tuple-element.46), channel_id=1, source_target_pairs={{0,8},{8,0},{1,9},{9,1},{2,10},{10,2},{3,11},{11,3},{4,12},{12,4},... | collective-permute-start | bytes 3145736 | tf_op jit(solution)/shard_map/ppermute | solution.py:334
  108.1 0.5 constant_dynamic-slice_fusion
  108.6 0.7 add_compare_fusion
  109.5 0.9 collective-permute-done.6
  110.4 1.5 multiply_reduce_fusion
  112.0 56.2 %all_to_all.15 = bf16[64,72,128]{2,1,0:T(8,128)(2,1)S(1)} all-to-all(bf16[64,72,128]{2,1,0:T(8,128)(2,1)S(1)} %fusion.2), channel_id=1, replica_groups=mesh['lib_0'=8,'lib_1'=4,'ctx'=2,'head'=8] {'lib_0','head'}, dimensions={0} | all-to-all | bytes 2359296 | tf_op jit(solution)/shard_map/all_to_all | solution.py:347
  168.3 0.7 multiply_reduce_fusion.1
  169.2 12.8 %all_gather.11.rows_ref = bf16[4,8,64,128]{3,2,1,0:T(8,128)(2,1)S(1)} all-gather(bf16[1,8,64,128]{3,2,1,0:T(8,128)(2,1)S(1)} %fusion.4), channel_id=1, replica_groups=mesh['lib_0'=8,'lib_1'=4,'ctx'=2,'head'=8] {'lib_1'}, dimensions={0}, use_global_device_ids=true | all-gather | bytes 655360 | tf_op jit(solution)/shard_map/all_gather | solution.py:354
  182.0 2.2 copy-done
  184.1 2.8 %shard_map.84 = bf16[8,256,256]{2,1,0:T(8,128)(2,1)S(1)} custom-call(bf16[4,8,64,128]{3,2,1,0:T(8,128)(2,1)S(1)} %all_gather.11.rows_ref, bf16[8,8,128,256]{3,2,1,0:T(8,128)(2,1)S(1)} %bitcast.63), custom_call_target="tpu_custom_call" | custom-call | tf_op jit(solution)/shard_map/pallas_call | solution.py:230
  186.9 31.1 %all_to_all.16 = bf16[8,256,256]{2,1,0:T(8,128)(2,1)S(1)} all-to-all(bf16[8,256,256]{2,1,0:T(8,128)(2,1)S(1)} %shard_map.84), channel_id=1, replica_groups=mesh['lib_0'=8,'lib_1'=4,'ctx'=2,'head'=8] {'lib_0'}, dimensions={0} | all-to-all | bytes 2097152 | tf_op jit(solution)/shard_map/all_to_all | solution.py:356
  218.1 0.8 reduce_sum.85
  (60 shorter events, 3.5 us)
Async XLA Ops:
  6.5 61.8 %all-gather.4.cloned.1.call-start = ((), (), s32[]{:S(2)}) async-start(), calls=%async_computation.3 | async-start | bytes 2654208 | tf_op jit(solution)/shard_map/all_gather | solution.py:294
  11.7 31.5 %collective-permute-start.1 = (bf16[4112,128]{1,0:T(8,128)(2,1)S(1)}, bf16[4112,128]{1,0:T(8,128)(2,1)}, u32[]{:S(2)}, u32[]{:S(2)}) collective-permute-start(bf16[4112,128]{1,0:T(8,128)(2,1)S(1)} %fusion.3.refs_0_), channel_id=1, source_target_pairs={{0,16},{16,32},{32,48},{48,0},{1,17},{17,33},{33,49},{49,1},{2,18}... | collective-permute-start | bytes 3158024 | tf_op jit(solution)/shard_map/ppermute | solution.py:21
  19.4 46.0 %collective-permute-start = (bf16[4112,128]{1,0:T(8,128)(2,1)S(1)}, bf16[4112,128]{1,0:T(8,128)(2,1)}, u32[]{:S(2)}, u32[]{:S(2)}) collective-permute-start(bf16[4112,128]{1,0:T(8,128)(2,1)S(1)} %fusion.3.refs_0_), channel_id=1, source_target_pairs={{0,48},{16,0},{32,16},{48,32},{1,49},{17,1},{33,17},{49,33},{2,50}... | collective-permute-start | bytes 3158024 | tf_op jit(solution)/shard_map/ppermute | solution.py:21
  21.4 39.7 %collective-permute-start.3 = (bf16[4096,128]{1,0:T(8,128)(2,1)}, bf16[4096,128]{1,0:T(8,128)(2,1)S(1)}, u32[]{:S(2)}, u32[]{:S(2)}) collective-permute-start(bf16[4096,128]{1,0:T(8,128)(2,1)} %bitcast.9.refs_3_), channel_id=1, source_target_pairs={{0,16},{16,32},{32,48},{48,0},{1,17},{17,33},{33,49},{49,1},{2,18}... | collective-permute-start | bytes 3145736 | tf_op jit(solution)/shard_map/ppermute | solution.py:21
  26.5 39.0 %collective-permute-start.2 = (bf16[4096,128]{1,0:T(8,128)(2,1)}, bf16[4096,128]{1,0:T(8,128)(2,1)}, u32[]{:S(2)}, u32[]{:S(2)}) collective-permute-start(bf16[4096,128]{1,0:T(8,128)(2,1)} %bitcast.9.refs_3_), channel_id=1, source_target_pairs={{0,48},{16,0},{32,16},{48,32},{1,49},{17,1},{33,17},{49,33},{2,50}... | collective-permute-start | bytes 3145736 | tf_op jit(solution)/shard_map/ppermute | solution.py:21
  43.1 25.2 %all-to-all-start.1 = ((bf16[8,128,256]{2,1,0:T(8,128)(2,1)}), bf16[8,128,256]{2,1,0:T(8,128)(2,1)}, u32[]{:S(2)}, u32[]{:S(2)}) async-start(bf16[8,128,256]{2,1,0:T(8,128)(2,1)} %bitcast.25), calls=%async_computation.1 | async-start | bytes 1048576 | tf_op jit(solution)/shard_map/all_to_all | solution.py:300
  47.3 120.9 %all-gather.6.cloned.1.call-start = ((), (), s32[]{:S(2)}) async-start(), calls=%async_computation.4 | async-start | bytes 4718592 | tf_op jit(solution)/shard_map/all_gather | solution.py:301
  61.0 1.0 copy-start.1
  62.1 29.7 %collective-permute-start.4 = (bf16[4112,128]{1,0:T(8,128)(2,1)}, bf16[4112,128]{1,0:T(8,128)(2,1)S(1)}, u32[]{:S(2)}, u32[]{:S(2)}) collective-permute-start(bf16[4112,128]{1,0:T(8,128)(2,1)} %collective-permute-done.1.refs_2_), channel_id=1, source_target_pairs={{0,16},{16,32},{32,48},{48,0},{1,17},{17,33},{33,49},{49,1},{2,18}... | collective-permute-start | bytes 3158024 | tf_op jit(solution)/shard_map/ppermute | solution.py:21
  65.5 27.3 %collective-permute-start.5 = (bf16[4096,128]{1,0:T(8,128)(2,1)}, bf16[4096,128]{1,0:T(8,128)(2,1)}, u32[]{:S(2)}, u32[]{:S(2)}) collective-permute-start(bf16[4096,128]{1,0:T(8,128)(2,1)} %collective-permute-done.2.refs_4_), channel_id=1, source_target_pairs={{0,48},{16,0},{32,16},{48,32},{1,49},{17,1},{33,17},{49,33},{2,50}... | collective-permute-start | bytes 3145736 | tf_op jit(solution)/shard_map/ppermute | solution.py:21
  70.9 1.2 copy-start.2
  103.6 5.7 %collective-permute-start.7 = (f32[8,8,64]{2,1,0:T(8,128)S(1)}, f32[8,8,64]{2,1,0:T(8,128)S(1)}, u32[]{:S(2)}, u32[]{:S(2)}) collective-permute-start(f32[8,8,64]{2,1,0:T(8,128)S(1)} %bitcast.73), channel_id=1, source_target_pairs={{0,8},{8,0},{1,9},{9,1},{2,10},{10,2},{3,11},{11,3},{4,12},{12,4},... | collective-permute-start | bytes 49160 | tf_op jit(solution)/shard_map/ppermute | solution.py:335
  105.7 4.7 %collective-permute-start.6 = (bf16[8,8,64,128]{3,2,1,0:T(8,128)(2,1)S(1)}, bf16[8,8,64,128]{3,2,1,0:T(8,128)(2,1)S(1)}, u32[]{:S(2)}, u32[]{:S(2)}) collective-permute-start(bf16[8,8,64,128]{3,2,1,0:T(8,128)(2,1)S(1)} %get-tuple-element.46), channel_id=1, source_target_pairs={{0,8},{8,0},{1,9},{9,1},{2,10},{10,2},{3,11},{11,3},{4,12},{12,4},... | collective-permute-start | bytes 3145736 | tf_op jit(solution)/shard_map/ppermute | solution.py:334
  182.0 2.2 copy-start
Sparse Core Ops, SparseCore 0:
  9.8 57.5 all-gather.3
  69.5 61.3 all-gather.5

commit v8 on v7

--- a/solution.py
+++ b/solution.py
@@ -287,20 +287,16 @@
     second = lax.optimization_barrier((values[1], keys[1]))[0]
     values[2] = shift(second, COL, -1)
 
-    asked = jnp.concatenate([passage_list[0], targets[0], row_counts])
-    asked = jnp.stack(coded(asked))
-    padded = jnp.pad(asked, ((0, 14), (0, features - asked.shape[1])))
-    query = jnp.concatenate([queries, padded[None]], axis=1)
-    query = lax.all_gather(query, ROW, axis=0, tiled=True)
-    asked = query[:, prompt_rows : prompt_rows + 2, : asked.shape[1]]
-    asked, keys[1], near_keys = lax.optimization_barrier((asked, keys[1], keys[3]))
-    asked = decoded(asked[:, 0], asked[:, 1])
-    weight, _ = lax.optimization_barrier((out_weight, keys[3]))
-    weight = weight.reshape(group, width, -1)
+    query = lax.all_gather(queries, ROW, axis=0, tiled=True)
+    asked = jnp.stack(coded(jnp.concatenate([passage_list[0], targets[0], row_counts])))
+    entries = asked.shape[1]
+    asked = jnp.pad(asked, ((0, 14), (0, out_weight.shape[1] - entries)))
+    asked = jnp.broadcast_to(asked, (rows_of, *asked.shape))
+    weight = jnp.concatenate([out_weight.reshape(group, width, -1), asked], axis=1)
     weight = lax.all_to_all(weight, ROW, split_axis=0, concat_axis=0, tiled=True)
-    weight = lax.all_gather(weight[None], "head", axis=0, tiled=True)
-
-    keys[3] = near_keys
+    asked = decoded(weight[:, width, :entries], weight[:, width + 1, :entries])
+    weight = lax.all_gather(weight[None, :, :width], "head", axis=0, tiled=True)
+
     local = asked[:, :listed] - y * columns * held
     mine = (local >= 0) & (local < columns * held)
     ahead = (local // held - x) % columns

time: 227 us -> 234 us (1.031)
  waiting for transfers between devices: 29.7 us -> 48.5 us
  Pallas kernels: 33 us -> 24.8 us
    ppermute x6, waiting for transfers between devices: 28.3 us -> 38 us  [shift(): return lax.ppermute(value, axis, [(i, (i + by) % n) for i in range(n)])]
    pallas_call x2, Pallas kernels: 30.2 us -> 22 us  [attend(): pl.pallas_call(functools.partial(attend_kernel, width ** (-0.5), len(keys...]
    all_to_all x1, waiting for transfers between devices: 0.41 us -> 7.72 us  [body(): lax.all_to_all(weight, ROW, split_axis=0, concat_axis=0, tiled=True)]
    ppermute x6, starting transfers between devices: 22.6 us -> 17.8 us  [shift(): return lax.ppermute(value, axis, [(i, (i + by) % n) for i in range(n)])]
    all_to_all x1, starting transfers between devices: 4.16 us -> 7.1 us  [body(): lax.all_to_all(weight, ROW, split_axis=0, concat_axis=0, tiled=True)]
  transfers between devices with their start and end apart: 11 -> 11, of which waited for: 4 -> 5; matrix products, arithmetic and copies ran while one was open for 4% -> 4% of each run, Pallas kernels for 13% -> 9%
where the time goes in v8:
time: 234 us; the launch traced here: 233 us
  blocking collectives  100 us (43%)
  waiting for transfers between devices  48.5 us (21%)
  starting transfers between devices  29.3 us (13%)
  Pallas kernels  24.8 us (11%)
  between operations  14.4 us (6%)
  other arithmetic  8.56 us (4%)
  local copies, waits for them, and re-layouts  7.91 us (3%)
    all_to_all x1, blocking collectives, body(): lax.all_to_all(sent, (ROW, 'head'), split_axis=0, concat_axis=0, tiled=True)  57.1 us
    ppermute x6, waiting for transfers between devices, shift(): return lax.ppermute(value, axis, [(i, (i + by) % n) for i in range(n)])  38 us
    all_to_all x1, blocking collectives, body(): terms = lax.all_to_all(terms, ROW, split_axis=0, concat_axis=0, tiled=True)  30.1 us
    pallas_call x2, Pallas kernels, attend(): pl.pallas_call(functools.partial(attend_kernel, width ** (-0.5), len(keys...  22 us
    ppermute x6, starting transfers between devices, shift(): return lax.ppermute(value, axis, [(i, (i + by) % n) for i in range(n)])  17.8 us
    all_gather x1, blocking collectives, body(): rows_in = lax.all_gather(attended[None], COL, axis=0, tiled=True)  12.8 us
    all_to_all x1, waiting for transfers between devices, body(): lax.all_to_all(weight, ROW, split_axis=0, concat_axis=0, tiled=True)  7.72 us
    all_to_all x1, starting transfers between devices, body(): lax.all_to_all(weight, ROW, split_axis=0, concat_axis=0, tiled=True)  7.1 us
  transfers between devices with their start and end apart: 11, of which 5 were waited for; matrix products, arithmetic and copies ran while one was open for 4% of the time, Pallas kernels for 9%

profile of v8, /device:TPU:6, one launch (start us, length us, event | category | flops | bytes accessed | tf_op | source)
XLA Modules:
  0.0 233.5 jit_solution(12528148631190443707)
XLA Ops:
  6.5 0.7 all-gather.4.cloned.1.call-update
  7.9 0.8 fusion.29
  8.7 1.9 pad_maximum_fusion
  10.6 7.1 %all-to-all-start = ((bf16[8,144,256]{2,1,0:T(8,128)(2,1)}), bf16[8,144,256]{2,1,0:T(8,128)(2,1)S(1)}, u32[]{:S(2)}, u32[]{:S(2)}) async-start(bf16[8,144,256]{2,1,0:T(8,128)(2,1)} %pad_maximum_fusion), calls=%async_computation | async-start | bytes 1179648 | tf_op jit(solution)/shard_map/all_to_all | solution.py:296
  17.9 4.2 %collective-permute-start.1 = (bf16[4112,128]{1,0:T(8,128)(2,1)S(1)}, bf16[4112,128]{1,0:T(8,128)(2,1)}, u32[]{:S(2)}, u32[]{:S(2)}) collective-permute-start(bf16[4112,128]{1,0:T(8,128)(2,1)S(1)} %fusion.3.refs_0_), channel_id=1, source_target_pairs={{0,16},{16,32},{32,48},{48,0},{1,17},{17,33},{33,49},{49,1},{2,18}... | collective-permute-start | bytes 3158024 | tf_op jit(solution)/shard_map/ppermute | solution.py:21
  22.1 1.9 collective-permute-start.3
  24.0 3.9 %collective-permute-start = (bf16[4112,128]{1,0:T(8,128)(2,1)S(1)}, bf16[4112,128]{1,0:T(8,128)(2,1)}, u32[]{:S(2)}, u32[]{:S(2)}) collective-permute-start(bf16[4112,128]{1,0:T(8,128)(2,1)S(1)} %fusion.3.refs_0_), channel_id=1, source_target_pairs={{0,48},{16,0},{32,16},{48,32},{1,49},{17,1},{33,17},{49,33},{2,50}... | collective-permute-start | bytes 3158024 | tf_op jit(solution)/shard_map/ppermute | solution.py:21
  28.0 1.9 collective-permute-start.2
  30.0 7.7 %all-to-all-done = bf16[8,144,256]{2,1,0:T(8,128)(2,1)S(1)} async-done(((bf16[8,144,256]{2,1,0:T(8,128)(2,1)}), bf16[8,144,256]{2,1,0:T(8,128)(2,1)S(1)}, u32[]{:S(2)}, u32[]{:S(2)}) %all-to-all-start) | async-done | bytes 589856 | tf_op jit(solution)/shard_map/all_to_all | solution.py:296
  38.3 0.8 slice.68
  39.9 27.0 %collective-permute-done.3.refs_5_ = bf16[4096,128]{1,0:T(8,128)(2,1)S(1)} collective-permute-done((bf16[4096,128]{1,0:T(8,128)(2,1)}, bf16[4096,128]{1,0:T(8,128)(2,1)S(1)}, u32[]{:S(2)}, u32[]{:S(2)}) %collective-permute-start.3) | collective-permute-done | bytes 1048608 | tf_op jit(solution)/shard_map/ppermute | solution.py:21
  67.0 1.0 copy-done.1
  68.0 3.6 %collective-permute-start.4 = (bf16[4112,128]{1,0:T(8,128)(2,1)}, bf16[4112,128]{1,0:T(8,128)(2,1)S(1)}, u32[]{:S(2)}, u32[]{:S(2)}) collective-permute-start(bf16[4112,128]{1,0:T(8,128)(2,1)} %collective-permute-done.1.refs_2_), channel_id=1, source_target_pairs={{0,16},{16,32},{32,48},{48,0},{1,17},{17,33},{33,49},{49,1},{2,18}... | collective-permute-start | bytes 3158024 | tf_op jit(solution)/shard_map/ppermute | solution.py:21
  71.6 0.7 slice_bitcast_fusion
  72.3 0.7 slice_bitcast_fusion.1
  73.5 2.2 collective-permute-start.5
  76.2 1.2 copy-done.2
  77.5 10.5 %shard_map.82 = (f32[8,1024,256]{2,1,0:T(8,128)}, f32[8,1024,128]{2,1,0:T(8,128)}) custom-call(s32[128]{0:T(128)S(1)} %reshape.438.slot_ref, bf16[8,128,1024]{2,1,0:T(8,128)(2,1)} %all-gather.4.cloned.1.call-done.q_ref, f32[8,16,128]{2,1,0:T(8,128)S(1)} %get-tuple-element.55.cos_ref, f32[8,16,128]{2,1,0:T(8,128)S(1)} %get-tuple-element.56.sin_ref, ...), custom_call_target="tpu_custom_call" | custom-call | flops 3221225472 | bytes 50331648 | tf_op jit(solution)/shard_map/pallas_call | solution.py:185
  87.9 6.1 %collective-permute-done.4.refs_0_ = bf16[4112,128]{1,0:T(8,128)(2,1)S(1)} collective-permute-done((bf16[4112,128]{1,0:T(8,128)(2,1)}, bf16[4112,128]{1,0:T(8,128)(2,1)S(1)}, u32[]{:S(2)}, u32[]{:S(2)}) %collective-permute-start.4) | collective-permute-done | bytes 1052704 | tf_op jit(solution)/shard_map/ppermute | solution.py:21
  94.9 4.9 %collective-permute-done.5.refs_1_ = bf16[4096,128]{1,0:T(8,128)(2,1)} collective-permute-done((bf16[4096,128]{1,0:T(8,128)(2,1)}, bf16[4096,128]{1,0:T(8,128)(2,1)}, u32[]{:S(2)}, u32[]{:S(2)}) %collective-permute-start.5) | collective-permute-done | bytes 1048608 | tf_op jit(solution)/shard_map/ppermute | solution.py:21
  99.7 11.5 %shard_map.83 = (bf16[2,8,8,64,128]{4,3,2,1,0:T(8,128)(2,1)S(1)}, f32[8,8,128]{2,1,0:T(8,128)S(1)}) custom-call(s32[128]{0:T(128)S(1)} %reshape.437.slot_ref, bf16[8,128,1024]{2,1,0:T(8,128)(2,1)} %all-gather.4.cloned.1.call-done.q_ref, f32[8,16,128]{2,1,0:T(8,128)S(1)} %pad_maximum_fusion.3.cos_ref, f32[8,16,128]{2,1,0:T(8,128)S(1)} %pad_maximum_fusion.4.sin_ref, ...), custom_call_target="tpu_custom_call" | custom-call | flops 1073741824 | bytes 16777216 | tf_op jit(solution)/shard_map/pallas_call | solution.py:185
  111.4 1.9 collective-permute-start.7
  113.6 2.4 %collective-permute-start.6 = (bf16[8,8,64,128]{3,2,1,0:T(8,128)(2,1)S(1)}, bf16[8,8,64,128]{3,2,1,0:T(8,128)(2,1)S(1)}, u32[]{:S(2)}, u32[]{:S(2)}) collective-permute-start(bf16[8,8,64,128]{3,2,1,0:T(8,128)(2,1)S(1)} %get-tuple-element.38), channel_id=1, source_target_pairs={{0,8},{8,0},{1,9},{9,1},{2,10},{10,2},{3,11},{11,3},{4,12},{12,4},... | collective-permute-start | bytes 3145736 | tf_op jit(solution)/shard_map/ppermute | solution.py:330
  116.2 2.0 collective-permute-done.6
  118.2 1.5 multiply_reduce_fusion
  119.8 57.1 %all_to_all.15 = bf16[64,72,128]{2,1,0:T(8,128)(2,1)S(1)} all-to-all(bf16[64,72,128]{2,1,0:T(8,128)(2,1)S(1)} %fusion.2), channel_id=1, replica_groups=mesh['lib_0'=8,'lib_1'=4,'ctx'=2,'head'=8] {'lib_0','head'}, dimensions={0} | all-to-all | bytes 2359296 | tf_op jit(solution)/shard_map/all_to_all | solution.py:343
  177.1 0.7 multiply_reduce_fusion.1
  177.9 12.8 %all_gather.11.rows_ref = bf16[4,8,64,128]{3,2,1,0:T(8,128)(2,1)S(1)} all-gather(bf16[1,8,64,128]{3,2,1,0:T(8,128)(2,1)S(1)} %fusion.4), channel_id=1, replica_groups=mesh['lib_0'=8,'lib_1'=4,'ctx'=2,'head'=8] {'lib_1'}, dimensions={0}, use_global_device_ids=true | all-gather | bytes 655360 | tf_op jit(solution)/shard_map/all_gather | solution.py:350
  190.7 2.2 copy-done
  192.9 2.8 %shard_map.84 = bf16[8,256,256]{2,1,0:T(8,128)(2,1)S(1)} custom-call(bf16[4,8,64,128]{3,2,1,0:T(8,128)(2,1)S(1)} %all_gather.11.rows_ref, bf16[8,8,128,256]{3,2,1,0:T(8,128)(2,1)S(1)} %bitcast.61), custom_call_target="tpu_custom_call" | custom-call | tf_op jit(solution)/shard_map/pallas_call | solution.py:230
  195.7 30.1 %all_to_all.16 = bf16[8,256,256]{2,1,0:T(8,128)(2,1)S(1)} all-to-all(bf16[8,256,256]{2,1,0:T(8,128)(2,1)S(1)} %shard_map.84), channel_id=1, replica_groups=mesh['lib_0'=8,'lib_1'=4,'ctx'=2,'head'=8] {'lib_0'}, dimensions={0} | all-to-all | bytes 2097152 | tf_op jit(solution)/shard_map/all_to_all | solution.py:352
  225.8 0.8 reduce_sum.85
  (65 shorter events, 4.2 us)
Async XLA Ops:
  6.5 11.2 %copy-start.4 = (s32[16]{0:T(128)S(1)}, s32[16]{0:T(128)}, u32[]{:S(2)}) copy-start(s32[16]{0:T(128)} %param.11) | copy-start | bytes 196
  6.5 11.3 %copy-start.3 = (bf16[16,256,128]{2,1,0:T(8,128)(2,1)S(1)}, bf16[16,256,128]{2,1,0:T(8,128)(2,1)}, u32[]{:S(2)}) copy-start(bf16[16,256,128]{2,1,0:T(8,128)(2,1)} %param.9) | copy-start | bytes 3145732
  6.5 69.7 %all-gather.4.cloned.1.call-start = ((), (), s32[]{:S(2)}) async-start(), calls=%async_computation.3 | async-start | bytes 2359296 | tf_op jit(solution)/shard_map/all_gather | solution.py:290
  10.6 27.1 %all-to-all-start = ((bf16[8,144,256]{2,1,0:T(8,128)(2,1)}), bf16[8,144,256]{2,1,0:T(8,128)(2,1)S(1)}, u32[]{:S(2)}, u32[]{:S(2)}) async-start(bf16[8,144,256]{2,1,0:T(8,128)(2,1)} %pad_maximum_fusion), calls=%async_computation | async-start | bytes 1179648 | tf_op jit(solution)/shard_map/all_to_all | solution.py:296
  17.7 159.2 %all-gather.6.cloned.1.call-start = ((), (), s32[]{:S(2)}) async-start(), calls=%async_computation.4 | async-start | bytes 4718592 | tf_op jit(solution)/shard_map/all_gather | solution.py:298
  17.9 50.1 %collective-permute-start.1 = (bf16[4112,128]{1,0:T(8,128)(2,1)S(1)}, bf16[4112,128]{1,0:T(8,128)(2,1)}, u32[]{:S(2)}, u32[]{:S(2)}) collective-permute-start(bf16[4112,128]{1,0:T(8,128)(2,1)S(1)} %fusion.3.refs_0_), channel_id=1, source_target_pairs={{0,16},{16,32},{32,48},{48,0},{1,17},{17,33},{33,49},{49,1},{2,18}... | collective-permute-start | bytes 3158024 | tf_op jit(solution)/shard_map/ppermute | solution.py:21
  22.1 44.9 %collective-permute-start.3 = (bf16[4096,128]{1,0:T(8,128)(2,1)}, bf16[4096,128]{1,0:T(8,128)(2,1)S(1)}, u32[]{:S(2)}, u32[]{:S(2)}) collective-permute-start(bf16[4096,128]{1,0:T(8,128)(2,1)} %bitcast.9.refs_3_), channel_id=1, source_target_pairs={{0,16},{16,32},{32,48},{48,0},{1,17},{17,33},{33,49},{49,1},{2,18}... | collective-permute-start | bytes 3145736 | tf_op jit(solution)/shard_map/ppermute | solution.py:21
  24.0 48.2 %collective-permute-start = (bf16[4112,128]{1,0:T(8,128)(2,1)S(1)}, bf16[4112,128]{1,0:T(8,128)(2,1)}, u32[]{:S(2)}, u32[]{:S(2)}) collective-permute-start(bf16[4112,128]{1,0:T(8,128)(2,1)S(1)} %fusion.3.refs_0_), channel_id=1, source_target_pairs={{0,48},{16,0},{32,16},{48,32},{1,49},{17,1},{33,17},{49,33},{2,50}... | collective-permute-start | bytes 3158024 | tf_op jit(solution)/shard_map/ppermute | solution.py:21
  28.0 45.5 %collective-permute-start.2 = (bf16[4096,128]{1,0:T(8,128)(2,1)}, bf16[4096,128]{1,0:T(8,128)(2,1)}, u32[]{:S(2)}, u32[]{:S(2)}) collective-permute-start(bf16[4096,128]{1,0:T(8,128)(2,1)} %bitcast.9.refs_3_), channel_id=1, source_target_pairs={{0,48},{16,0},{32,16},{48,32},{1,49},{17,1},{33,17},{49,33},{2,50}... | collective-permute-start | bytes 3145736 | tf_op jit(solution)/shard_map/ppermute | solution.py:21
  67.0 1.0 copy-start.1
  68.0 26.0 %collective-permute-start.4 = (bf16[4112,128]{1,0:T(8,128)(2,1)}, bf16[4112,128]{1,0:T(8,128)(2,1)S(1)}, u32[]{:S(2)}, u32[]{:S(2)}) collective-permute-start(bf16[4112,128]{1,0:T(8,128)(2,1)} %collective-permute-done.1.refs_2_), channel_id=1, source_target_pairs={{0,16},{16,32},{32,48},{48,0},{1,17},{17,33},{33,49},{49,1},{2,18}... | collective-permute-start | bytes 3158024 | tf_op jit(solution)/shard_map/ppermute | solution.py:21
  73.5 26.2 %collective-permute-start.5 = (bf16[4096,128]{1,0:T(8,128)(2,1)}, bf16[4096,128]{1,0:T(8,128)(2,1)}, u32[]{:S(2)}, u32[]{:S(2)}) collective-permute-start(bf16[4096,128]{1,0:T(8,128)(2,1)} %collective-permute-done.2.refs_4_), channel_id=1, source_target_pairs={{0,48},{16,0},{32,16},{48,32},{1,49},{17,1},{33,17},{49,33},{2,50}... | collective-permute-start | bytes 3145736 | tf_op jit(solution)/shard_map/ppermute | solution.py:21
  76.2 1.2 copy-start.2
  111.4 4.6 %collective-permute-start.7 = (f32[8,8,64]{2,1,0:T(8,128)S(1)}, f32[8,8,64]{2,1,0:T(8,128)S(1)}, u32[]{:S(2)}, u32[]{:S(2)}) collective-permute-start(f32[8,8,64]{2,1,0:T(8,128)S(1)} %bitcast.72), channel_id=1, source_target_pairs={{0,8},{8,0},{1,9},{9,1},{2,10},{10,2},{3,11},{11,3},{4,12},{12,4},... | collective-permute-start | bytes 49160 | tf_op jit(solution)/shard_map/ppermute | solution.py:331
  113.6 4.7 %collective-permute-start.6 = (bf16[8,8,64,128]{3,2,1,0:T(8,128)(2,1)S(1)}, bf16[8,8,64,128]{3,2,1,0:T(8,128)(2,1)S(1)}, u32[]{:S(2)}, u32[]{:S(2)}) collective-permute-start(bf16[8,8,64,128]{3,2,1,0:T(8,128)(2,1)S(1)} %get-tuple-element.38), channel_id=1, source_target_pairs={{0,8},{8,0},{1,9},{9,1},{2,10},{10,2},{3,11},{11,3},{4,12},{12,4},... | collective-permute-start | bytes 3145736 | tf_op jit(solution)/shard_map/ppermute | solution.py:330
  190.7 2.2 copy-start
Sparse Core Ops, SparseCore 0:
  9.4 50.8 all-gather.3
  62.4 59.8 all-gather.5

commit v9 on v8

--- a/solution.py
+++ b/solution.py
@@ -89,7 +89,6 @@
             sine = sin_ref[0, pl.ds(entry[i], 1), :]
             turned = keys * cosine + pltpu.roll(keys, width // 2, 1) * sine
             k_scr[b * tokens : (b + 1) * tokens] = turned.astype(jnp.bfloat16)
-        both = 2 * t + 1 < count
         for span in chunks:
             s = lax.dot_general(
                 q_scr[span],
@@ -100,8 +99,6 @@
             highest = m_scr[span]
             for u in range(0, 2 * tokens, width):
                 part = s[:, u : u + width]
-                if u >= tokens:
-                    part = jnp.where(both, part, EMPTY)
                 s_scr[t, span, u : u + width] = part
                 highest = jnp.maximum(highest, part)
             m_scr[span] = highest
@@ -121,7 +118,12 @@
     def weigh(t, carry):
         for b in range(2):
             i = jnp.minimum(2 * t + b, count - 1)
-            v_scr[b * tokens : (b + 1) * tokens, :width] = fetch(value_refs, used[i])
+            values = fetch(value_refs, used[i])
+            if b == 1:
+                both = 2 * t + 1 < count
+                values = jnp.where(both, values, jnp.zeros_like(values))
+                v_scr[tokens:, width:] = jnp.where(both, 1.0, jnp.zeros((tokens, width))).astype(v_scr.dtype)
+            v_scr[b * tokens : (b + 1) * tokens, :width] = values
         for span in chunks:
             m = m_scr[span]
             parts = [
@@ -294,7 +296,9 @@
     asked = jnp.broadcast_to(asked, (rows_of, *asked.shape))
     weight = jnp.concatenate([out_weight.reshape(group, width, -1), asked], axis=1)
     weight = lax.all_to_all(weight, ROW, split_axis=0, concat_axis=0, tiled=True)
-    asked = decoded(weight[:, width, :entries], weight[:, width + 1, :entries])
+    asked = weight[:, width : width + 2, :entries]
+    asked, keys[1], keys[3] = lax.optimization_barrier((asked, keys[1], keys[3]))
+    asked = decoded(asked[:, 0], asked[:, 1])
     weight = lax.all_gather(weight[None, :, :width], "head", axis=0, tiled=True)
 
     local = asked[:, :listed] - y * columns * held

time: 234 us -> 225 us (0.962)
  waiting for transfers between devices: 48.5 us -> 30.7 us
  Pallas kernels: 24.8 us -> 31.7 us
  starting transfers between devices: 29.3 us -> 33 us
    ppermute x6, waiting for transfers between devices: 38 us -> 10.9 us  [shift(): return lax.ppermute(value, axis, [(i, (i + by) % n) for i in range(n)])]
    all_to_all x1, waiting for transfers between devices: 7.72 us -> 17 us  [body(): lax.all_to_all(weight, ROW, split_axis=0, concat_axis=0, tiled=True)]
    pallas_call x2, Pallas kernels: 22 us -> 28.9 us  [attend(): pl.pallas_call(functools.partial(attend_kernel, width ** (-0.5), len(keys...]
    ppermute x6, starting transfers between devices: 17.8 us -> 24.2 us  [shift(): return lax.ppermute(value, axis, [(i, (i + by) % n) for i in range(n)])]
    all_to_all x1, blocking collectives: 57.1 us -> 54.3 us  [body(): lax.all_to_all(sent, (ROW, 'head'), split_axis=0, concat_axis=0, tiled=True)]
    all_to_all x1, starting transfers between devices: 7.1 us -> 4.47 us  [body(): lax.all_to_all(weight, ROW, split_axis=0, concat_axis=0, tiled=True)]
  transfers between devices with their start and end apart: 11 -> 11, of which waited for: 5 -> 4; matrix products, arithmetic and copies ran while one was open for 4% -> 4% of each run, Pallas kernels for 9% -> 13%
where the time goes in v9:
time: 225 us
  blocking collectives  98.7 us (44%)
  starting transfers between devices  33 us (15%)
  Pallas kernels  31.7 us (14%)
  waiting for transfers between devices  30.7 us (14%)
  between operations  14.5 us (6%)
  other arithmetic  8.77 us (4%)
  local copies, waits for them, and re-layouts  7.25 us (3%)
    all_to_all x1, blocking collectives, body(): lax.all_to_all(sent, (ROW, 'head'), split_axis=0, concat_axis=0, tiled=True)  54.3 us
    all_to_all x1, blocking collectives, body(): terms = lax.all_to_all(terms, ROW, split_axis=0, concat_axis=0, tiled=True)  31.2 us
    pallas_call x2, Pallas kernels, attend(): pl.pallas_call(functools.partial(attend_kernel, width ** (-0.5), len(keys...  28.9 us
    ppermute x6, starting transfers between devices, shift(): return lax.ppermute(value, axis, [(i, (i + by) % n) for i in range(n)])  24.2 us
    all_to_all x1, waiting for transfers between devices, body(): lax.all_to_all(weight, ROW, split_axis=0, concat_axis=0, tiled=True)  17 us
    all_gather x1, blocking collectives, body(): rows_in = lax.all_gather(attended[None], COL, axis=0, tiled=True)  13.2 us
    ppermute x6, waiting for transfers between devices, shift(): return lax.ppermute(value, axis, [(i, (i + by) % n) for i in range(n)])  10.9 us
    unnamed x15, local copies, waits for them, and re-layouts  4.51 us
  transfers between devices with their start and end apart: 11, of which 4 were waited for; matrix products, arithmetic and copies ran while one was open for 4% of the time, Pallas kernels for 13%

profile of v9, /device:TPU:6, one launch (start us, length us, event | category | flops | bytes accessed | tf_op | source)
XLA Modules:
  0.0 224.6 jit_solution(3833664403315881342)
XLA Ops:
  6.5 0.7 all-gather.4.cloned.1.call-update
  7.3 0.7 convert_bitcast_fusion
  7.9 1.3 fusion.3.refs_0_
  9.2 2.7 %collective-permute-start = (bf16[4112,128]{1,0:T(8,128)(2,1)S(1)}, bf16[4112,128]{1,0:T(8,128)(2,1)S(1)}, u32[]{:S(2)}, u32[]{:S(2)}) collective-permute-start(bf16[4112,128]{1,0:T(8,128)(2,1)S(1)} %fusion.3.refs_0_), channel_id=1, source_target_pairs={{0,48},{16,0},{32,16},{48,32},{1,49},{17,1},{33,17},{49,33},{2,50}... | collective-permute-start | bytes 3158024 | tf_op jit(solution)/shard_map/ppermute | solution.py:21
  12.0 6.9 %collective-permute-start.1 = (bf16[4112,128]{1,0:T(8,128)(2,1)S(1)}, bf16[4112,128]{1,0:T(8,128)(2,1)}, u32[]{:S(2)}, u32[]{:S(2)}) collective-permute-start(bf16[4112,128]{1,0:T(8,128)(2,1)S(1)} %fusion.3.refs_0_), channel_id=1, source_target_pairs={{0,16},{16,32},{32,48},{48,0},{1,17},{17,33},{33,49},{49,1},{2,18}... | collective-permute-start | bytes 3158024 | tf_op jit(solution)/shard_map/ppermute | solution.py:21
  19.7 0.9 pad_maximum_fusion
  20.6 4.5 %all-to-all-start = ((bf16[8,144,256]{2,1,0:T(8,128)(2,1)}), bf16[8,144,256]{2,1,0:T(8,128)(2,1)S(1)}, u32[]{:S(2)}, u32[]{:S(2)}) async-start(bf16[8,144,256]{2,1,0:T(8,128)(2,1)} %pad_maximum_fusion), calls=%async_computation | async-start | bytes 1179648 | tf_op jit(solution)/shard_map/all_to_all | solution.py:298
  25.1 1.9 collective-permute-start.2
  27.1 5.1 %collective-permute-start.3 = (bf16[4096,128]{1,0:T(8,128)(2,1)}, bf16[4096,128]{1,0:T(8,128)(2,1)}, u32[]{:S(2)}, u32[]{:S(2)}) collective-permute-start(bf16[4096,128]{1,0:T(8,128)(2,1)} %bitcast.9.refs_3_), channel_id=1, source_target_pairs={{0,16},{16,32},{32,48},{48,0},{1,17},{17,33},{33,49},{49,1},{2,18}... | collective-permute-start | bytes 3145736 | tf_op jit(solution)/shard_map/ppermute | solution.py:21
  32.2 17.0 %all-to-all-done = bf16[8,144,256]{2,1,0:T(8,128)(2,1)S(1)} async-done(((bf16[8,144,256]{2,1,0:T(8,128)(2,1)}), bf16[8,144,256]{2,1,0:T(8,128)(2,1)S(1)}, u32[]{:S(2)}, u32[]{:S(2)}) %all-to-all-start) | async-done | bytes 589856 | tf_op jit(solution)/shard_map/all_to_all | solution.py:298
  49.2 0.9 slice.69
  50.1 0.7 slice_bitcast_fusion.1
  50.8 1.0 copy-done.1
  52.1 9.0 %collective-permute-done.3.refs_5_ = bf16[4096,128]{1,0:T(8,128)(2,1)} collective-permute-done((bf16[4096,128]{1,0:T(8,128)(2,1)}, bf16[4096,128]{1,0:T(8,128)(2,1)}, u32[]{:S(2)}, u32[]{:S(2)}) %collective-permute-start.3) | collective-permute-done | bytes 1048608 | tf_op jit(solution)/shard_map/ppermute | solution.py:21
  61.2 5.5 %collective-permute-start.4 = (bf16[4112,128]{1,0:T(8,128)(2,1)}, bf16[4112,128]{1,0:T(8,128)(2,1)S(1)}, u32[]{:S(2)}, u32[]{:S(2)}) collective-permute-start(bf16[4112,128]{1,0:T(8,128)(2,1)} %collective-permute-done.1.refs_2_), channel_id=1, source_target_pairs={{0,16},{16,32},{32,48},{48,0},{1,17},{17,33},{33,49},{49,1},{2,18}... | collective-permute-start | bytes 3158024 | tf_op jit(solution)/shard_map/ppermute | solution.py:21
  67.1 1.9 collective-permute-start.5
  69.6 0.7 add_compare_fusion
  70.8 1.2 copy-done.2
  72.0 16.6 %shard_map.82 = (f32[8,1024,256]{2,1,0:T(8,128)}, f32[8,1024,128]{2,1,0:T(8,128)}) custom-call(s32[128]{0:T(128)S(1)} %reshape.439.slot_ref, bf16[8,128,1024]{2,1,0:T(8,128)(2,1)} %all-gather.4.cloned.1.call-done.q_ref, f32[8,16,128]{2,1,0:T(8,128)S(1)} %pad_maximum_fusion.1.cos_ref, f32[8,16,128]{2,1,0:T(8,128)S(1)} %pad_maximum_fusion.2.sin_ref, ...), custom_call_target="tpu_custom_call" | custom-call | flops 3221225472 | bytes 50331648 | tf_op jit(solution)/shard_map/pallas_call | solution.py:187
  89.5 1.9 collective-permute-done.5.refs_1_
  91.3 12.3 %shard_map.83 = (bf16[2,8,8,64,128]{4,3,2,1,0:T(8,128)(2,1)S(1)}, f32[8,8,128]{2,1,0:T(8,128)S(1)}) custom-call(s32[128]{0:T(128)S(1)} %reshape.438.slot_ref, bf16[8,128,1024]{2,1,0:T(8,128)(2,1)} %all-gather.4.cloned.1.call-done.q_ref, f32[8,16,128]{2,1,0:T(8,128)S(1)} %pad_maximum_fusion.3.cos_ref, f32[8,16,128]{2,1,0:T(8,128)S(1)} %pad_maximum_fusion.4.sin_ref, ...), custom_call_target="tpu_custom_call" | custom-call | flops 1073741824 | bytes 16777216 | tf_op jit(solution)/shard_map/pallas_call | solution.py:187
  103.9 1.9 collective-permute-start.7
  106.0 2.4 %collective-permute-start.6 = (bf16[8,8,64,128]{3,2,1,0:T(8,128)(2,1)S(1)}, bf16[8,8,64,128]{3,2,1,0:T(8,128)(2,1)S(1)}, u32[]{:S(2)}, u32[]{:S(2)}) collective-permute-start(bf16[8,8,64,128]{3,2,1,0:T(8,128)(2,1)S(1)} %get-tuple-element.44), channel_id=1, source_target_pairs={{0,8},{8,0},{1,9},{9,1},{2,10},{10,2},{3,11},{11,3},{4,12},{12,4},... | collective-permute-start | bytes 3145736 | tf_op jit(solution)/shard_map/ppermute | solution.py:334
  108.6 2.0 collective-permute-done.6
  110.7 1.5 multiply_reduce_fusion
  112.3 54.3 %all_to_all.15 = bf16[64,72,128]{2,1,0:T(8,128)(2,1)S(1)} all-to-all(bf16[64,72,128]{2,1,0:T(8,128)(2,1)S(1)} %fusion.2), channel_id=1, replica_groups=mesh['lib_0'=8,'lib_1'=4,'ctx'=2,'head'=8] {'lib_0','head'}, dimensions={0} | all-to-all | bytes 2359296 | tf_op jit(solution)/shard_map/all_to_all | solution.py:347
  166.7 0.7 multiply_reduce_fusion.1
  167.5 13.2 %all_gather.11.rows_ref = bf16[4,8,64,128]{3,2,1,0:T(8,128)(2,1)S(1)} all-gather(bf16[1,8,64,128]{3,2,1,0:T(8,128)(2,1)S(1)} %fusion.4), channel_id=1, replica_groups=mesh['lib_0'=8,'lib_1'=4,'ctx'=2,'head'=8] {'lib_1'}, dimensions={0}, use_global_device_ids=true | all-gather | bytes 655360 | tf_op jit(solution)/shard_map/all_gather | solution.py:354
  180.7 2.2 copy-done
  182.9 2.8 %shard_map.84 = bf16[8,256,256]{2,1,0:T(8,128)(2,1)S(1)} custom-call(bf16[4,8,64,128]{3,2,1,0:T(8,128)(2,1)S(1)} %all_gather.11.rows_ref, bf16[8,8,128,256]{3,2,1,0:T(8,128)(2,1)S(1)} %bitcast.61), custom_call_target="tpu_custom_call" | custom-call | tf_op jit(solution)/shard_map/pallas_call | solution.py:232
  185.7 31.2 %all_to_all.16 = bf16[8,256,256]{2,1,0:T(8,128)(2,1)S(1)} all-to-all(bf16[8,256,256]{2,1,0:T(8,128)(2,1)S(1)} %shard_map.84), channel_id=1, replica_groups=mesh['lib_0'=8,'lib_1'=4,'ctx'=2,'head'=8] {'lib_0'}, dimensions={0} | all-to-all | bytes 2097152 | tf_op jit(solution)/shard_map/all_to_all | solution.py:356
  216.9 0.8 reduce_sum.85
  (68 shorter events, 3.6 us)
Async XLA Ops:
  6.5 13.1 %copy-start.5 = (s32[1,16]{1,0:T(1,128)S(1)}, s32[1,16]{1,0:T(1,128)}, u32[]{:S(2)}) copy-start(s32[1,16]{1,0:T(1,128)} %param.13) | copy-start | bytes 196
  6.5 13.1 %copy-start.4 = (s32[1,16]{1,0:T(1,128)S(1)}, s32[1,16]{1,0:T(1,128)}, u32[]{:S(2)}) copy-start(s32[1,16]{1,0:T(1,128)} %param.14) | copy-start | bytes 196
  6.5 13.2 %copy-start.3 = (bf16[1024,256]{1,0:T(8,128)(2,1)S(1)}, bf16[1024,256]{1,0:T(8,128)(2,1)}, u32[]{:S(2)}) copy-start(bf16[1024,256]{1,0:T(8,128)(2,1)} %param.12) | copy-start | bytes 1572868
  6.5 64.2 %all-gather.4.cloned.1.call-start = ((), (), s32[]{:S(2)}) async-start(), calls=%async_computation.3 | async-start | bytes 2359296 | tf_op jit(solution)/shard_map/all_gather | solution.py:292
  9.2 40.9 %collective-permute-start = (bf16[4112,128]{1,0:T(8,128)(2,1)S(1)}, bf16[4112,128]{1,0:T(8,128)(2,1)S(1)}, u32[]{:S(2)}, u32[]{:S(2)}) collective-permute-start(bf16[4112,128]{1,0:T(8,128)(2,1)S(1)} %fusion.3.refs_0_), channel_id=1, source_target_pairs={{0,48},{16,0},{32,16},{48,32},{1,49},{17,1},{33,17},{49,33},{2,50}... | collective-permute-start | bytes 3158024 | tf_op jit(solution)/shard_map/ppermute | solution.py:21
  12.0 38.1 %collective-permute-start.1 = (bf16[4112,128]{1,0:T(8,128)(2,1)S(1)}, bf16[4112,128]{1,0:T(8,128)(2,1)}, u32[]{:S(2)}, u32[]{:S(2)}) collective-permute-start(bf16[4112,128]{1,0:T(8,128)(2,1)S(1)} %fusion.3.refs_0_), channel_id=1, source_target_pairs={{0,16},{16,32},{32,48},{48,0},{1,17},{17,33},{33,49},{49,1},{2,18}... | collective-permute-start | bytes 3158024 | tf_op jit(solution)/shard_map/ppermute | solution.py:21
  20.6 28.6 %all-to-all-start = ((bf16[8,144,256]{2,1,0:T(8,128)(2,1)}), bf16[8,144,256]{2,1,0:T(8,128)(2,1)S(1)}, u32[]{:S(2)}, u32[]{:S(2)}) async-start(bf16[8,144,256]{2,1,0:T(8,128)(2,1)} %pad_maximum_fusion), calls=%async_computation | async-start | bytes 1179648 | tf_op jit(solution)/shard_map/all_to_all | solution.py:298
  25.1 141.5 %all-gather.6.cloned.1.call-start = ((), (), s32[]{:S(2)}) async-start(), calls=%async_computation.4 | async-start | bytes 4718592 | tf_op jit(solution)/shard_map/all_gather | solution.py:302
  25.1 42.0 %collective-permute-start.2 = (bf16[4096,128]{1,0:T(8,128)(2,1)}, bf16[4096,128]{1,0:T(8,128)(2,1)}, u32[]{:S(2)}, u32[]{:S(2)}) collective-permute-start(bf16[4096,128]{1,0:T(8,128)(2,1)} %bitcast.9.refs_3_), channel_id=1, source_target_pairs={{0,48},{16,0},{32,16},{48,32},{1,49},{17,1},{33,17},{49,33},{2,50}... | collective-permute-start | bytes 3145736 | tf_op jit(solution)/shard_map/ppermute | solution.py:21
  27.1 34.1 %collective-permute-start.3 = (bf16[4096,128]{1,0:T(8,128)(2,1)}, bf16[4096,128]{1,0:T(8,128)(2,1)}, u32[]{:S(2)}, u32[]{:S(2)}) collective-permute-start(bf16[4096,128]{1,0:T(8,128)(2,1)} %bitcast.9.refs_3_), channel_id=1, source_target_pairs={{0,16},{16,32},{32,48},{48,0},{1,17},{17,33},{33,49},{49,1},{2,18}... | collective-permute-start | bytes 3145736 | tf_op jit(solution)/shard_map/ppermute | solution.py:21
  50.8 1.0 copy-start.1
  61.2 27.4 %collective-permute-start.4 = (bf16[4112,128]{1,0:T(8,128)(2,1)}, bf16[4112,128]{1,0:T(8,128)(2,1)S(1)}, u32[]{:S(2)}, u32[]{:S(2)}) collective-permute-start(bf16[4112,128]{1,0:T(8,128)(2,1)} %collective-permute-done.1.refs_2_), channel_id=1, source_target_pairs={{0,16},{16,32},{32,48},{48,0},{1,17},{17,33},{33,49},{49,1},{2,18}... | collective-permute-start | bytes 3158024 | tf_op jit(solution)/shard_map/ppermute | solution.py:21
  67.1 24.2 %collective-permute-start.5 = (bf16[4096,128]{1,0:T(8,128)(2,1)}, bf16[4096,128]{1,0:T(8,128)(2,1)}, u32[]{:S(2)}, u32[]{:S(2)}) collective-permute-start(bf16[4096,128]{1,0:T(8,128)(2,1)} %collective-permute-done.2.refs_4_), channel_id=1, source_target_pairs={{0,48},{16,0},{32,16},{48,32},{1,49},{17,1},{33,17},{49,33},{2,50}... | collective-permute-start | bytes 3145736 | tf_op jit(solution)/shard_map/ppermute | solution.py:21
  70.8 1.2 copy-start.2
  103.9 4.6 %collective-permute-start.7 = (f32[8,8,64]{2,1,0:T(8,128)S(1)}, f32[8,8,64]{2,1,0:T(8,128)S(1)}, u32[]{:S(2)}, u32[]{:S(2)}) collective-permute-start(f32[8,8,64]{2,1,0:T(8,128)S(1)} %bitcast.72), channel_id=1, source_target_pairs={{0,8},{8,0},{1,9},{9,1},{2,10},{10,2},{3,11},{11,3},{4,12},{12,4},... | collective-permute-start | bytes 49160 | tf_op jit(solution)/shard_map/ppermute | solution.py:335
  106.0 4.7 %collective-permute-start.6 = (bf16[8,8,64,128]{3,2,1,0:T(8,128)(2,1)S(1)}, bf16[8,8,64,128]{3,2,1,0:T(8,128)(2,1)S(1)}, u32[]{:S(2)}, u32[]{:S(2)}) collective-permute-start(bf16[8,8,64,128]{3,2,1,0:T(8,128)(2,1)S(1)} %get-tuple-element.44), channel_id=1, source_target_pairs={{0,8},{8,0},{1,9},{9,1},{2,10},{10,2},{3,11},{11,3},{4,12},{12,4},... | collective-permute-start | bytes 3145736 | tf_op jit(solution)/shard_map/ppermute | solution.py:334
  180.7 2.2 copy-start
Sparse Core Ops, SparseCore 0:
  9.4 56.2 all-gather.3
  67.8 59.2 all-gather.5
